TPU v7x, 512 devices: a whole 4x8x8 slice. The times are simulated.
512 devices in a mesh: fsdp: 32 (over z_hi, y), tensor: 16 (over z_lo, x, core).
Axes of the slice: x: 4, y: 8, z: 8 (z_hi: 4, z_lo: 2; z = z_hi * 2 + z_lo), core: 2. Of those that a mesh axis runs over, the one named last changes fastest.
Arguments:
- stream_in: bfloat16 [4096, 4096], P('fsdp', 'tensor'), may hold values from -6 to 6
- newer_partial: bfloat16 [16, 4096, 4096], P('tensor', 'fsdp'), may hold values from -1.5 to 1.5
- norm_gain: bfloat16 [4096], replicated, may hold values from 0.099609375 to 1.8984375
- query_weight: bfloat16 [4096, 4096], P('fsdp', 'tensor'), may hold values from -0.09375 to 0.09375
- keys_values: bfloat16 [4096, 2048], P('fsdp'), may hold values from -160 to 160, as said below
- out_weight: bfloat16 [4096, 4096], P('tensor', 'fsdp'), may hold values from -0.09375 to 0.09375
- cot_stream: bfloat16 [4096, 4096], P('fsdp', 'tensor'), may hold values from -0.59765625 to 0.59765625
- cot_attn: bfloat16 [4096, 4096], P('fsdp', 'tensor'), may hold values from -6 to 6
Outputs:
- stream_out: bfloat16 [4096, 4096], P('fsdp')
- attn_partial: bfloat16 [16, 4096, 4096], P('tensor', 'fsdp')
- stream_grad: bfloat16 [4096, 4096], P('fsdp', 'tensor')
- kv_grad: bfloat16 [4096, 2048], P('fsdp')
- query_weight_grad: bfloat16 [4096, 4096], P('fsdp', 'tensor')
- out_weight_grad: bfloat16 [4096, 4096], P('tensor', 'fsdp')
Inputs may be any that keep to these rules, and one draw needn't show every extreme that they name: `keys_values`: keys and values of 8 heads, each head's key before its value.
All inputs are finite; a program needn't handle non-finite values.
Results may differ from a plain program's by a relative error of at most 0.035.
The roundings to bfloat16 on the way count: a program that leaves them out, or rounds other values in their place, can miss the bound.
Values may be sent and summed in bfloat16 or wider, within the bound.
No kernel may reach another device: no remote copies, remote signals or barrier semaphores. Data moves between devices by JAX's collectives and lax.ppermute only.
A program may use at most 64 MiB of HBM per device.

v0:
```python
import math

import jax
import jax.numpy as jnp
from jax import lax
from jax.sharding import PartitionSpec as P

HEADS = 32
HS = 128
KVH = 8


def per_device(
    stream_in, newer_partial, norm_gain, query_weight, keys_values, out_weight, cot_stream, cot_attn
):
    tensor_rank = lax.axis_index("tensor")
    seq_len = stream_in.shape[0]
    local_width = stream_in.shape[1]
    cols = query_weight.shape[1]
    heads_here = cols // HS
    group = HEADS // KVH
    kv_here = max(1, heads_here // group)
    per_kv = heads_here // kv_here
    first_kv = tensor_rank * heads_here // group
    scale = 1.0 / math.sqrt(HS)
    contract_last = (((1,), (1,)), ((), ()))
    contract_first = (((0,), (0,)), ((), ()))
    whole = lax.all_gather(stream_in, "tensor", axis=1, tiled=True)
    pending = lax.psum(newer_partial[0].astype(jnp.float32).astype(jnp.bfloat16), "tensor").astype(
        jnp.float32
    )
    stream_f = whole.astype(jnp.float32)
    inv_rms = lax.rsqrt(jnp.mean(stream_f * stream_f, -1, keepdims=True) + 1e-05)
    gain_f = norm_gain.astype(jnp.float32)
    normed = (stream_f * inv_rms * gain_f).astype(jnp.bfloat16)
    query_full = lax.all_gather(query_weight, "fsdp", axis=0, tiled=True)
    out_full = lax.all_gather(out_weight, "fsdp", axis=1, tiled=True)
    queries = jnp.dot(normed, query_full, preferred_element_type=jnp.float32)
    queries = queries.astype(jnp.bfloat16)
    kv_block = lax.dynamic_slice_in_dim(keys_values, first_kv * 2 * HS, kv_here * 2 * HS, 1)
    kv_block = kv_block.reshape(seq_len, kv_here, 2, HS)
    keys = kv_block[:, :, 0]
    values = kv_block[:, :, 1]
    q_four = queries.reshape(seq_len, kv_here, per_kv, HS)
    scores = jnp.einsum("qkgd,skd->kgqs", q_four, keys, preferred_element_type=jnp.float32) * scale
    causal = jnp.arange(seq_len)[:, None] >= jnp.arange(seq_len)[None, :]
    scores = jnp.where(causal[None, None], scores, -1e30)
    top = jnp.max(scores, -1, keepdims=True)
    weights = jnp.exp(scores - top)
    probs = weights / jnp.sum(weights, -1, keepdims=True)
    probs_low = probs.astype(jnp.bfloat16)
    attended = jnp.einsum(
        "kgqs,skd->qkgd", probs_low, values, preferred_element_type=jnp.float32
    ).astype(jnp.bfloat16)
    att_flat = attended.reshape(seq_len, cols)
    partial_out = jnp.dot(att_flat, out_full, preferred_element_type=jnp.float32)
    attn_partial = partial_out.astype(jnp.bfloat16)[None]
    grad_attn = lax.all_gather(cot_attn, "tensor", axis=1, tiled=True)
    grad_heads = lax.dot_general(
        grad_attn, out_full, contract_last, preferred_element_type=jnp.float32
    )
    grad_heads = grad_heads.astype(jnp.bfloat16)
    grad_four = grad_heads.reshape(seq_len, kv_here, per_kv, HS)
    delta = jnp.sum(grad_four.astype(jnp.float32) * attended.astype(jnp.float32), -1).transpose(
        1, 2, 0
    )
    grad_probs = jnp.einsum("qkgd,skd->kgqs", grad_four, values, preferred_element_type=jnp.float32)
    grad_scores = (probs * (grad_probs - delta[..., None]) * scale).astype(jnp.bfloat16)
    grad_q = jnp.einsum(
        "kgqs,skd->qkgd", grad_scores, keys, preferred_element_type=jnp.float32
    ).astype(jnp.bfloat16)
    grad_q = grad_q.reshape(seq_len, cols)
    grad_keys = jnp.einsum(
        "kgqs,qkgd->skd", grad_scores, q_four, preferred_element_type=jnp.float32
    )
    grad_values = jnp.einsum(
        "kgqs,qkgd->skd", probs_low, grad_four, preferred_element_type=jnp.float32
    )
    kv_part = jnp.stack([grad_keys, grad_values], 2).reshape(seq_len, kv_here * 2 * HS)
    kv_total = lax.dynamic_update_slice_in_dim(
        jnp.zeros((seq_len, keys_values.shape[1]), jnp.float32), kv_part, first_kv * 2 * HS, 1
    )
    kv_grad = lax.psum(kv_total.astype(jnp.bfloat16), "tensor")
    normed_part = lax.dot_general(
        grad_q, query_full, contract_last, preferred_element_type=jnp.float32
    )
    normed_grad = lax.psum(normed_part.astype(jnp.bfloat16), "tensor").astype(jnp.float32)
    scaled = gain_f * normed_grad
    grad_stream = inv_rms * scaled - stream_f * inv_rms**3 * jnp.mean(
        scaled * stream_f, -1, keepdims=True
    )
    own_part = lax.dynamic_slice_in_dim(grad_stream, tensor_rank * local_width, local_width, 1)
    stream_out = (stream_f + pending).astype(jnp.bfloat16)
    stream_grad = (cot_stream.astype(jnp.float32) + own_part).astype(jnp.bfloat16)
    query_weight_grad = lax.psum_scatter(
        lax.dot_general(normed, grad_q, contract_first, preferred_element_type=jnp.float32).astype(
            jnp.bfloat16
        ),
        "fsdp",
        scatter_dimension=0,
        tiled=True,
    )
    out_term = lax.dot_general(
        att_flat, grad_attn, contract_first, preferred_element_type=jnp.float32
    )
    out_weight_grad = lax.psum_scatter(
        out_term.astype(jnp.bfloat16), "fsdp", scatter_dimension=1, tiled=True
    )
    return (stream_out, attn_partial, stream_grad, kv_grad, query_weight_grad, out_weight_grad)


def solution(mesh):
    return jax.shard_map(
        per_device,
        mesh=mesh,
        in_specs=(
            P("fsdp", "tensor"),
            P("tensor", "fsdp", None),
            P(),
            P("fsdp", "tensor"),
            P("fsdp", None),
            P("tensor", "fsdp"),
            P("fsdp", "tensor"),
            P("fsdp", "tensor"),
        ),
        out_specs=(
            P("fsdp", None),
            P("tensor", "fsdp", None),
            P("fsdp", "tensor"),
            P("fsdp", None),
            P("fsdp", "tensor"),
            P("tensor", "fsdp"),
        ),
        check_vma=False,
    )
```

profile of v0, /device:TPU:6, one launch (start us, length us, event | category | flops | bytes accessed | tf_op | source)
XLA Modules:
  0.0 882.7 jit_solution(15931734982256096634)
XLA Ops:
  8.0 0.7 all-gather.11.cloned.1.call-update
  10.0 0.7 convert_element_type.91
  10.9 42.2 %all-gather.5.cloned.1.call-done = bf16[128,4096]{1,0:T(8,128)(2,1)} async-done(((bf16[128,256]{1,0:T(8,128)(2,1)}), bf16[128,4096]{1,0:T(8,128)(2,1)}) %all-gather.5.cloned.1.call-update) | async-done | bytes 1048592 | tf_op jit(solution)/shard_map/all_gather | solution.py:28
  53.1 1.6 multiply_reduce_fusion.1
  54.7 40.0 %all-gather.11.cloned.1.call-done = bf16[128,4096]{1,0:T(8,128)(2,1)} async-done(((bf16[128,256]{1,0:T(8,128)(2,1)}), bf16[128,4096]{1,0:T(8,128)(2,1)}) %all-gather.11.cloned.1.call-update) | async-done | bytes 1048592 | tf_op jit(solution)/shard_map/all_gather | solution.py:58
  94.7 94.1 %all-gather.9.cloned.1.call-done = bf16[256,4096]{1,0:T(8,128)(2,1)} async-done(((bf16[256,128]{1,0:T(8,128)(2,1)}), bf16[256,4096]{1,0:T(8,128)(2,1)}) %all-gather.9.cloned.1.call-update) | async-done | bytes 2097168 | tf_op jit(solution)/shard_map/all_gather | solution.py:37
  188.8 2.8 convolution_convert_fusion.4
  191.8 81.9 %all-gather.7.cloned.1.call-done = bf16[4096,256]{1,0:T(8,128)(2,1)} async-done(((bf16[128,256]{1,0:T(8,128)(2,1)}), bf16[4096,256]{1,0:T(8,128)(2,1)}) %all-gather.7.cloned.1.call-update) | async-done | bytes 2097168 | tf_op jit(solution)/shard_map/all_gather | solution.py:36
  273.6 2.1 convolution_convert_fusion.5
  277.2 3.6 convolution_convert_fusion.2
  280.9 1.1 copy-done.3
  282.0 2.0 convolution_convert_fusion
  284.1 4.1 copy.62
  288.2 2.1 convolution_convert_fusion.1
  290.4 1.6 convert_element_type.88
  291.9 0.8 copy-done.2
  292.7 1.4 fusion
  294.2 114.8 %all-reduce.3.cloned.1.call-done = (bf16[128,4096]{1,0:T(8,128)(2,1)}, bf16[128,4096]{1,0:T(8,128)(2,1)}, bf16[128,2048]{1,0:T(8,128)(2,1)}) async-done(((bf16[128,4096]{1,0:T(8,128)(2,1)}, bf16[128,4096]{1,0:T(8,128)(2,1)}, bf16[128,2048]{1,0:T(8,128)(2,1)}), (bf16[128,4096]{1,0:T(8,128)(2,1)}, bf16[128,4096]{1,0:T(8,128)(2,1)}, bf16[128,2048]{1,0:T(8,128)(2,1)})) %all-reduce.3.cloned.1.call-update) | async-done | bytes 2621456 | tf_op jit(solution)/shard_map/psum | solution.py:29
  409.0 3.1 multiply_reduce_fusion
  412.1 1.7 fusion.10
  413.8 231.1 %reduce-scatter.7.cloned.1.call-done = bf16[128,256]{1,0:T(8,128)(2,1)} async-done(((bf16[4096,256]{1,0:T(8,128)(2,1)}), bf16[128,256]{1,0:T(8,128)(2,1)}) %reduce-scatter.7.cloned.1.call-update) | async-done | bytes 65552
  644.9 1.6 copy.63
  646.4 228.6 %reduce-scatter.5.cloned.1.call-done = bf16[128,256]{1,0:T(8,128)(2,1)} async-done(((bf16[4096,256]{1,0:T(8,128)(2,1)}), bf16[128,256]{1,0:T(8,128)(2,1)}) %reduce-scatter.5.cloned.1.call-update) | async-done | bytes 65552 | tf_op jit(solution)/shard_map/reduce_scatter | solution.py:95
  875.0 0.8 copy.73
  (44 shorter events, 4.0 us)
Async XLA Ops:
  7.2 3.6 copy-start
  7.2 45.9 %all-gather.5.cloned.1.call-start = ((), (), s32[]{:S(2)}) async-start(), calls=%async_computation.2 | async-start | bytes 1114112 | tf_op jit(solution)/shard_map/all_gather | solution.py:28
  7.9 86.8 %all-gather.11.cloned.1.call-start = ((), (), s32[]{:S(2)}) async-start(), calls=%async_computation.5 | async-start | bytes 1114112 | tf_op jit(solution)/shard_map/all_gather | solution.py:58
  8.7 180.1 %all-gather.9.cloned.1.call-start = ((), (), s32[]{:S(2)}) async-start(), calls=%async_computation.4 | async-start | bytes 2162688 | tf_op jit(solution)/shard_map/all_gather | solution.py:37
  9.4 264.2 %all-gather.7.cloned.1.call-start = ((), (), s32[]{:S(2)}) async-start(), calls=%async_computation.3 | async-start | bytes 2162688 | tf_op jit(solution)/shard_map/all_gather | solution.py:36
  10.0 399.0 %all-reduce.3.cloned.1.call-start = ((), (), s32[]{:S(2)}) async-start(), calls=%async_computation.8 | async-start | bytes 5242880 | tf_op jit(solution)/shard_map/psum | solution.py:29
  53.1 220.5 %copy-start.1 = (bf16[128,4096]{1,0:T(8,128)(2,1)S(1)}, bf16[128,4096]{1,0:T(8,128)(2,1)}, u32[]{:S(2)}) copy-start(bf16[128,4096]{1,0:T(8,128)(2,1)} %all-gather.5.cloned.1.call-done) | copy-start | bytes 3145732
  277.2 3.6 copy-start.4
  280.8 1.2 copy-start.3
  280.8 364.0 %reduce-scatter.7.cloned.1.call-start = ((), (), s32[]{:S(2)}) async-start(), calls=%async_computation.7 | async-start | bytes 2162688
  288.1 586.9 %reduce-scatter.5.cloned.1.call-start = ((), (), s32[]{:S(2)}) async-start(), calls=%async_computation.6 | async-start | bytes 2162688 | tf_op jit(solution)/shard_map/reduce_scatter | solution.py:95
  290.4 2.4 copy-start.2
  409.0 3.1 copy-start.6
  409.0 466.0 %copy-start.5 = (bf16[128,2048]{1,0:T(8,128)(2,1)S(1)}, bf16[128,2048]{1,0:T(8,128)(2,1)}, u32[]{:S(2)}) copy-start(bf16[128,2048]{1,0:T(8,128)(2,1)} %get-tuple-element.21) | copy-start | bytes 1572868
Sparse Core Ops, SparseCore 0:
  10.1 43.0 all-gather.4
  55.2 39.4 all-gather.10
  97.8 90.9 all-gather.8
  191.8 81.7 all-gather.6
  281.0 128.0 all-reduce.2
  413.3 231.4 reduce-scatter.6
  650.5 224.4 reduce-scatter.4
where the time goes:
time: 883 us
  waiting for transfers between devices  835 us (95%)
  matrix products  15.1 us (2%)
  between operations  14.3 us (2%)
  local copies, waits for them, and re-layouts  9.02 us (1%)
    unnamed x8, waiting for transfers between devices  234 us
    reduce_scatter x1, waiting for transfers between devices, per_device(): lax.psum_scatter(lax.dot_general(normed, grad_q, contract_first, preferre...  229 us
    psum x1, waiting for transfers between devices, per_device(): lax.psum(newer_partial[0].astype(jnp.float32).astype(jnp.bfloat16), 'tens...  115 us
    all_gather x1, waiting for transfers between devices, per_device(): out_full = lax.all_gather(out_weight, 'fsdp', axis=1, tiled=True)  94.1 us
    all_gather x1, waiting for transfers between devices, per_device(): query_full = lax.all_gather(query_weight, 'fsdp', axis=0, tiled=True)  81.9 us
    all_gather x1, waiting for transfers between devices, per_device(): whole = lax.all_gather(stream_in, 'tensor', axis=1, tiled=True)  42.2 us
    all_gather x1, waiting for transfers between devices, per_device(): grad_attn = lax.all_gather(cot_attn, 'tensor', axis=1, tiled=True)  40 us
  transfers between devices with their start and end apart: 7, of which 7 were waited for; matrix products, arithmetic and copies ran while one was open for 3% of the time, Pallas kernels for 0%

commit v1 on v0

v1 whole, which is shorter than its diff:
```python
import math

import jax
import jax.numpy as jnp
from jax import lax
from jax.experimental import pallas as pl
from jax.experimental.pallas import tpu as pltpu
from jax.sharding import Mesh, PartitionSpec as P

HS = 128
GROUP = 4
ZH, Y, ZL, X, CORE = 4, 8, 2, 4, 2
NT = ZL * X * CORE
NF = ZH * Y
TENSOR = ("zl", "x", "c")
FSDP = ("zh", "y")
S = 128
W = 256
D = NT * W
B = D // NF
EXTRA = 16
F32, BF16 = jnp.float32, jnp.bfloat16
VMEM = pl.BlockSpec(memory_space=pltpu.VMEM)


def call(body, outs, flops=0, nbytes=0):
    return pl.pallas_call(
        body,
        out_shape=outs,
        out_specs=jax.tree.map(lambda _: VMEM, outs),
        compiler_params=pltpu.CompilerParams(vmem_limit_bytes=56 * 2**20),
        cost_estimate=pl.CostEstimate(flops=flops, bytes_accessed=nbytes, transcendentals=0),
    )


def arr(*dims, of=BF16):
    return jax.ShapeDtypeStruct(dims, of)


def place(f):
    return (f % Y) * ZH + f // Y


def nn(a, b):
    return lax.dot_general(a, b, (((1,), (0,)), ((), ())), preferred_element_type=F32)


def nt(a, b):
    return lax.dot_general(a, b, (((1,), (1,)), ((), ())), preferred_element_type=F32)


def flip(a):
    return a.astype(F32).T


def pack_weights(wq, wo, out):
    out[:, :W] = wq[...]
    out[:, W:] = flip(wo[...]).astype(BF16)


def pack_forward(stream, cot, partial, out):
    for t in range(NT):
        out[t, :S] = stream[...]
        out[t, S : 2 * S] = cot[...]
        out[t, 2 * S :] = partial[0, :, t * W : (t + 1) * W]


def prepare(got, stream, gain, normed, cot, normed_t, cot_t, inv_out, out_slice):
    squares = jnp.zeros((S, 1), F32)
    pending = jnp.zeros((S, W), F32)
    for t in range(NT):
        block = got[t, :S].astype(F32)
        squares += jnp.sum(block * block, -1, keepdims=True)
        pending += got[t, 2 * S :].astype(F32)
    inv = lax.rsqrt(squares * (1.0 / D) + 1e-05)
    inv_out[...] = jnp.broadcast_to(inv, (S, 128))
    out_slice[...] = (stream[...].astype(F32) + pending).astype(BF16)
    for f in range(NF):
        t, half = f // 2, (f % 2) * B
        at = place(f) * B
        block = got[t, :S, half : half + B].astype(F32)
        block = block * inv * gain[:, f * B : (f + 1) * B].astype(F32)
        normed[:, at : at + B] = block.astype(BF16)
        normed_t[at : at + B] = block.T.astype(BF16)
        piece = got[t, S : 2 * S, half : half + B]
        cot[:, at : at + B] = piece
        cot_t[at : at + B] = flip(piece).astype(BF16)


def attend(normed, cot, normed_t, cot_t, weights, kv, terms, att_out, gq_out, kv_out):
    scale = 1.0 / math.sqrt(HS)
    step = 512

    def gather(i, carry):
        q, g = carry
        k = pl.ds(pl.multiple_of(i * step, step), step)
        q += nn(normed[:, k], weights[k, :W])
        g += nn(cot[:, k], weights[k, W:])
        return q, g

    zero = jnp.zeros((S, W), F32)
    queries, grads = lax.fori_loop(0, D // step, gather, (zero, zero))
    queries, grads = queries.astype(BF16), grads.astype(BF16)
    keys, values = kv[:, :HS], kv[:, HS:]
    causal = lax.broadcasted_iota(jnp.int32, (S, S), 0) >= lax.broadcasted_iota(jnp.int32, (S, S), 1)
    grad_keys = jnp.zeros((S, HS), F32)
    grad_values = jnp.zeros((S, HS), F32)
    for h in range(W // HS):
        at = slice(h * HS, (h + 1) * HS)
        q, g = queries[:, at], grads[:, at]
        scores = jnp.where(causal, nt(q, keys) * scale, -1e30)
        weight = jnp.exp(scores - jnp.max(scores, -1, keepdims=True))
        probs = weight / jnp.sum(weight, -1, keepdims=True)
        low = probs.astype(BF16)
        att = nn(low, values).astype(BF16)
        delta = jnp.sum(g.astype(F32) * att.astype(F32), -1, keepdims=True)
        gs = (probs * (nt(g, values) - delta) * scale).astype(BF16)
        gq_out[:, at] = nn(gs, keys).astype(BF16)
        att_out[:, at] = att
        grad_keys += nn(flip(gs).astype(BF16), q)
        grad_values += nn(flip(low).astype(BF16), g)
    kv_out[:, :HS] = grad_keys.astype(BF16)
    kv_out[:, HS:] = grad_values.astype(BF16)
    att, gq = att_out[...], gq_out[...]

    def scatter(i, _):
        k = pl.ds(pl.multiple_of(i * step, step), step)
        terms[k, :W] = nn(normed_t[k], gq).astype(BF16)
        terms[k, W:] = nn(cot_t[k], att).astype(BF16)
        return 0

    lax.fori_loop(0, D // step, scatter, 0)


def project(att, gq, weights, got, gain, kv_part, out_slice, partial, send):
    rows = jnp.zeros((S, 1), F32)
    for y in range(Y):
        k = slice(y * ZH * B, (y + 1) * ZH * B)
        out = nt(att[...], weights[k, W:]).astype(BF16)
        grad = nt(gq[...], weights[k, :W]).astype(BF16)
        for z in range(ZH):
            f = z * Y + y
            t, half = f // 2, (f % 2) * B
            block = grad[:, z * B : (z + 1) * B]
            partial[0, :, f * B : (f + 1) * B] = out[:, z * B : (z + 1) * B]
            send[t, :S, half : half + B] = block
            stream = got[t, :, half : half + B].astype(F32)
            scaled = gain[:, f * B : (f + 1) * B].astype(F32) * block.astype(F32)
            rows += jnp.sum(scaled * stream, -1, keepdims=True)
    across = jnp.broadcast_to(rows, (S, S)).T[:EXTRA]
    high = across.astype(BF16).astype(F32)
    middle = (across - high).astype(BF16).astype(F32)
    low = across - high - middle
    line = lax.broadcasted_iota(jnp.int32, (EXTRA, S), 0)
    zero = jnp.zeros_like(low)
    pieces = jnp.where(line == 0, high, jnp.where(line == 1, middle, jnp.where(line == 2, low, zero)))
    pieces = jnp.concatenate([pieces, jnp.zeros((EXTRA, W - S), F32)], 1).astype(BF16)
    for t in range(NT):
        send[t, S : 2 * S] = kv_part[...]
        send[t, 2 * S : 3 * S] = out_slice[...]
        send[t, 3 * S :] = pieces


def finish(got, stream, cot_stream, gain, inv_in, stream_out, stream_grad, kv_grad):
    grad = jnp.zeros((S, W), F32)
    lines = jnp.zeros((EXTRA, S), F32)
    for t in range(NT):
        grad += got[t, :S].astype(F32)
        lines += got[t, 3 * S :, :S].astype(F32)
        stream_out[:, t * W : (t + 1) * W] = got[t, 2 * S : 3 * S]
    share = GROUP * HS // W
    for j in range(NT // share):
        total = got[share * j, S : 2 * S].astype(F32)
        for i in range(1, share):
            total += got[share * j + i, S : 2 * S].astype(F32)
        kv_grad[:, j * W : (j + 1) * W] = total.astype(BF16)
    total = jnp.sum(lines, 0, keepdims=True)
    mean = jnp.broadcast_to(total, (S, S)).T[:, :1] * (1.0 / D)
    inv = inv_in[:, :1]
    grad = inv * (gain[...].astype(F32) * grad) - stream[...].astype(F32) * (inv * inv * inv) * mean
    stream_grad[...] = (cot_stream[...].astype(F32) + grad).astype(BF16)


def add_up(got, wq_grad, wo_grad):
    total = got[0].astype(F32)
    for z in range(1, ZH):
        total += got[z].astype(F32)
    wq_grad[...] = total[:, :W].astype(BF16)
    wo_grad[...] = total[:, W:].T.astype(BF16)


def per_device(
    stream_in, newer_partial, norm_gain, query_weight, keys_values, out_weight, cot_stream, cot_attn
):
    rank = lax.axis_index(TENSOR)
    gain = norm_gain.reshape(1, D)
    gain_own = lax.dynamic_slice_in_dim(gain, rank * W, W, 1)
    kv_own = lax.dynamic_slice_in_dim(keys_values, rank * W // HS // GROUP * 2 * HS, 2 * HS, 1)

    weights = call(pack_weights, arr(B, 2 * W))(query_weight, out_weight)
    weights = lax.all_gather(weights, "zh", axis=0, tiled=True)
    weights = lax.all_gather(weights, "y", axis=0, tiled=True)

    send = call(pack_forward, arr(NT, 3 * S, W))(stream_in, cot_attn, newer_partial)
    got = lax.all_to_all(send, TENSOR, 0, 0, tiled=True)
    normed, cot, normed_t, cot_t, inv, out_slice = call(
        prepare, [arr(S, D), arr(S, D), arr(D, S), arr(D, S), arr(S, 128, of=F32), arr(S, W)]
    )(got, stream_in, gain)

    terms, att, gq, kv_part = call(
        attend, [arr(D, 2 * W), arr(S, W), arr(S, W), arr(S, 2 * HS)], flops=8 * S * D * W
    )(normed, cot, normed_t, cot_t, weights, kv_own)

    terms = lax.psum_scatter(terms, "y", scatter_dimension=0, tiled=True)
    terms = lax.all_to_all(terms.reshape(ZH, B, 2 * W), "zh", 0, 0, tiled=True)
    wq_grad, wo_grad = call(add_up, [arr(B, W), arr(W, B)])(terms)

    attn_partial, send = call(
        project, [arr(1, S, D), arr(NT, 3 * S + EXTRA, W)], flops=4 * S * D * W
    )(att, gq, weights, got[:, :S], gain, kv_part, out_slice)
    got = lax.all_to_all(send, TENSOR, 0, 0, tiled=True)
    stream_out, stream_grad, kv_grad = call(finish, [arr(S, D), arr(S, W), arr(*keys_values.shape)])(
        got, stream_in, cot_stream, gain_own, inv
    )
    return (stream_out, attn_partial, stream_grad, kv_grad, wq_grad, wo_grad)


def solution(mesh):
    fine = Mesh(mesh.devices.reshape(ZH, Y, ZL, X, CORE), FSDP + TENSOR)
    return jax.shard_map(
        per_device,
        mesh=fine,
        in_specs=(
            P(FSDP, TENSOR),
            P(TENSOR, FSDP, None),
            P(),
            P(FSDP, TENSOR),
            P(FSDP, None),
            P(TENSOR, FSDP),
            P(FSDP, TENSOR),
            P(FSDP, TENSOR),
        ),
        out_specs=(
            P(FSDP, None),
            P(TENSOR, FSDP, None),
            P(FSDP, TENSOR),
            P(FSDP, None),
            P(FSDP, TENSOR),
            P(TENSOR, FSDP),
        ),
        check_vma=False,
    )
```

time: 883 us -> 192 us (0.22)
  waiting for transfers between devices: 835 us -> 59.6 us
  blocking collectives: 0 us -> 66 us
  Pallas kernels: 0 us -> 32.2 us
  matrix products: 15.1 us -> 0 us
  starting transfers between devices: 0.27 us -> 14.7 us
    all_gather x4 -> x1, waiting for transfers between devices: 258 us -> 0.01 us  [per_device(): weights = lax.all_gather(weights, 'y', axis=0, tiled=True)]
    unnamed x8 -> x2, waiting for transfers between devices: 234 us -> 0.03 us
    reduce_scatter x1, waiting for transfers between devices: 229 us -> 4.2 us  [per_device(): terms = lax.psum_scatter(terms, 'y', scatter_dimension=0, tiled=True)]
    psum x1 -> x0, waiting for transfers between devices: 115 us -> none  [per_device(): lax.psum(newer_partial[0].astype(jnp.float32).astype(jnp.bfloat16), 'tens...]
    all_to_all x0 -> x2, waiting for transfers between devices: none -> 55.4 us  [the longest x1 44.1 us: per_device(): got = lax.all_to_all(send, TENSOR, 0, 0, tiled=True)]
    all_to_all x0 -> x1, blocking collectives: none -> 43.6 us  [per_device(): got = lax.all_to_all(send, TENSOR, 0, 0, tiled=True)]
    pallas_call x0 -> x7, Pallas kernels: none -> 32.2 us  [the longest x1 11 us: per_device(): call(attend, [arr(D, 2 * W), arr(S, W), arr(S, W), arr(S, 2 * HS)], flops...]
    all_gather x0 -> x1, blocking collectives: none -> 22.4 us  [per_device(): weights = lax.all_gather(weights, 'zh', axis=0, tiled=True)]
  transfers between devices with their start and end apart: 7 -> 4, of which waited for: 7 -> 3; matrix products, arithmetic and copies ran while one was open for 3% -> 2% of each run, Pallas kernels for 0% -> 9%
where the time goes in v1:
time: 192 us
  blocking collectives  66 us (34%)
  waiting for transfers between devices  59.6 us (31%)
  Pallas kernels  32.2 us (17%)
  starting transfers between devices  14.7 us (8%)
  between operations  14.1 us (7%)
  local copies, waits for them, and re-layouts  4.98 us (3%)
    all_to_all x1, waiting for transfers between devices, per_device(): got = lax.all_to_all(send, TENSOR, 0, 0, tiled=True)  44.1 us
    all_to_all x1, blocking collectives, per_device(): got = lax.all_to_all(send, TENSOR, 0, 0, tiled=True)  43.6 us
    all_gather x1, blocking collectives, per_device(): weights = lax.all_gather(weights, 'zh', axis=0, tiled=True)  22.4 us
    all_to_all x1, waiting for transfers between devices, per_device(): terms = lax.all_to_all(terms.reshape(ZH, B, 2 * W), 'zh', 0, 0, tiled=True)  11.3 us
    pallas_call x1, Pallas kernels, per_device(): call(attend, [arr(D, 2 * W), arr(S, W), arr(S, W), arr(S, 2 * HS)], flops...  11 us
    all_to_all x1, starting transfers between devices, per_device(): terms = lax.all_to_all(terms.reshape(ZH, B, 2 * W), 'zh', 0, 0, tiled=True)  7.37 us
    all_to_all x1, starting transfers between devices, per_device(): got = lax.all_to_all(send, TENSOR, 0, 0, tiled=True)  7.27 us
    pallas_call x1, Pallas kernels, per_device(): call(project, [arr(1, S, D), arr(NT, 3 * S + EXTRA, W)], flops=4 * S * D...  6.21 us
  transfers between devices with their start and end apart: 4, of which 3 were waited for; matrix products, arithmetic and copies ran while one was open for 2% of the time, Pallas kernels for 9%

profile of v1, /device:TPU:6, one launch (start us, length us, event | category | flops | bytes accessed | tf_op | source)
XLA Modules:
  0.0 191.6 jit_solution(17829643167480625356)
XLA Ops:
  7.2 0.0 all-gather.2.cloned.1.call-start
  7.2 1.7 shard_map.129
  8.9 22.4 %all_gather.6 = bf16[512,512]{1,0:T(8,128)(2,1)} all-gather(bf16[128,512]{1,0:T(8,128)(2,1)} %shard_map.129), channel_id=1, replica_groups=mesh['zh'=4,'y'=8,'zl'=2,'x'=4,'c'=2] {'zh'}, dimensions={0}, use_global_device_ids=true | all-gather | bytes 655360 | tf_op jit(solution)/shard_map/all_gather | solution.py:201
  31.3 0.0 all-gather.2.cloned.1.call-update
  31.4 3.2 %shard_map.127 = bf16[16,384,256]{2,1,0:T(8,128)(2,1)} custom-call(bf16[128,256]{1,0:T(8,128)(2,1)} %stream.5, bf16[128,256]{1,0:T(8,128)(2,1)} %cot.1, bf16[1,128,4096]{2,1,0:T(8,128)(2,1)} %partial.1), custom_call_target="tpu_custom_call" | custom-call | tf_op jit(solution)/shard_map/pallas_call | solution.py:204
  34.6 7.3 %all-to-all-start = ((bf16[16,384,256]{2,1,0:T(8,128)(2,1)}), bf16[16,384,256]{2,1,0:T(8,128)(2,1)}, u32[]{:S(2)}, u32[]{:S(2)}) async-start(bf16[16,384,256]{2,1,0:T(8,128)(2,1)} %shard_map.127), calls=%async_computation | async-start | bytes 6291456 | tf_op jit(solution)/shard_map/all_to_all | solution.py:205
  41.8 0.0 reduce-scatter.2.cloned.1.call-start
  41.9 0.6 reshape.19.gain
  42.5 0.6 constant_dynamic-slice_fusion.kv
  43.2 44.1 %all-to-all-done.got = bf16[16,384,256]{2,1,0:T(8,128)(2,1)} async-done(((bf16[16,384,256]{2,1,0:T(8,128)(2,1)}), bf16[16,384,256]{2,1,0:T(8,128)(2,1)}, u32[]{:S(2)}, u32[]{:S(2)}) %all-to-all-start) | async-done | bytes 3145760 | tf_op jit(solution)/shard_map/all_to_all | solution.py:205
  87.3 4.9 %shard_map.128 = (bf16[128,4096]{1,0:T(8,128)(2,1)}, bf16[128,4096]{1,0:T(8,128)(2,1)}, bf16[4096,128]{1,0:T(8,128)(2,1)}, bf16[4096,128]{1,0:T(8,128)(2,1)}, f3...) custom-call(bf16[16,384,256]{2,1,0:T(8,128)(2,1)} %all-to-all-done.got, bf16[128,256]{1,0:T(8,128)(2,1)} %stream.5, ...), custom_call_target="tpu_custom_call" | custom-call | tf_op jit(solution)/shard_map/pallas_call | solution.py:206
  92.2 11.0 %shard_map.130 = (bf16[4096,512]{1,0:T(8,128)(2,1)}, bf16[128,256]{1,0:T(8,128)(2,1)}, bf16[128,256]{1,0:T(8,128)(2,1)}, bf16[128,256]{1,0:T(8,128)(2,1)}) custom-call(bf16[128,4096]{1,0:T(8,128)(2,1)} %get-tuple-element.23.normed, bf16[128,4096]{1,0:T(8,128)(2,1)} %get-tuple-element.24.cot, bf16[4096,128]{1,0:T(8,128)(2,1)} %get-tuple-element.25.normed_t, ...), custom_call_target="tpu_custom_call" | custom-call | flops 1073741824 | tf_op jit(solution)/shard_map/pallas_call | solution.py:210
  103.2 0.0 reduce-scatter.2.cloned.1.call-update
  103.2 2.3 %slice.4.got = bf16[16,128,256]{2,1,0:T(8,128)(2,1)} slice(bf16[16,384,256]{2,1,0:T(8,128)(2,1)} %all-to-all-done.got), slice={[0:16], [0:128], [0:256]} | slice | bytes 2097152 | tf_op jit(solution)/shard_map/slice | solution.py:220
  105.5 6.2 %shard_map.131 = (bf16[1,128,4096]{2,1,0:T(8,128)(2,1)}, bf16[16,400,256]{2,1,0:T(8,128)(2,1)}) custom-call(bf16[128,256]{1,0:T(8,128)(2,1)} %get-tuple-element.27.att, bf16[128,256]{1,0:T(8,128)(2,1)} %get-tuple-element.28.gq, bf16[4096,512]{1,0:T(8,128)(2,1)} %all-gather.2.cloned.1.call-done.weights, bf16[16,128,256]{2,1,0:T(8,128)(2,1)} %slice.4.got, ...), custom_call_target="tpu_custom_call" | custom-call | flops 536870912 | tf_op jit(solution)/shard_map/pallas_call | solution.py:218
  111.7 43.6 %all_to_all.15.got = bf16[16,400,256]{2,1,0:T(8,128)(2,1)} all-to-all(bf16[16,400,256]{2,1,0:T(8,128)(2,1)} %get-tuple-element.31), channel_id=1, replica_groups=mesh['zh'=4,'y'=8,'zl'=2,'x'=4,'c'=2] {'zl','x','c'}, dimensions={0} | all-to-all | bytes 6553600 | tf_op jit(solution)/shard_map/all_to_all | solution.py:221
  155.3 4.2 %reduce-scatter.2.cloned.1.call-done = bf16[512,512]{1,0:T(8,128)(2,1)} async-done(((bf16[4096,512]{1,0:T(8,128)(2,1)}), bf16[512,512]{1,0:T(8,128)(2,1)}) %reduce-scatter.2.cloned.1.call-update) | async-done | bytes 524304 | tf_op jit(solution)/shard_map/reduce_scatter | solution.py:214
  159.5 7.4 %all-to-all-start.2 = ((bf16[4,128,512]{2,1,0:T(8,128)(2,1)}), bf16[4,128,512]{2,1,0:T(8,128)(2,1)S(1)}, u32[]{:S(2)}, u32[]{:S(2)}) async-start(bf16[4,128,512]{2,1,0:T(8,128)(2,1)} %bitcast.1), calls=%async_computation.3 | async-start | bytes 1048576 | tf_op jit(solution)/shard_map/all_to_all | solution.py:215
  166.8 0.1 dynamic-slice.3
  166.9 0.6 dynamic_slice.7.gain
  167.5 3.4 %shard_map.132 = (bf16[128,4096]{1,0:T(8,128)(2,1)}, bf16[128,256]{1,0:T(8,128)(2,1)}, bf16[128,2048]{1,0:T(8,128)(2,1)}) custom-call(bf16[16,400,256]{2,1,0:T(8,128)(2,1)} %all_to_all.15.got, bf16[128,256]{1,0:T(8,128)(2,1)} %stream.5, bf16[128,256]{1,0:T(8,128)(2,1)} %cot_stream.1, bf16[1,256]{1,0:T(2,128)(2,1)} %dynamic_slice.7.gain, ...), custom_call_target="tpu_custom_call" | custom-call | tf_op jit(solution)/shard_map/pallas_call | solution.py:222
  170.9 11.3 %all-to-all-done.2.got = bf16[4,128,512]{2,1,0:T(8,128)(2,1)S(1)} async-done(((bf16[4,128,512]{2,1,0:T(8,128)(2,1)}), bf16[4,128,512]{2,1,0:T(8,128)(2,1)S(1)}, u32[]{:S(2)}, u32[]{:S(2)}) %all-to-all-start.2) | async-done | bytes 524320 | tf_op jit(solution)/shard_map/all_to_all | solution.py:215
  182.2 0.8 copy-done.1
  183.0 1.8 shard_map.133
  (6 shorter events, 0.0 us)
Async XLA Ops:
  7.2 35.4 %copy-start = (bf16[128,2048]{1,0:T(8,128)(2,1)S(1)}, bf16[128,2048]{1,0:T(8,128)(2,1)}, u32[]{:S(2)}) copy-start(bf16[128,2048]{1,0:T(8,128)(2,1)} %param.12) | copy-start | bytes 1572868
  7.2 85.0 %all-gather.2.cloned.1.call-start = ((), (), s32[]{:S(2)}) async-start(), calls=%async_computation.4 | async-start | bytes 4718592 | tf_op jit(solution)/shard_map/all_gather | solution.py:202
  34.6 7.4 %copy-start.2 = (bf16[4096]{0:T(1024)(128)(2,1)S(1)}, bf16[4096]{0:T(1024)(128)(2,1)}, u32[]{:S(2)}) copy-start(bf16[4096]{0:T(1024)(128)(2,1)} %param.10) | copy-start | bytes 24580
  34.6 52.7 %all-to-all-start = ((bf16[16,384,256]{2,1,0:T(8,128)(2,1)}), bf16[16,384,256]{2,1,0:T(8,128)(2,1)}, u32[]{:S(2)}, u32[]{:S(2)}) async-start(bf16[16,384,256]{2,1,0:T(8,128)(2,1)} %shard_map.127), calls=%async_computation | async-start | bytes 6291456 | tf_op jit(solution)/shard_map/all_to_all | solution.py:205
  41.8 117.6 %reduce-scatter.2.cloned.1.call-start = ((), (), s32[]{:S(2)}) async-start(), calls=%async_computation.5 | async-start | bytes 4718592 | tf_op jit(solution)/shard_map/reduce_scatter | solution.py:214
  159.5 22.7 %all-to-all-start.2 = ((bf16[4,128,512]{2,1,0:T(8,128)(2,1)}), bf16[4,128,512]{2,1,0:T(8,128)(2,1)S(1)}, u32[]{:S(2)}, u32[]{:S(2)}) async-start(bf16[4,128,512]{2,1,0:T(8,128)(2,1)} %bitcast.1), calls=%async_computation.3 | async-start | bytes 1048576 | tf_op jit(solution)/shard_map/all_to_all | solution.py:215
  182.2 0.8 copy-start.1
Sparse Core Ops, SparseCore 0:
  31.5 57.3 all-gather.1
  103.3 56.1 reduce-scatter.1

commit v2 on v1

--- a/solution.py
+++ b/solution.py
@@ -20,16 +20,19 @@
 B = D // NF
 EXTRA = 16
 F32, BF16 = jnp.float32, jnp.bfloat16
+ANY = pl.BlockSpec(memory_space=pl.ANY)
 VMEM = pl.BlockSpec(memory_space=pltpu.VMEM)
-
-
-def call(body, outs, flops=0, nbytes=0):
+SMEM = pl.BlockSpec(memory_space=pltpu.SMEM)
+R = ZH * B
+
+
+def call(body, outs, flops=0, nbytes=0, **specs):
     return pl.pallas_call(
         body,
         out_shape=outs,
-        out_specs=jax.tree.map(lambda _: VMEM, outs),
         compiler_params=pltpu.CompilerParams(vmem_limit_bytes=56 * 2**20),
         cost_estimate=pl.CostEstimate(flops=flops, bytes_accessed=nbytes, transcendentals=0),
+        **specs,
     )
 
 
@@ -54,11 +57,11 @@
 
 
 def pack_weights(wq, wo, out):
-    out[:, :W] = wq[...]
-    out[:, W:] = flip(wo[...]).astype(BF16)
-
-
-def pack_forward(stream, cot, partial, out):
+    out[0] = wq[...]
+    out[1] = flip(wo[...]).astype(BF16)
+
+
+def pack_forward(stream, cot, partial, _, out):
     for t in range(NT):
         out[t, :S] = stream[...]
         out[t, S : 2 * S] = cot[...]
@@ -87,19 +90,28 @@
         cot_t[at : at + B] = flip(piece).astype(BF16)
 
 
-def attend(normed, cot, normed_t, cot_t, weights, kv, terms, att_out, gq_out, kv_out):
+def rows_of(me, distance):
+    return lax.rem(me + (distance + Y), Y)
+
+
+def block(index):
+    return pl.ds(pl.multiple_of(index * R, R), R)
+
+
+FIRST, REST = (4, 3), (5, 2, 6, 1, 7, 0)
+
+
+def attend(me, normed, cot, normed_t, cot_t, kv, *refs):
+    wq, wo = refs[0], refs[1 : Y + 1]
+    q_terms, *o_terms = refs[Y + 1 : Y + 4]
+    att_out, gq_out, kv_out = refs[Y + 4 :]
     scale = 1.0 / math.sqrt(HS)
-    step = 512
-
-    def gather(i, carry):
-        q, g = carry
-        k = pl.ds(pl.multiple_of(i * step, step), step)
-        q += nn(normed[:, k], weights[k, :W])
-        g += nn(cot[:, k], weights[k, W:])
-        return q, g
-
-    zero = jnp.zeros((S, W), F32)
-    queries, grads = lax.fori_loop(0, D // step, gather, (zero, zero))
+    queries = jnp.zeros((S, W), F32)
+    grads = jnp.zeros((S, W), F32)
+    for d in range(Y):
+        k = block(rows_of(me[0], d))
+        queries += nn(normed[:, k], wq[k])
+        grads += nn(cot[:, k], wo[d][...])
     queries, grads = queries.astype(BF16), grads.astype(BF16)
     keys, values = kv[:, :HS], kv[:, HS:]
     causal = lax.broadcasted_iota(jnp.int32, (S, S), 0) >= lax.broadcasted_iota(jnp.int32, (S, S), 1)
@@ -121,31 +133,37 @@
         grad_values += nn(flip(low).astype(BF16), g)
     kv_out[:, :HS] = grad_keys.astype(BF16)
     kv_out[:, HS:] = grad_values.astype(BF16)
-    att, gq = att_out[...], gq_out[...]
-
-    def scatter(i, _):
-        k = pl.ds(pl.multiple_of(i * step, step), step)
-        terms[k, :W] = nn(normed_t[k], gq).astype(BF16)
-        terms[k, W:] = nn(cot_t[k], att).astype(BF16)
-        return 0
-
-    lax.fori_loop(0, D // step, scatter, 0)
-
-
-def project(att, gq, weights, got, gain, kv_part, out_slice, partial, send):
+    write_terms(me, cot_t, att_out, o_terms, FIRST)
+    gq = gq_out[...]
+    for y in range(Y):
+        q_terms[y * R : (y + 1) * R] = nn(normed_t[y * R : (y + 1) * R], gq).astype(BF16)
+
+
+def write_terms(me, cot_t, att, outs, distances):
+    for d, out in zip(distances, outs):
+        out[...] = nn(cot_t[block(rows_of(me[0], d))], att[...]).astype(BF16)
+
+
+def attend_rest(me, cot_t, att, *outs):
+    write_terms(me, cot_t, att, outs, REST)
+
+
+def project(me, att, gq, got, gain, kv_part, out_slice, *refs):
+    wq, wo, (partial, send) = refs[0], refs[1 : Y + 1], refs[Y + 1 :]
     rows = jnp.zeros((S, 1), F32)
-    for y in range(Y):
-        k = slice(y * ZH * B, (y + 1) * ZH * B)
-        out = nt(att[...], weights[k, W:]).astype(BF16)
-        grad = nt(gq[...], weights[k, :W]).astype(BF16)
+    for d in range(Y):
+        y = rows_of(me[0], d)
+        out = nt(att[...], wo[d][...]).astype(BF16)
+        grad = nt(gq[...], wq[block(y)]).astype(BF16)
+        half = pl.ds(pl.multiple_of(lax.rem(y, 2) * B, B), B)
         for z in range(ZH):
-            f = z * Y + y
-            t, half = f // 2, (f % 2) * B
-            block = grad[:, z * B : (z + 1) * B]
-            partial[0, :, f * B : (f + 1) * B] = out[:, z * B : (z + 1) * B]
-            send[t, :S, half : half + B] = block
-            stream = got[t, :, half : half + B].astype(F32)
-            scaled = gain[:, f * B : (f + 1) * B].astype(F32) * block.astype(F32)
+            t = z * (Y // 2) + y // 2
+            at = pl.ds(pl.multiple_of((z * Y + y) * B, B), B)
+            piece = grad[:, z * B : (z + 1) * B]
+            partial[0, :, at] = out[:, z * B : (z + 1) * B]
+            send[t, :S, half] = piece
+            stream = got[t, :, half].astype(F32)
+            scaled = gain[:, at].astype(F32) * piece.astype(F32)
             rows += jnp.sum(scaled * stream, -1, keepdims=True)
     across = jnp.broadcast_to(rows, (S, S)).T[:EXTRA]
     high = across.astype(BF16).astype(F32)
@@ -159,6 +177,13 @@
         send[t, S : 2 * S] = kv_part[...]
         send[t, 2 * S : 3 * S] = out_slice[...]
         send[t, 3 * S :] = pieces
+
+
+def close(q, own, went_up, went_down, _, out):
+    o = own[...].astype(F32) + went_up[...].astype(F32) + went_down[...].astype(F32)
+    for z in range(ZH):
+        out[z, :B] = q[z * B : (z + 1) * B]
+        out[z, B:] = o[z * B : (z + 1) * B].astype(BF16)
 
 
 def finish(got, stream, cot_stream, gain, inv_in, stream_out, stream_grad, kv_grad):
@@ -185,8 +210,39 @@
     total = got[0].astype(F32)
     for z in range(1, ZH):
         total += got[z].astype(F32)
-    wq_grad[...] = total[:, :W].astype(BF16)
-    wo_grad[...] = total[:, W:].T.astype(BF16)
+    wq_grad[...] = total[:B].astype(BF16)
+    wo_grad[...] = total[B:].T.astype(BF16)
+
+
+def up(a):
+    return lax.ppermute(a, "y", [(i, (i + 1) % Y) for i in range(Y)])
+
+
+def down(a):
+    return lax.ppermute(a, "y", [(i, (i - 1) % Y) for i in range(Y)])
+
+
+def gather_ring(own):
+    blocks = {0: own}
+    for step in range(1, 5):
+        blocks[step] = down(blocks[step - 1])
+        if step < 4:
+            blocks[-step % Y] = up(blocks[(1 - step) % Y])
+    return [blocks[d] for d in range(Y)]
+
+
+def plus(a, b):
+    return (a.astype(F32) + b.astype(F32)).astype(BF16)
+
+
+def scatter_ring(terms):
+    went_up, went_down = terms[3], terms[4]
+    for step in range(3):
+        went_down = plus(down(went_down), terms[5 + step])
+        went_up = up(went_up)
+        if step < 2:
+            went_up = plus(went_up, terms[2 - step])
+    return terms[0], went_up, down(went_down)
 
 
 def per_device(
@@ -197,31 +253,52 @@
     gain_own = lax.dynamic_slice_in_dim(gain, rank * W, W, 1)
     kv_own = lax.dynamic_slice_in_dim(keys_values, rank * W // HS // GROUP * 2 * HS, 2 * HS, 1)
 
-    weights = call(pack_weights, arr(B, 2 * W))(query_weight, out_weight)
-    weights = lax.all_gather(weights, "zh", axis=0, tiled=True)
-    weights = lax.all_gather(weights, "y", axis=0, tiled=True)
-
-    send = call(pack_forward, arr(NT, 3 * S, W))(stream_in, cot_attn, newer_partial)
+    me = lax.axis_index("y").reshape(1)
+
+    weights = call(pack_weights, arr(2, B, W))(query_weight, out_weight)
+    weights = lax.all_gather(weights, "zh", axis=1, tiled=True)
+    wq = lax.all_gather(weights[0], "y", axis=0, tiled=True)
+    wo = gather_ring(weights[1])
+
+    send = call(pack_forward, arr(NT, 3 * S, W), in_specs=[VMEM] * 3 + [ANY])(
+        stream_in, cot_attn, newer_partial, weights
+    )
     got = lax.all_to_all(send, TENSOR, 0, 0, tiled=True)
     normed, cot, normed_t, cot_t, inv, out_slice = call(
         prepare, [arr(S, D), arr(S, D), arr(D, S), arr(D, S), arr(S, 128, of=F32), arr(S, W)]
     )(got, stream_in, gain)
 
-    terms, att, gq, kv_part = call(
-        attend, [arr(D, 2 * W), arr(S, W), arr(S, W), arr(S, 2 * HS)], flops=8 * S * D * W
-    )(normed, cot, normed_t, cot_t, weights, kv_own)
-
-    terms = lax.psum_scatter(terms, "y", scatter_dimension=0, tiled=True)
-    terms = lax.all_to_all(terms.reshape(ZH, B, 2 * W), "zh", 0, 0, tiled=True)
-    wq_grad, wo_grad = call(add_up, [arr(B, W), arr(W, B)])(terms)
-
+    term = arr(R, W)
+    q_terms, o4, o3, att, gq, kv_part = call(
+        attend,
+        [arr(D, W), term, term, arr(S, W), arr(S, W), arr(S, 2 * HS)],
+        flops=7 * S * D * W,
+        in_specs=[SMEM] + [VMEM] * (6 + Y),
+    )(me, normed, cot, normed_t, cot_t, kv_own, wq, *wo)
+    rest = call(attend_rest, [term] * 6, flops=2 * S * D * W, in_specs=[SMEM] + [VMEM] * 2)(
+        me, cot_t, att
+    )
+    o_terms = {4: o4, 3: o3} | dict(zip(REST, rest))
+
+    streams = pl.BlockSpec((NT, S, W), lambda i: (0, 0, 0))
     attn_partial, send = call(
-        project, [arr(1, S, D), arr(NT, 3 * S + EXTRA, W)], flops=4 * S * D * W
-    )(att, gq, weights, got[:, :S], gain, kv_part, out_slice)
+        project,
+        [arr(1, S, D), arr(NT, 3 * S + EXTRA, W)],
+        flops=4 * S * D * W,
+        grid=(1,),
+        in_specs=[SMEM] + [VMEM] * 2 + [streams] + [VMEM] * (4 + Y),
+        out_specs=[VMEM, VMEM],
+    )(me, att, gq, got, gain, kv_part, out_slice, wq, *wo)
     got = lax.all_to_all(send, TENSOR, 0, 0, tiled=True)
     stream_out, stream_grad, kv_grad = call(finish, [arr(S, D), arr(S, W), arr(*keys_values.shape)])(
         got, stream_in, cot_stream, gain_own, inv
     )
+
+    q_sum = lax.psum_scatter(q_terms, "y", scatter_dimension=0, tiled=True)
+    o_sums = scatter_ring(o_terms)
+    sums = call(close, arr(ZH, 2 * B, W), in_specs=[VMEM] * 4 + [ANY])(q_sum, *o_sums, got)
+    sums = lax.all_to_all(sums, "zh", 0, 0, tiled=True)
+    wq_grad, wo_grad = call(add_up, [arr(B, W), arr(W, B)])(sums)
     return (stream_out, attn_partial, stream_grad, kv_grad, wq_grad, wo_grad)
 
 

time: 192 us -> 204 us (1.062); the launches traced: 192 us -> 202 us
  starting transfers between devices: 14.7 us -> 72.1 us
  blocking collectives: 66 us -> 22.4 us
  waiting for transfers between devices: 59.6 us -> 50.3 us
  other arithmetic: 0 us -> 4.18 us
    ppermute x0 -> x14, starting transfers between devices: none -> 53.4 us  [the longest x8 41.2 us: down(): return lax.ppermute(a, 'y', [(i, (i - 1) % Y) for i in range(Y)])]
    all_to_all x1 -> x2, waiting for transfers between devices: 44.1 us -> 0.01 us  [per_device(): got = lax.all_to_all(send, TENSOR, 0, 0, tiled=True)]
    all_to_all x1 -> x0, blocking collectives: 43.6 us -> none  [per_device(): got = lax.all_to_all(send, TENSOR, 0, 0, tiled=True)]
    ppermute x0 -> x14, waiting for transfers between devices: none -> 42.2 us  [the longest x8 31.4 us: down(): return lax.ppermute(a, 'y', [(i, (i - 1) % Y) for i in range(Y)])]
    all_to_all x1 -> x2, starting transfers between devices: 7.27 us -> 13.4 us  [per_device(): got = lax.all_to_all(send, TENSOR, 0, 0, tiled=True)]
    reduce_scatter x1, waiting for transfers between devices: 4.2 us -> 0.01 us  [per_device(): q_sum = lax.psum_scatter(q_terms, 'y', scatter_dimension=0, tiled=True)]
    convert_element_type x0 -> x5, other arithmetic: none -> 4.18 us  [plus(): return (a.astype(F32) + b.astype(F32)).astype(BF16)]
    all_to_all x1, waiting for transfers between devices: 11.3 us -> 7.31 us  [per_device(): sums = lax.all_to_all(sums, 'zh', 0, 0, tiled=True)]
  transfers between devices with their start and end apart: 4 -> 19, of which waited for: 3 -> 11; matrix products, arithmetic and copies ran while one was open for 2% -> 3% of each run, Pallas kernels for 9% -> 5%
where the time goes in v2:
time: 204 us; the launch traced here: 202 us
  starting transfers between devices  72.1 us (35%)
  waiting for transfers between devices  50.3 us (25%)
  Pallas kernels  33.3 us (16%)
  blocking collectives  22.4 us (11%)
  between operations  14.4 us (7%)
  local copies, waits for them, and re-layouts  4.86 us (2%)
  other arithmetic  4.18 us (2%)
    ppermute x8, starting transfers between devices, down(): return lax.ppermute(a, 'y', [(i, (i - 1) % Y) for i in range(Y)])  41.2 us
    ppermute x8, waiting for transfers between devices, down(): return lax.ppermute(a, 'y', [(i, (i - 1) % Y) for i in range(Y)])  31.4 us
    all_gather x1, blocking collectives, per_device(): weights = lax.all_gather(weights, 'zh', axis=1, tiled=True)  22.4 us
    all_to_all x2, starting transfers between devices, per_device(): got = lax.all_to_all(send, TENSOR, 0, 0, tiled=True)  13.4 us
    ppermute x6, starting transfers between devices, up(): return lax.ppermute(a, 'y', [(i, (i + 1) % Y) for i in range(Y)])  12.2 us
    ppermute x6, waiting for transfers between devices, up(): return lax.ppermute(a, 'y', [(i, (i + 1) % Y) for i in range(Y)])  10.8 us
    pallas_call x1, Pallas kernels, per_device(): call(attend, [arr(D, W), term, term, arr(S, W), arr(S, W), arr(S, 2 * HS)...  7.48 us
    all_to_all x1, waiting for transfers between devices, per_device(): sums = lax.all_to_all(sums, 'zh', 0, 0, tiled=True)  7.31 us
  transfers between devices with their start and end apart: 19, of which 11 were waited for; matrix products, arithmetic and copies ran while one was open for 3% of the time, Pallas kernels for 5%

profile of v2, /device:TPU:6, one launch (start us, length us, event | category | flops | bytes accessed | tf_op | source)
XLA Modules:
  0.0 201.5 jit_solution(8820130360162720949)
XLA Ops:
  8.9 22.4 %all_gather.6._ = bf16[2,512,256]{2,1,0:T(8,128)(2,1)} all-gather(bf16[2,128,256]{2,1,0:T(8,128)(2,1)} %shard_map.127), channel_id=1, replica_groups=mesh['zh'=4,'y'=8,'zl'=2,'x'=4,'c'=2] {'zh'}, dimensions={1}, use_global_device_ids=true | all-gather | bytes 655360 | tf_op jit(solution)/shard_map/all_gather | solution.py:259
  31.3 3.2 %shard_map.128 = bf16[16,384,256]{2,1,0:T(8,128)(2,1)} custom-call(bf16[128,256]{1,0:T(8,128)(2,1)} %stream.5, bf16[128,256]{1,0:T(8,128)(2,1)} %cot.1, bf16[1,128,4096]{2,1,0:T(8,128)(2,1)} %partial.1, bf16[2,512,256]{2,1,0:T(8,128)(2,1)} %all_gather.6._), custom_call_target="tpu_custom_call" | custom-call | tf_op jit(solution)/shard_map/pallas_call | solution.py:263
  34.5 7.3 %all-to-all-start = ((bf16[16,384,256]{2,1,0:T(8,128)(2,1)}), bf16[16,384,256]{2,1,0:T(8,128)(2,1)}, u32[]{:S(2)}, u32[]{:S(2)}) async-start(bf16[16,384,256]{2,1,0:T(8,128)(2,1)} %shard_map.128), calls=%async_computation | async-start | bytes 6291456 | tf_op jit(solution)/shard_map/all_to_all | solution.py:266
  42.5 5.4 %collective-permute-start = (bf16[512,256]{1,0:T(8,128)(2,1)S(1)}, bf16[512,256]{1,0:T(8,128)(2,1)S(1)}, u32[]{:S(2)}, u32[]{:S(2)}) collective-permute-start(bf16[512,256]{1,0:T(8,128)(2,1)S(1)} %get-tuple-element.56.refs_1_), channel_id=1, source_target_pairs={{0,112},{16,0},{32,16},{48,32},{64,48},{80,64},{96,80},{112,96},{1... | collective-permute-start | bytes 786440 | tf_op jit(solution)/shard_map/ppermute | solution.py:222
  49.9 3.9 %collective-permute-done.refs_2_ = bf16[512,256]{1,0:T(8,128)(2,1)S(1)} collective-permute-done((bf16[512,256]{1,0:T(8,128)(2,1)S(1)}, bf16[512,256]{1,0:T(8,128)(2,1)S(1)}, u32[]{:S(2)}, u32[]{:S(2)}) %collective-permute-start) | collective-permute-done | bytes 262176 | tf_op jit(solution)/shard_map/ppermute | solution.py:222
  53.8 5.6 %collective-permute-start.1 = (bf16[512,256]{1,0:T(8,128)(2,1)S(1)}, bf16[512,256]{1,0:T(8,128)(2,1)S(1)}, u32[]{:S(2)}, u32[]{:S(2)}) collective-permute-start(bf16[512,256]{1,0:T(8,128)(2,1)S(1)} %collective-permute-done.refs_2_), channel_id=1, source_target_pairs={{0,112},{16,0},{32,16},{48,32},{64,48},{80,64},{96,80},{112,96},{1... | collective-permute-start | bytes 786440 | tf_op jit(solution)/shard_map/ppermute | solution.py:222
  61.3 9.0 %collective-permute-done.1.refs_3_ = bf16[512,256]{1,0:T(8,128)(2,1)S(1)} collective-permute-done((bf16[512,256]{1,0:T(8,128)(2,1)S(1)}, bf16[512,256]{1,0:T(8,128)(2,1)S(1)}, u32[]{:S(2)}, u32[]{:S(2)}) %collective-permute-start.1) | collective-permute-done | bytes 262176 | tf_op jit(solution)/shard_map/ppermute | solution.py:222
  70.3 5.6 %collective-permute-start.2 = (bf16[512,256]{1,0:T(8,128)(2,1)S(1)}, bf16[512,256]{1,0:T(8,128)(2,1)S(1)}, u32[]{:S(2)}, u32[]{:S(2)}) collective-permute-start(bf16[512,256]{1,0:T(8,128)(2,1)S(1)} %collective-permute-done.1.refs_3_), channel_id=1, source_target_pairs={{0,112},{16,0},{32,16},{48,32},{64,48},{80,64},{96,80},{112,96},{1... | collective-permute-start | bytes 786440 | tf_op jit(solution)/shard_map/ppermute | solution.py:222
  77.9 8.9 %collective-permute-done.2.refs_4_ = bf16[512,256]{1,0:T(8,128)(2,1)S(1)} collective-permute-done((bf16[512,256]{1,0:T(8,128)(2,1)S(1)}, bf16[512,256]{1,0:T(8,128)(2,1)S(1)}, u32[]{:S(2)}, u32[]{:S(2)}) %collective-permute-start.2) | collective-permute-done | bytes 262176 | tf_op jit(solution)/shard_map/ppermute | solution.py:222
  86.8 5.6 %collective-permute-start.3 = (bf16[512,256]{1,0:T(8,128)(2,1)S(1)}, bf16[512,256]{1,0:T(8,128)(2,1)S(1)}, u32[]{:S(2)}, u32[]{:S(2)}) collective-permute-start(bf16[512,256]{1,0:T(8,128)(2,1)S(1)} %collective-permute-done.2.refs_4_), channel_id=1, source_target_pairs={{0,112},{16,0},{32,16},{48,32},{64,48},{80,64},{96,80},{112,96},{1... | collective-permute-start | bytes 786440 | tf_op jit(solution)/shard_map/ppermute | solution.py:222
  93.7 4.9 %shard_map.129 = (bf16[128,4096]{1,0:T(8,128)(2,1)}, bf16[128,4096]{1,0:T(8,128)(2,1)}, bf16[4096,128]{1,0:T(8,128)(2,1)}, bf16[4096,128]{1,0:T(8,128)(2,1)}, f3...) custom-call(bf16[16,384,256]{2,1,0:T(8,128)(2,1)} %all-to-all-done.got, bf16[128,256]{1,0:T(8,128)(2,1)} %stream.5, ...), custom_call_target="tpu_custom_call" | custom-call | tf_op jit(solution)/shard_map/pallas_call | solution.py:267
  99.4 7.5 %shard_map.130 = (bf16[4096,256]{1,0:T(8,128)(2,1)}, bf16[512,256]{1,0:T(8,128)(2,1)}, bf16[512,256]{1,0:T(8,128)(2,1)}, bf16[128,256]{1,0:T(8,128)(2,1)}, bf16[...) custom-call(s32[1]{0:T(128)} %bitcast.me, bf16[128,4096]{1,0:T(8,128)(2,1)} %get-tuple-element.31.normed, ...), custom_call_target="tpu_custom_call" | custom-call | flops 939524096 | tf_op jit(solution)/shard_map/pallas_call | solution.py:272
  106.8 6.1 %shard_map.131 = (bf16[1,128,4096]{2,1,0:T(8,128)(2,1)}, bf16[16,400,256]{2,1,0:T(8,128)(2,1)}) custom-call(s32[1]{0:T(128)} %bitcast.me, bf16[128,256]{1,0:T(8,128)(2,1)} %get-tuple-element.35.att, bf16[128,256]{1,0:T(8,128)(2,1)} %get-tuple-element.36.gq, bf16[16,384,256]{2,1,0:T(8,128)(2,1)} %all-to-all-done.got, bf16[1,4096]{1,0:T(2,128)(2,1)} %reshape.20.gain, ...), custom_call_target="tpu_custom_call" | custom-call | flops 536870912 | tf_op jit(solution)/shard_map/pallas_call | solution.py:284
  113.0 6.2 %all-to-all-start.1 = ((bf16[16,400,256]{2,1,0:T(8,128)(2,1)}), bf16[16,400,256]{2,1,0:T(8,128)(2,1)}, u32[]{:S(2)}, u32[]{:S(2)}) async-start(bf16[16,400,256]{2,1,0:T(8,128)(2,1)} %get-tuple-element.39), calls=%async_computation.1 | async-start | bytes 6553600 | tf_op jit(solution)/shard_map/all_to_all | solution.py:292
  119.9 3.3 %collective-permute-start.10 = (bf16[512,256]{1,0:T(8,128)(2,1)S(1)}, bf16[512,256]{1,0:T(8,128)(2,1)S(1)}, u32[]{:S(2)}, u32[]{:S(2)}) collective-permute-start(bf16[512,256]{1,0:T(8,128)(2,1)S(1)} %copy-done.16), channel_id=1, source_target_pairs={{0,112},{16,0},{32,16},{48,32},{64,48},{80,64},{96,80},{112,96},{1... | collective-permute-start | bytes 786440 | tf_op jit(solution)/shard_map/ppermute | solution.py:222
  131.2 4.5 %collective-permute-start.11 = (bf16[512,256]{1,0:T(8,128)(2,1)S(1)}, bf16[512,256]{1,0:T(8,128)(2,1)S(1)}, u32[]{:S(2)}, u32[]{:S(2)}) collective-permute-start(bf16[512,256]{1,0:T(8,128)(2,1)S(1)} %add_convert_fusion.2), channel_id=1, source_target_pairs={{0,112},{16,0},{32,16},{48,32},{64,48},{80,64},{96,80},{112,96},{1... | collective-permute-start | bytes 786440 | tf_op jit(solution)/shard_map/ppermute | solution.py:222
  135.8 5.7 %collective-permute-done.7 = bf16[512,256]{1,0:T(8,128)(2,1)S(1)} collective-permute-done((bf16[512,256]{1,0:T(8,128)(2,1)S(1)}, bf16[512,256]{1,0:T(8,128)(2,1)S(1)}, u32[]{:S(2)}, u32[]{:S(2)}) %collective-permute-start.7) | collective-permute-done | bytes 262176 | tf_op jit(solution)/shard_map/ppermute | solution.py:218
  147.6 5.6 %collective-permute-start.12 = (bf16[512,256]{1,0:T(8,128)(2,1)S(1)}, bf16[512,256]{1,0:T(8,128)(2,1)S(1)}, u32[]{:S(2)}, u32[]{:S(2)}) collective-permute-start(bf16[512,256]{1,0:T(8,128)(2,1)S(1)} %add_convert_fusion.1), channel_id=1, source_target_pairs={{0,112},{16,0},{32,16},{48,32},{64,48},{80,64},{96,80},{112,96},{1... | collective-permute-start | bytes 786440 | tf_op jit(solution)/shard_map/ppermute | solution.py:222
  153.2 5.0 %collective-permute-done.8 = bf16[512,256]{1,0:T(8,128)(2,1)S(1)} collective-permute-done((bf16[512,256]{1,0:T(8,128)(2,1)S(1)}, bf16[512,256]{1,0:T(8,128)(2,1)S(1)}, u32[]{:S(2)}, u32[]{:S(2)}) %collective-permute-start.8) | collective-permute-done | bytes 262176 | tf_op jit(solution)/shard_map/ppermute | solution.py:218
  163.3 5.6 %collective-permute-start.13 = (bf16[512,256]{1,0:T(8,128)(2,1)S(1)}, bf16[512,256]{1,0:T(8,128)(2,1)S(1)}, u32[]{:S(2)}, u32[]{:S(2)}) collective-permute-start(bf16[512,256]{1,0:T(8,128)(2,1)S(1)} %add_convert_fusion), channel_id=1, source_target_pairs={{0,112},{16,0},{32,16},{48,32},{64,48},{80,64},{96,80},{112,96},{1... | collective-permute-start | bytes 786440 | tf_op jit(solution)/shard_map/ppermute | solution.py:222
  169.0 3.8 %collective-permute-done.13.went_down = bf16[512,256]{1,0:T(8,128)(2,1)S(1)} collective-permute-done((bf16[512,256]{1,0:T(8,128)(2,1)S(1)}, bf16[512,256]{1,0:T(8,128)(2,1)S(1)}, u32[]{:S(2)}, u32[]{:S(2)}) %collective-permute-start.13) | collective-permute-done | bytes 262176 | tf_op jit(solution)/shard_map/ppermute | solution.py:222
  175.6 5.2 %all-to-all-start.2 = ((bf16[4,256,256]{2,1,0:T(8,128)(2,1)}), bf16[4,256,256]{2,1,0:T(8,128)(2,1)S(1)}, u32[]{:S(2)}, u32[]{:S(2)}) async-start(bf16[4,256,256]{2,1,0:T(8,128)(2,1)} %shard_map.134), calls=%async_computation.3 | async-start | bytes 1048576 | tf_op jit(solution)/shard_map/all_to_all | solution.py:300
  181.4 3.4 %shard_map.132 = (bf16[128,4096]{1,0:T(8,128)(2,1)}, bf16[128,256]{1,0:T(8,128)(2,1)}, bf16[128,2048]{1,0:T(8,128)(2,1)}) custom-call(bf16[16,400,256]{2,1,0:T(8,128)(2,1)} %all-to-all-done.1.got._, bf16[128,256]{1,0:T(8,128)(2,1)} %stream.5, bf16[128,256]{1,0:T(8,128)(2,1)} %cot_stream.1, bf16[1,256]{1,0:T(2,128)(2,1)} %dynamic_slice.7.gain, ...), custom_call_target="tpu_custom_call" | custom-call | tf_op jit(solution)/shard_map/pallas_call | solution.py:293
  184.8 7.3 %all-to-all-done.2.got = bf16[4,256,256]{2,1,0:T(8,128)(2,1)S(1)} async-done(((bf16[4,256,256]{2,1,0:T(8,128)(2,1)}), bf16[4,256,256]{2,1,0:T(8,128)(2,1)S(1)}, u32[]{:S(2)}, u32[]{:S(2)}) %all-to-all-start.2) | async-done | bytes 524320 | tf_op jit(solution)/shard_map/all_to_all | solution.py:300
  (70 shorter events, 36.3 us)
Async XLA Ops:
  7.2 85.9 %copy-start = (bf16[128,2048]{1,0:T(8,128)(2,1)S(1)}, bf16[128,2048]{1,0:T(8,128)(2,1)}, u32[]{:S(2)}) copy-start(bf16[128,2048]{1,0:T(8,128)(2,1)} %param.12) | copy-start | bytes 1572868
  34.5 58.0 %copy-start.14 = (bf16[4096]{0:T(1024)(128)(2,1)S(1)}, bf16[4096]{0:T(1024)(128)(2,1)}, u32[]{:S(2)}) copy-start(bf16[4096]{0:T(1024)(128)(2,1)} %param.10) | copy-start | bytes 24580
  34.5 59.2 %all-to-all-start = ((bf16[16,384,256]{2,1,0:T(8,128)(2,1)}), bf16[16,384,256]{2,1,0:T(8,128)(2,1)}, u32[]{:S(2)}, u32[]{:S(2)}) async-start(bf16[16,384,256]{2,1,0:T(8,128)(2,1)} %shard_map.128), calls=%async_computation | async-start | bytes 6291456 | tf_op jit(solution)/shard_map/all_to_all | solution.py:266
  41.7 56.9 %all-gather.3.cloned.1.call-start = ((), (), s32[]{:S(2)}) async-start(), calls=%async_computation.5 | async-start | bytes 2359296 | tf_op jit(solution)/shard_map/all_gather | solution.py:260
  42.5 56.1 %copy-start.2 = (bf16[512,256]{1,0:T(8,128)(2,1)}, bf16[512,256]{1,0:T(8,128)(2,1)S(1)}, u32[]{:S(2)}) copy-start(bf16[512,256]{1,0:T(8,128)(2,1)S(1)} %get-tuple-element.56.refs_1_) | copy-start | bytes 786436
  42.5 11.2 %collective-permute-start = (bf16[512,256]{1,0:T(8,128)(2,1)S(1)}, bf16[512,256]{1,0:T(8,128)(2,1)S(1)}, u32[]{:S(2)}, u32[]{:S(2)}) collective-permute-start(bf16[512,256]{1,0:T(8,128)(2,1)S(1)} %get-tuple-element.56.refs_1_), channel_id=1, source_target_pairs={{0,112},{16,0},{32,16},{48,32},{64,48},{80,64},{96,80},{112,96},{1... | collective-permute-start | bytes 786440 | tf_op jit(solution)/shard_map/ppermute | solution.py:222
  47.9 11.5 %collective-permute-start.4 = (bf16[512,256]{1,0:T(8,128)(2,1)S(1)}, bf16[512,256]{1,0:T(8,128)(2,1)S(1)}, u32[]{:S(2)}, u32[]{:S(2)}) collective-permute-start(bf16[512,256]{1,0:T(8,128)(2,1)S(1)} %get-tuple-element.56.refs_1_), channel_id=1, source_target_pairs={{0,16},{16,32},{32,48},{48,64},{64,80},{80,96},{96,112},{112,0},{1... | collective-permute-start | bytes 786440 | tf_op jit(solution)/shard_map/ppermute | solution.py:218
  53.8 44.8 %copy-start.4 = (bf16[512,256]{1,0:T(8,128)(2,1)}, bf16[512,256]{1,0:T(8,128)(2,1)S(1)}, u32[]{:S(2)}) copy-start(bf16[512,256]{1,0:T(8,128)(2,1)S(1)} %collective-permute-done.refs_2_) | copy-start | bytes 786436
  53.8 16.5 %collective-permute-start.1 = (bf16[512,256]{1,0:T(8,128)(2,1)S(1)}, bf16[512,256]{1,0:T(8,128)(2,1)S(1)}, u32[]{:S(2)}, u32[]{:S(2)}) collective-permute-start(bf16[512,256]{1,0:T(8,128)(2,1)S(1)} %collective-permute-done.refs_2_), channel_id=1, source_target_pairs={{0,112},{16,0},{32,16},{48,32},{64,48},{80,64},{96,80},{112,96},{1... | collective-permute-start | bytes 786440 | tf_op jit(solution)/shard_map/ppermute | solution.py:222
  59.4 39.2 %copy-start.5 = (bf16[512,256]{1,0:T(8,128)(2,1)}, bf16[512,256]{1,0:T(8,128)(2,1)S(1)}, u32[]{:S(2)}) copy-start(bf16[512,256]{1,0:T(8,128)(2,1)S(1)} %collective-permute-done.4.refs_8_) | copy-start | bytes 786436
  59.4 16.5 %collective-permute-start.5 = (bf16[512,256]{1,0:T(8,128)(2,1)S(1)}, bf16[512,256]{1,0:T(8,128)(2,1)S(1)}, u32[]{:S(2)}, u32[]{:S(2)}) collective-permute-start(bf16[512,256]{1,0:T(8,128)(2,1)S(1)} %collective-permute-done.4.refs_8_), channel_id=1, source_target_pairs={{0,16},{16,32},{32,48},{48,64},{64,80},{80,96},{96,112},{112,0},{1... | collective-permute-start | bytes 786440 | tf_op jit(solution)/shard_map/ppermute | solution.py:218
  70.3 16.4 %collective-permute-start.2 = (bf16[512,256]{1,0:T(8,128)(2,1)S(1)}, bf16[512,256]{1,0:T(8,128)(2,1)S(1)}, u32[]{:S(2)}, u32[]{:S(2)}) collective-permute-start(bf16[512,256]{1,0:T(8,128)(2,1)S(1)} %collective-permute-done.1.refs_3_), channel_id=1, source_target_pairs={{0,112},{16,0},{32,16},{48,32},{64,48},{80,64},{96,80},{112,96},{1... | collective-permute-start | bytes 786440 | tf_op jit(solution)/shard_map/ppermute | solution.py:222
  75.9 22.6 %collective-permute-start.6 = (bf16[512,256]{1,0:T(8,128)(2,1)S(1)}, bf16[512,256]{1,0:T(8,128)(2,1)S(1)}, u32[]{:S(2)}, u32[]{:S(2)}) collective-permute-start(bf16[512,256]{1,0:T(8,128)(2,1)S(1)} %collective-permute-done.5.refs_7_), channel_id=1, source_target_pairs={{0,16},{16,32},{32,48},{48,64},{64,80},{80,96},{96,112},{112,0},{1... | collective-permute-start | bytes 786440 | tf_op jit(solution)/shard_map/ppermute | solution.py:218
  86.8 11.8 %collective-permute-start.3 = (bf16[512,256]{1,0:T(8,128)(2,1)S(1)}, bf16[512,256]{1,0:T(8,128)(2,1)S(1)}, u32[]{:S(2)}, u32[]{:S(2)}) collective-permute-start(bf16[512,256]{1,0:T(8,128)(2,1)S(1)} %collective-permute-done.2.refs_4_), channel_id=1, source_target_pairs={{0,112},{16,0},{32,16},{48,32},{64,48},{80,64},{96,80},{112,96},{1... | collective-permute-start | bytes 786440 | tf_op jit(solution)/shard_map/ppermute | solution.py:222
  113.0 59.8 %all-to-all-start.1 = ((bf16[16,400,256]{2,1,0:T(8,128)(2,1)}), bf16[16,400,256]{2,1,0:T(8,128)(2,1)}, u32[]{:S(2)}, u32[]{:S(2)}) async-start(bf16[16,400,256]{2,1,0:T(8,128)(2,1)} %get-tuple-element.39), calls=%async_computation.1 | async-start | bytes 6553600 | tf_op jit(solution)/shard_map/all_to_all | solution.py:292
  119.2 53.6 %reduce-scatter.2.cloned.1.call-start = ((), (), s32[]{:S(2)}) async-start(), calls=%async_computation.4 | async-start | bytes 2359296 | tf_op jit(solution)/shard_map/reduce_scatter | solution.py:297
  119.9 10.3 %collective-permute-start.10 = (bf16[512,256]{1,0:T(8,128)(2,1)S(1)}, bf16[512,256]{1,0:T(8,128)(2,1)S(1)}, u32[]{:S(2)}, u32[]{:S(2)}) collective-permute-start(bf16[512,256]{1,0:T(8,128)(2,1)S(1)} %copy-done.16), channel_id=1, source_target_pairs={{0,112},{16,0},{32,16},{48,32},{64,48},{80,64},{96,80},{112,96},{1... | collective-permute-start | bytes 786440 | tf_op jit(solution)/shard_map/ppermute | solution.py:222
  125.9 15.6 %collective-permute-start.7 = (bf16[512,256]{1,0:T(8,128)(2,1)S(1)}, bf16[512,256]{1,0:T(8,128)(2,1)S(1)}, u32[]{:S(2)}, u32[]{:S(2)}) collective-permute-start(bf16[512,256]{1,0:T(8,128)(2,1)S(1)} %copy-done.15), channel_id=1, source_target_pairs={{0,16},{16,32},{32,48},{48,64},{64,80},{80,96},{96,112},{112,0},{1... | collective-permute-start | bytes 786440 | tf_op jit(solution)/shard_map/ppermute | solution.py:218
  131.2 15.3 %collective-permute-start.11 = (bf16[512,256]{1,0:T(8,128)(2,1)S(1)}, bf16[512,256]{1,0:T(8,128)(2,1)S(1)}, u32[]{:S(2)}, u32[]{:S(2)}) collective-permute-start(bf16[512,256]{1,0:T(8,128)(2,1)S(1)} %add_convert_fusion.2), channel_id=1, source_target_pairs={{0,112},{16,0},{32,16},{48,32},{64,48},{80,64},{96,80},{112,96},{1... | collective-permute-start | bytes 786440 | tf_op jit(solution)/shard_map/ppermute | solution.py:222
  142.5 15.6 %collective-permute-start.8 = (bf16[512,256]{1,0:T(8,128)(2,1)S(1)}, bf16[512,256]{1,0:T(8,128)(2,1)S(1)}, u32[]{:S(2)}, u32[]{:S(2)}) collective-permute-start(bf16[512,256]{1,0:T(8,128)(2,1)S(1)} %add_convert_fusion.4), channel_id=1, source_target_pairs={{0,16},{16,32},{32,48},{48,64},{64,80},{80,96},{96,112},{112,0},{1... | collective-permute-start | bytes 786440 | tf_op jit(solution)/shard_map/ppermute | solution.py:218
  147.6 15.7 %collective-permute-start.12 = (bf16[512,256]{1,0:T(8,128)(2,1)S(1)}, bf16[512,256]{1,0:T(8,128)(2,1)S(1)}, u32[]{:S(2)}, u32[]{:S(2)}) collective-permute-start(bf16[512,256]{1,0:T(8,128)(2,1)S(1)} %add_convert_fusion.1), channel_id=1, source_target_pairs={{0,112},{16,0},{32,16},{48,32},{64,48},{80,64},{96,80},{112,96},{1... | collective-permute-start | bytes 786440 | tf_op jit(solution)/shard_map/ppermute | solution.py:222
  159.1 9.9 %collective-permute-start.9 = (bf16[512,256]{1,0:T(8,128)(2,1)S(1)}, bf16[512,256]{1,0:T(8,128)(2,1)S(1)}, u32[]{:S(2)}, u32[]{:S(2)}) collective-permute-start(bf16[512,256]{1,0:T(8,128)(2,1)S(1)} %add_convert_fusion.3), channel_id=1, source_target_pairs={{0,16},{16,32},{32,48},{48,64},{64,80},{80,96},{96,112},{112,0},{1... | collective-permute-start | bytes 786440 | tf_op jit(solution)/shard_map/ppermute | solution.py:218
  163.3 9.5 %collective-permute-start.13 = (bf16[512,256]{1,0:T(8,128)(2,1)S(1)}, bf16[512,256]{1,0:T(8,128)(2,1)S(1)}, u32[]{:S(2)}, u32[]{:S(2)}) collective-permute-start(bf16[512,256]{1,0:T(8,128)(2,1)S(1)} %add_convert_fusion), channel_id=1, source_target_pairs={{0,112},{16,0},{32,16},{48,32},{64,48},{80,64},{96,80},{112,96},{1... | collective-permute-start | bytes 786440 | tf_op jit(solution)/shard_map/ppermute | solution.py:222
  175.6 16.6 %all-to-all-start.2 = ((bf16[4,256,256]{2,1,0:T(8,128)(2,1)}), bf16[4,256,256]{2,1,0:T(8,128)(2,1)S(1)}, u32[]{:S(2)}, u32[]{:S(2)}) async-start(bf16[4,256,256]{2,1,0:T(8,128)(2,1)} %shard_map.134), calls=%async_computation.3 | async-start | bytes 1048576 | tf_op jit(solution)/shard_map/all_to_all | solution.py:300
  (12 other events, 128.0 us)
Sparse Core Ops, SparseCore 0:
  45.2 49.7 all-gather.2
  122.8 45.1 reduce-scatter.1

commit v3 on v1

--- a/solution.py
+++ b/solution.py
@@ -20,16 +20,18 @@
 B = D // NF
 EXTRA = 16
 F32, BF16 = jnp.float32, jnp.bfloat16
+HBM = pl.BlockSpec(memory_space=pltpu.HBM)
 VMEM = pl.BlockSpec(memory_space=pltpu.VMEM)
-
-
-def call(body, outs, flops=0, nbytes=0):
+STEP = 512
+
+
+def call(body, outs, mib, flops=0, nbytes=0, **specs):
     return pl.pallas_call(
         body,
         out_shape=outs,
-        out_specs=jax.tree.map(lambda _: VMEM, outs),
-        compiler_params=pltpu.CompilerParams(vmem_limit_bytes=56 * 2**20),
+        compiler_params=pltpu.CompilerParams(vmem_limit_bytes=mib * 2**20),
         cost_estimate=pl.CostEstimate(flops=flops, bytes_accessed=nbytes, transcendentals=0),
+        **specs,
     )
 
 
@@ -87,19 +89,22 @@
         cot_t[at : at + B] = flip(piece).astype(BF16)
 
 
-def attend(normed, cot, normed_t, cot_t, weights, kv, terms, att_out, gq_out, kv_out):
+def attend(
+    normed, cot, normed_t, cot_t, weights, kv, terms, att_out, gq_out, kv_out, w_held, t_held, w_sem, t_sem
+):
     scale = 1.0 / math.sqrt(HS)
-    step = 512
-
-    def gather(i, carry):
-        q, g = carry
-        k = pl.ds(pl.multiple_of(i * step, step), step)
-        q += nn(normed[:, k], weights[k, :W])
-        g += nn(cot[:, k], weights[k, W:])
-        return q, g
-
-    zero = jnp.zeros((S, W), F32)
-    queries, grads = lax.fori_loop(0, D // step, gather, (zero, zero))
+    chunks = [slice(i * STEP, (i + 1) * STEP) for i in range(D // STEP)]
+    arrived = [
+        pltpu.make_async_copy(weights.at[k], w_held.at[k], w_sem.at[i]) for i, k in enumerate(chunks)
+    ]
+    for copy in arrived:
+        copy.start()
+    queries = jnp.zeros((S, W), F32)
+    grads = jnp.zeros((S, W), F32)
+    for copy, k in zip(arrived, chunks):
+        copy.wait()
+        queries += nn(normed[:, k], w_held[k, :W])
+        grads += nn(cot[:, k], w_held[k, W:])
     queries, grads = queries.astype(BF16), grads.astype(BF16)
     keys, values = kv[:, :HS], kv[:, HS:]
     causal = lax.broadcasted_iota(jnp.int32, (S, S), 0) >= lax.broadcasted_iota(jnp.int32, (S, S), 1)
@@ -122,14 +127,14 @@
     kv_out[:, :HS] = grad_keys.astype(BF16)
     kv_out[:, HS:] = grad_values.astype(BF16)
     att, gq = att_out[...], gq_out[...]
-
-    def scatter(i, _):
-        k = pl.ds(pl.multiple_of(i * step, step), step)
-        terms[k, :W] = nn(normed_t[k], gq).astype(BF16)
-        terms[k, W:] = nn(cot_t[k], att).astype(BF16)
-        return 0
-
-    lax.fori_loop(0, D // step, scatter, 0)
+    leaving = []
+    for i, k in enumerate(chunks):
+        t_held[k, :W] = nn(normed_t[k], gq).astype(BF16)
+        t_held[k, W:] = nn(cot_t[k], att).astype(BF16)
+        leaving.append(pltpu.make_async_copy(t_held.at[k], terms.at[k], t_sem.at[i]))
+        leaving[-1].start()
+    for copy in leaving:
+        copy.wait()
 
 
 def project(att, gq, weights, got, gain, kv_part, out_slice, partial, send):
@@ -197,31 +202,49 @@
     gain_own = lax.dynamic_slice_in_dim(gain, rank * W, W, 1)
     kv_own = lax.dynamic_slice_in_dim(keys_values, rank * W // HS // GROUP * 2 * HS, 2 * HS, 1)
 
-    weights = call(pack_weights, arr(B, 2 * W))(query_weight, out_weight)
+    weights = call(pack_weights, arr(B, 2 * W), 4)(query_weight, out_weight)
     weights = lax.all_gather(weights, "zh", axis=0, tiled=True)
     weights = lax.all_gather(weights, "y", axis=0, tiled=True)
 
-    send = call(pack_forward, arr(NT, 3 * S, W))(stream_in, cot_attn, newer_partial)
+    send = call(pack_forward, arr(NT, 3 * S, W), 10)(stream_in, cot_attn, newer_partial)
     got = lax.all_to_all(send, TENSOR, 0, 0, tiled=True)
     normed, cot, normed_t, cot_t, inv, out_slice = call(
-        prepare, [arr(S, D), arr(S, D), arr(D, S), arr(D, S), arr(S, 128, of=F32), arr(S, W)]
+        prepare, [arr(S, D), arr(S, D), arr(D, S), arr(D, S), arr(S, 128, of=F32), arr(S, W)], 14
     )(got, stream_in, gain)
 
     terms, att, gq, kv_part = call(
-        attend, [arr(D, 2 * W), arr(S, W), arr(S, W), arr(S, 2 * HS)], flops=8 * S * D * W
+        attend,
+        [arr(D, 2 * W), arr(S, W), arr(S, W), arr(S, 2 * HS)],
+        48,
+        flops=8 * S * D * W,
+        in_specs=[VMEM] * 4 + [HBM, VMEM],
+        out_specs=[HBM] + [VMEM] * 3,
+        scratch_shapes=[
+            pltpu.VMEM((D, 2 * W), BF16),
+            pltpu.VMEM((D, 2 * W), BF16),
+            pltpu.SemaphoreType.DMA((D // STEP,)),
+            pltpu.SemaphoreType.DMA((D // STEP,)),
+        ],
     )(normed, cot, normed_t, cot_t, weights, kv_own)
 
     terms = lax.psum_scatter(terms, "y", scatter_dimension=0, tiled=True)
     terms = lax.all_to_all(terms.reshape(ZH, B, 2 * W), "zh", 0, 0, tiled=True)
-    wq_grad, wo_grad = call(add_up, [arr(B, W), arr(W, B)])(terms)
-
+    wq_grad, wo_grad = call(add_up, [arr(B, W), arr(W, B)], 4)(terms)
+
+    streams = pl.BlockSpec((NT, S, W), lambda i: (0, 0, 0))
     attn_partial, send = call(
-        project, [arr(1, S, D), arr(NT, 3 * S + EXTRA, W)], flops=4 * S * D * W
-    )(att, gq, weights, got[:, :S], gain, kv_part, out_slice)
+        project,
+        [arr(1, S, D), arr(NT, 3 * S + EXTRA, W)],
+        22,
+        flops=4 * S * D * W,
+        grid=(1,),
+        in_specs=[VMEM] * 3 + [streams] + [VMEM] * 3,
+        out_specs=[VMEM, VMEM],
+    )(att, gq, weights, got, gain, kv_part, out_slice)
     got = lax.all_to_all(send, TENSOR, 0, 0, tiled=True)
-    stream_out, stream_grad, kv_grad = call(finish, [arr(S, D), arr(S, W), arr(*keys_values.shape)])(
-        got, stream_in, cot_stream, gain_own, inv
-    )
+    stream_out, stream_grad, kv_grad = call(
+        finish, [arr(S, D), arr(S, W), arr(*keys_values.shape)], 12
+    )(got, stream_in, cot_stream, gain_own, inv)
     return (stream_out, attn_partial, stream_grad, kv_grad, wq_grad, wo_grad)
 
 

time: 192 us -> 189 us (0.984)
  Pallas kernels: 32.2 us -> 15.3 us
  local copies, waits for them, and re-layouts: 4.98 us -> 14.9 us
  waiting for transfers between devices: 59.6 us -> 64.7 us
    pallas_call x6, Pallas kernels: 27.3 us -> 12.2 us  [the longest x1 5.91 us: per_device(): call(attend, [arr(D, 2 * W), arr(S, W), arr(S, W), arr(S, 2 * HS)], 48, f...]
    unnamed x6 -> x32, local copies, waits for them, and re-layouts: 0.8 us -> 14.8 us
    reduce_scatter x1, waiting for transfers between devices: 4.2 us -> 7.52 us  [per_device(): terms = lax.psum_scatter(terms, 'y', scatter_dimension=0, tiled=True)]
    slice x1 -> x0, local copies, waits for them, and re-layouts: 2.29 us -> none  [per_device(): got[:, :S]]
  transfers between devices with their start and end apart: 4 -> 4, of which waited for: 3 -> 3; matrix products, arithmetic and copies ran while one was open for 2% -> 0% of each run, Pallas kernels for 9% -> 5%
where the time goes in v3:
time: 189 us; the launch traced here: 188 us
  blocking collectives  65.7 us (35%)
  waiting for transfers between devices  64.7 us (34%)
  Pallas kernels  15.3 us (8%)
  local copies, waits for them, and re-layouts  14.9 us (8%)
  between operations  14.2 us (8%)
  starting transfers between devices  13.4 us (7%)
    all_to_all x1, waiting for transfers between devices, per_device(): got = lax.all_to_all(send, TENSOR, 0, 0, tiled=True)  45.3 us
    all_to_all x1, blocking collectives, per_device(): got = lax.all_to_all(send, TENSOR, 0, 0, tiled=True)  43.5 us
    all_gather x1, blocking collectives, per_device(): weights = lax.all_gather(weights, 'zh', axis=0, tiled=True)  22.3 us
    unnamed x32, local copies, waits for them, and re-layouts  14.8 us
    all_to_all x1, waiting for transfers between devices, per_device(): terms = lax.all_to_all(terms.reshape(ZH, B, 2 * W), 'zh', 0, 0, tiled=True)  11.9 us
    reduce_scatter x1, waiting for transfers between devices, per_device(): terms = lax.psum_scatter(terms, 'y', scatter_dimension=0, tiled=True)  7.52 us
    all_to_all x1, starting transfers between devices, per_device(): terms = lax.all_to_all(terms.reshape(ZH, B, 2 * W), 'zh', 0, 0, tiled=True)  7.37 us
    all_to_all x1, starting transfers between devices, per_device(): got = lax.all_to_all(send, TENSOR, 0, 0, tiled=True)  5.97 us
  transfers between devices with their start and end apart: 4, of which 3 were waited for; matrix products, arithmetic and copies ran while one was open for 0% of the time, Pallas kernels for 5%

profile of v3, /device:TPU:6, one launch (start us, length us, event | category | flops | bytes accessed | tf_op | source)
XLA Modules:
  0.0 188.2 jit_solution(2365644709221345521)
XLA Ops:
  7.2 0.9 copy-done.13
  8.1 0.8 copy-done.14
  9.1 22.3 %all_gather.6 = bf16[512,512]{1,0:T(8,128)(2,1)} all-gather(bf16[128,512]{1,0:T(8,128)(2,1)S(1)} %shard_map.129), channel_id=1, replica_groups=mesh['zh'=4,'y'=8,'zl'=2,'x'=4,'c'=2] {'zh'}, dimensions={0}, use_global_device_ids=true | all-gather | bytes 655360 | tf_op jit(solution)/shard_map/all_gather | solution.py:206
  31.4 1.2 copy-done.4
  32.6 0.8 copy-done.9
  33.4 0.8 copy-done.11
  34.5 1.7 copy-done.3
  36.2 6.0 %all-to-all-start = ((bf16[16,384,256]{2,1,0:T(8,128)(2,1)}), bf16[16,384,256]{2,1,0:T(8,128)(2,1)}, u32[]{:S(2)}, u32[]{:S(2)}) async-start(bf16[16,384,256]{2,1,0:T(8,128)(2,1)} %copy-done.3), calls=%async_computation | async-start | bytes 6291456 | tf_op jit(solution)/shard_map/all_to_all | solution.py:210
  42.3 45.3 %all-to-all-done.got = bf16[16,384,256]{2,1,0:T(8,128)(2,1)} async-done(((bf16[16,384,256]{2,1,0:T(8,128)(2,1)}), bf16[16,384,256]{2,1,0:T(8,128)(2,1)}, u32[]{:S(2)}, u32[]{:S(2)}) %all-to-all-start) | async-done | bytes 3145760 | tf_op jit(solution)/shard_map/all_to_all | solution.py:210
  87.6 3.1 %shard_map.128 = (bf16[128,4096]{1,0:T(8,128)(2,1)S(1)}, bf16[128,4096]{1,0:T(8,128)(2,1)S(1)}, bf16[4096,128]{1,0:T(8,128)(2,1)S(1)}, bf16[4096,128]{1,0:T(8,12...) custom-call(bf16[16,384,256]{2,1,0:T(8,128)(2,1)} %all-to-all-done.got, ...), custom_call_target="tpu_custom_call" | custom-call | tf_op jit(solution)/shard_map/pallas_call | solution.py:211
  90.7 1.0 copy-done.5
  91.7 1.0 copy-done.7
  92.6 1.2 copy-done.6
  93.9 1.2 copy-done.8
  95.1 5.9 %shard_map.130 = (bf16[4096,512]{1,0:T(8,128)(2,1)}, bf16[128,256]{1,0:T(8,128)(2,1)S(1)}, bf16[128,256]{1,0:T(8,128)(2,1)S(1)}, bf16[128,256]{1,0:T(8,128)(2,1)S(1)}) custom-call(bf16[128,4096]{1,0:T(8,128)(2,1)S(1)} %get-tuple-element.23.normed, bf16[128,4096]{1,0:T(8,128)(2,1)S(1)} %get-tuple-element.24.cot, bf16[4096,128]{1,0:T(8,128)(2,1)S(1)} %copy-done.6, ...), custom_call_target="tpu_custom_call" | custom-call | flops 1073741824 | tf_op jit(solution)/shard_map/pallas_call | solution.py:215
  101.0 2.2 %copy-done.1 = bf16[4096,512]{1,0:T(8,128)(2,1)S(1)} copy-done((bf16[4096,512]{1,0:T(8,128)(2,1)S(1)}, bf16[4096,512]{1,0:T(8,128)(2,1)}, u32[]{:S(2)}) %copy-start.1) | copy-done | bytes 4194328
  103.2 3.8 %shard_map.131 = (bf16[1,128,4096]{2,1,0:T(8,128)(2,1)}, bf16[16,400,256]{2,1,0:T(8,128)(2,1)S(1)}) custom-call(bf16[128,256]{1,0:T(8,128)(2,1)S(1)} %get-tuple-element.27.att, bf16[128,256]{1,0:T(8,128)(2,1)S(1)} %get-tuple-element.28.gq, bf16[4096,512]{1,0:T(8,128)(2,1)S(1)} %copy-done.1, bf16[16,384,256]{2,1,0:T(8,128)(2,1)} %all-to-all-done.got, ...), custom_call_target="tpu_custom_call" | custom-call | flops 536870912 | tf_op jit(solution)/shard_map/pallas_call | solution.py:235
  107.0 43.5 %all_to_all.15.got = bf16[16,400,256]{2,1,0:T(8,128)(2,1)} all-to-all(bf16[16,400,256]{2,1,0:T(8,128)(2,1)S(1)} %get-tuple-element.31), channel_id=1, replica_groups=mesh['zh'=4,'y'=8,'zl'=2,'x'=4,'c'=2] {'zl','x','c'}, dimensions={0} | all-to-all | bytes 6553600 | tf_op jit(solution)/shard_map/all_to_all | solution.py:244
  150.5 7.5 %reduce-scatter.2.cloned.1.call-done = bf16[512,512]{1,0:T(8,128)(2,1)} async-done(((bf16[4096,512]{1,0:T(8,128)(2,1)}), bf16[512,512]{1,0:T(8,128)(2,1)}) %reduce-scatter.2.cloned.1.call-update) | async-done | bytes 524304 | tf_op jit(solution)/shard_map/reduce_scatter | solution.py:230
  158.0 7.4 %all-to-all-start.2 = ((bf16[4,128,512]{2,1,0:T(8,128)(2,1)}), bf16[4,128,512]{2,1,0:T(8,128)(2,1)S(1)}, u32[]{:S(2)}, u32[]{:S(2)}) async-start(bf16[4,128,512]{2,1,0:T(8,128)(2,1)} %bitcast.1), calls=%async_computation.3 | async-start | bytes 1048576 | tf_op jit(solution)/shard_map/all_to_all | solution.py:231
  165.4 1.9 %copy-done.2 = bf16[16,400,256]{2,1,0:T(8,128)(2,1)S(1)} copy-done((bf16[16,400,256]{2,1,0:T(8,128)(2,1)S(1)}, bf16[16,400,256]{2,1,0:T(8,128)(2,1)}, u32[]{:S(2)}) %copy-start.2) | copy-done | bytes 3276824
  167.4 1.4 shard_map.132
  168.8 11.9 %all-to-all-done.2.got = bf16[4,128,512]{2,1,0:T(8,128)(2,1)S(1)} async-done(((bf16[4,128,512]{2,1,0:T(8,128)(2,1)}), bf16[4,128,512]{2,1,0:T(8,128)(2,1)S(1)}, u32[]{:S(2)}, u32[]{:S(2)}) %all-to-all-start.2) | async-done | bytes 524320 | tf_op jit(solution)/shard_map/all_to_all | solution.py:231
  180.7 0.7 shard_map.133
  (31 shorter events, 0.6 us)
Async XLA Ops:
  7.2 35.1 %copy-start = (bf16[128,2048]{1,0:T(8,128)(2,1)S(1)}, bf16[128,2048]{1,0:T(8,128)(2,1)}, u32[]{:S(2)}) copy-start(bf16[128,2048]{1,0:T(8,128)(2,1)} %param.12) | copy-start | bytes 1572868
  7.2 85.4 %all-gather.2.cloned.1.call-start = ((), (), s32[]{:S(2)}) async-start(), calls=%async_computation.4 | async-start | bytes 4718592 | tf_op jit(solution)/shard_map/all_gather | solution.py:207
  7.2 0.9 copy-start.13
  8.1 0.8 copy-start.14
  31.4 1.2 copy-start.4
  32.6 0.8 copy-start.9
  33.4 0.8 copy-start.11
  34.5 1.7 copy-start.3
  36.2 6.1 %copy-start.15 = (bf16[4096]{0:T(1024)(128)(2,1)S(1)}, bf16[4096]{0:T(1024)(128)(2,1)}, u32[]{:S(2)}) copy-start(bf16[4096]{0:T(1024)(128)(2,1)} %param.10) | copy-start | bytes 24580
  36.2 51.4 %copy-start.10 = (bf16[128,256]{1,0:T(8,128)(2,1)S(1)}, bf16[128,256]{1,0:T(8,128)(2,1)}, u32[]{:S(2)}) copy-start(bf16[128,256]{1,0:T(8,128)(2,1)} %stream.5) | copy-start | bytes 196612
  36.2 51.4 %all-to-all-start = ((bf16[16,384,256]{2,1,0:T(8,128)(2,1)}), bf16[16,384,256]{2,1,0:T(8,128)(2,1)}, u32[]{:S(2)}, u32[]{:S(2)}) async-start(bf16[16,384,256]{2,1,0:T(8,128)(2,1)} %copy-done.3), calls=%async_computation | async-start | bytes 6291456 | tf_op jit(solution)/shard_map/all_to_all | solution.py:210
  42.1 115.8 %reduce-scatter.2.cloned.1.call-start = ((), (), s32[]{:S(2)}) async-start(), calls=%async_computation.5 | async-start | bytes 4718592 | tf_op jit(solution)/shard_map/reduce_scatter | solution.py:230
  90.7 1.0 copy-start.5
  91.7 1.0 copy-start.7
  92.6 1.2 copy-start.6
  93.9 1.2 copy-start.8
  101.0 2.2 %copy-start.1 = (bf16[4096,512]{1,0:T(8,128)(2,1)S(1)}, bf16[4096,512]{1,0:T(8,128)(2,1)}, u32[]{:S(2)}) copy-start(bf16[4096,512]{1,0:T(8,128)(2,1)} %all-gather.2.cloned.1.call-done.weights) | copy-start | bytes 12582916
  107.0 58.4 %copy-start.12 = (bf16[128,256]{1,0:T(8,128)(2,1)S(1)}, bf16[128,256]{1,0:T(8,128)(2,1)}, u32[]{:S(2)}) copy-start(bf16[128,256]{1,0:T(8,128)(2,1)} %cot_stream.1) | copy-start | bytes 196612
  158.0 22.7 %all-to-all-start.2 = ((bf16[4,128,512]{2,1,0:T(8,128)(2,1)}), bf16[4,128,512]{2,1,0:T(8,128)(2,1)S(1)}, u32[]{:S(2)}, u32[]{:S(2)}) async-start(bf16[4,128,512]{2,1,0:T(8,128)(2,1)} %bitcast.1), calls=%async_computation.3 | async-start | bytes 1048576 | tf_op jit(solution)/shard_map/all_to_all | solution.py:231
  165.4 1.9 %copy-start.2 = (bf16[16,400,256]{2,1,0:T(8,128)(2,1)S(1)}, bf16[16,400,256]{2,1,0:T(8,128)(2,1)}, u32[]{:S(2)}) copy-start(bf16[16,400,256]{2,1,0:T(8,128)(2,1)} %all_to_all.15.got) | copy-start | bytes 9830404
Sparse Core Ops, SparseCore 0:
  31.5 57.1 all-gather.1
  101.2 56.7 reduce-scatter.1

commit v4 on v3

--- a/solution.py
+++ b/solution.py
@@ -55,9 +55,13 @@
     return a.astype(F32).T
 
 
-def pack_weights(wq, wo, out):
-    out[:, :W] = wq[...]
-    out[:, W:] = flip(wo[...]).astype(BF16)
+def pack_weights(wq, wo, out, wo_held, sem):
+    copies = [pltpu.make_async_copy(wo, wo_held, sem.at[0]), pltpu.make_async_copy(wq, out.at[:, :W], sem.at[1])]
+    for copy in copies:
+        copy.start()
+    copies[0].wait()
+    out[:, W:] = flip(wo_held[...]).astype(BF16)
+    copies[1].wait()
 
 
 def pack_forward(stream, cot, partial, out):
@@ -90,26 +94,33 @@
 
 
 def attend(
-    normed, cot, normed_t, cot_t, weights, kv, terms, att_out, gq_out, kv_out, w_held, t_held, w_sem, t_sem
+    normed_in, cot_in, normed_t_in, cot_t_in, weights, kv,
+    terms, kept,
+    normed, cot, normed_t, cot_t, w_held, t_held, sem, w_sem, t_sem,
 ):
     scale = 1.0 / math.sqrt(HS)
     chunks = [slice(i * STEP, (i + 1) * STEP) for i in range(D // STEP)]
+    pairs = ((normed_in, normed), (cot_in, cot), (normed_t_in, normed_t), (cot_t_in, cot_t))
+    brought = [pltpu.make_async_copy(a, b, sem.at[i]) for i, (a, b) in enumerate(pairs)]
     arrived = [
         pltpu.make_async_copy(weights.at[k], w_held.at[k], w_sem.at[i]) for i, k in enumerate(chunks)
     ]
-    for copy in arrived:
+    for copy in brought[:2] + arrived + brought[2:]:
         copy.start()
     queries = jnp.zeros((S, W), F32)
     grads = jnp.zeros((S, W), F32)
+    for copy in brought[:2]:
+        copy.wait()
     for copy, k in zip(arrived, chunks):
         copy.wait()
         queries += nn(normed[:, k], w_held[k, :W])
         grads += nn(cot[:, k], w_held[k, W:])
     queries, grads = queries.astype(BF16), grads.astype(BF16)
+    att_out, gq_out, low_out, gs_out = (kept.at[i] for i in range(4))
+    kept[4] = queries
+    kept[5] = grads
     keys, values = kv[:, :HS], kv[:, HS:]
     causal = lax.broadcasted_iota(jnp.int32, (S, S), 0) >= lax.broadcasted_iota(jnp.int32, (S, S), 1)
-    grad_keys = jnp.zeros((S, HS), F32)
-    grad_values = jnp.zeros((S, HS), F32)
     for h in range(W // HS):
         at = slice(h * HS, (h + 1) * HS)
         q, g = queries[:, at], grads[:, at]
@@ -122,11 +133,11 @@
         gs = (probs * (nt(g, values) - delta) * scale).astype(BF16)
         gq_out[:, at] = nn(gs, keys).astype(BF16)
         att_out[:, at] = att
-        grad_keys += nn(flip(gs).astype(BF16), q)
-        grad_values += nn(flip(low).astype(BF16), g)
-    kv_out[:, :HS] = grad_keys.astype(BF16)
-    kv_out[:, HS:] = grad_values.astype(BF16)
+        low_out[:, at] = low
+        gs_out[:, at] = gs
     att, gq = att_out[...], gq_out[...]
+    for copy in brought[2:]:
+        copy.wait()
     leaving = []
     for i, k in enumerate(chunks):
         t_held[k, :W] = nn(normed_t[k], gq).astype(BF16)
@@ -137,7 +148,15 @@
         copy.wait()
 
 
-def project(att, gq, weights, got, gain, kv_part, out_slice, partial, send):
+def project(kept, weights, got, gain, out_slice, partial, send):
+    att, gq, low, gs, q, g = (kept.at[i] for i in range(6))
+    grad_keys = jnp.zeros((S, HS), F32)
+    grad_values = jnp.zeros((S, HS), F32)
+    for h in range(W // HS):
+        at = slice(h * HS, (h + 1) * HS)
+        grad_keys += nn(flip(gs[:, at]).astype(BF16), q[:, at])
+        grad_values += nn(flip(low[:, at]).astype(BF16), g[:, at])
+    kv_part = jnp.concatenate([grad_keys, grad_values], 1).astype(BF16)
     rows = jnp.zeros((S, 1), F32)
     for y in range(Y):
         k = slice(y * ZH * B, (y + 1) * ZH * B)
@@ -155,13 +174,13 @@
     across = jnp.broadcast_to(rows, (S, S)).T[:EXTRA]
     high = across.astype(BF16).astype(F32)
     middle = (across - high).astype(BF16).astype(F32)
-    low = across - high - middle
+    rest = across - high - middle
     line = lax.broadcasted_iota(jnp.int32, (EXTRA, S), 0)
-    zero = jnp.zeros_like(low)
-    pieces = jnp.where(line == 0, high, jnp.where(line == 1, middle, jnp.where(line == 2, low, zero)))
+    zero = jnp.zeros_like(rest)
+    pieces = jnp.where(line == 0, high, jnp.where(line == 1, middle, jnp.where(line == 2, rest, zero)))
     pieces = jnp.concatenate([pieces, jnp.zeros((EXTRA, W - S), F32)], 1).astype(BF16)
     for t in range(NT):
-        send[t, S : 2 * S] = kv_part[...]
+        send[t, S : 2 * S] = kv_part
         send[t, 2 * S : 3 * S] = out_slice[...]
         send[t, 3 * S :] = pieces
 
@@ -202,26 +221,38 @@
     gain_own = lax.dynamic_slice_in_dim(gain, rank * W, W, 1)
     kv_own = lax.dynamic_slice_in_dim(keys_values, rank * W // HS // GROUP * 2 * HS, 2 * HS, 1)
 
-    weights = call(pack_weights, arr(B, 2 * W), 4)(query_weight, out_weight)
+    weights = call(
+        pack_weights,
+        arr(B, 2 * W),
+        56,
+        in_specs=[HBM] * 2,
+        out_specs=VMEM,
+        scratch_shapes=[pltpu.VMEM((W, B), BF16), pltpu.SemaphoreType.DMA((2,))],
+    )(query_weight, out_weight)
     weights = lax.all_gather(weights, "zh", axis=0, tiled=True)
     weights = lax.all_gather(weights, "y", axis=0, tiled=True)
 
     send = call(pack_forward, arr(NT, 3 * S, W), 10)(stream_in, cot_attn, newer_partial)
     got = lax.all_to_all(send, TENSOR, 0, 0, tiled=True)
     normed, cot, normed_t, cot_t, inv, out_slice = call(
-        prepare, [arr(S, D), arr(S, D), arr(D, S), arr(D, S), arr(S, 128, of=F32), arr(S, W)], 14
+        prepare, [arr(S, D), arr(S, D), arr(D, S), arr(D, S), arr(S, 128, of=F32), arr(S, W)], 56
     )(got, stream_in, gain)
 
-    terms, att, gq, kv_part = call(
+    terms, kept = call(
         attend,
-        [arr(D, 2 * W), arr(S, W), arr(S, W), arr(S, 2 * HS)],
-        48,
+        [arr(D, 2 * W), arr(6, S, W)],
+        56,
         flops=8 * S * D * W,
-        in_specs=[VMEM] * 4 + [HBM, VMEM],
-        out_specs=[HBM] + [VMEM] * 3,
+        in_specs=[HBM] * 5 + [VMEM],
+        out_specs=[HBM, VMEM],
         scratch_shapes=[
+            pltpu.VMEM((S, D), BF16),
+            pltpu.VMEM((S, D), BF16),
+            pltpu.VMEM((D, S), BF16),
+            pltpu.VMEM((D, S), BF16),
             pltpu.VMEM((D, 2 * W), BF16),
             pltpu.VMEM((D, 2 * W), BF16),
+            pltpu.SemaphoreType.DMA((4,)),
             pltpu.SemaphoreType.DMA((D // STEP,)),
             pltpu.SemaphoreType.DMA((D // STEP,)),
         ],
@@ -235,12 +266,12 @@
     attn_partial, send = call(
         project,
         [arr(1, S, D), arr(NT, 3 * S + EXTRA, W)],
-        22,
+        56,
         flops=4 * S * D * W,
         grid=(1,),
-        in_specs=[VMEM] * 3 + [streams] + [VMEM] * 3,
+        in_specs=[VMEM] * 2 + [streams] + [VMEM] * 2,
         out_specs=[VMEM, VMEM],
-    )(att, gq, weights, got, gain, kv_part, out_slice)
+    )(kept, weights, got, gain, out_slice)
     got = lax.all_to_all(send, TENSOR, 0, 0, tiled=True)
     stream_out, stream_grad, kv_grad = call(
         finish, [arr(S, D), arr(S, W), arr(*keys_values.shape)], 12

time: 189 us -> 190 us (level)
  Pallas kernels: 15.3 us -> 23.8 us
  local copies, waits for them, and re-layouts: 14.9 us -> 7.86 us
  waiting for transfers between devices: 64.7 us -> 62.2 us
    unnamed x32 -> x20, local copies, waits for them, and re-layouts: 14.8 us -> 6.53 us
    pallas_call x3, Pallas kernels: 9.79 us -> 16.6 us  [the longest x1 8.56 us: per_device(): call(attend, [arr(D, 2 * W), arr(6, S, W)], 56, flops=8 * S * D * W, in_s...]
  transfers between devices with their start and end apart: 4 -> 4, of which waited for: 3 -> 3; matrix products, arithmetic and copies ran while one was open for 0% -> 1% of each run, Pallas kernels for 5% -> 7%
where the time goes in v4:
time: 190 us; the launch traced here: 189 us
  blocking collectives  66.1 us (35%)
  waiting for transfers between devices  62.2 us (33%)
  Pallas kernels  23.8 us (13%)
  starting transfers between devices  14.7 us (8%)
  between operations  14.2 us (7%)
  local copies, waits for them, and re-layouts  7.86 us (4%)
    all_to_all x1, waiting for transfers between devices, per_device(): got = lax.all_to_all(send, TENSOR, 0, 0, tiled=True)  44.1 us
    all_to_all x1, blocking collectives, per_device(): got = lax.all_to_all(send, TENSOR, 0, 0, tiled=True)  43.7 us
    all_gather x1, blocking collectives, per_device(): weights = lax.all_gather(weights, 'zh', axis=0, tiled=True)  22.4 us
    all_to_all x1, waiting for transfers between devices, per_device(): terms = lax.all_to_all(terms.reshape(ZH, B, 2 * W), 'zh', 0, 0, tiled=True)  11.9 us
    pallas_call x1, Pallas kernels, per_device(): call(attend, [arr(D, 2 * W), arr(6, S, W)], 56, flops=8 * S * D * W, in_s...  8.56 us
    all_to_all x1, starting transfers between devices, per_device(): terms = lax.all_to_all(terms.reshape(ZH, B, 2 * W), 'zh', 0, 0, tiled=True)  7.38 us
    all_to_all x1, starting transfers between devices, per_device(): got = lax.all_to_all(send, TENSOR, 0, 0, tiled=True)  7.28 us
    unnamed x20, local copies, waits for them, and re-layouts  6.53 us
  transfers between devices with their start and end apart: 4, of which 3 were waited for; matrix products, arithmetic and copies ran while one was open for 1% of the time, Pallas kernels for 7%

profile of v4, /device:TPU:6, one launch (start us, length us, event | category | flops | bytes accessed | tf_op | source)
XLA Modules:
  0.0 188.9 jit_solution(3397964882930160092)
XLA Ops:
  7.2 0.0 all-gather.2.cloned.1.call-start
  7.2 1.7 shard_map.129
  8.9 22.4 %all_gather.6 = bf16[512,512]{1,0:T(8,128)(2,1)} all-gather(bf16[128,512]{1,0:T(8,128)(2,1)} %shard_map.129), channel_id=1, replica_groups=mesh['zh'=4,'y'=8,'zl'=2,'x'=4,'c'=2] {'zh'}, dimensions={0}, use_global_device_ids=true | all-gather | bytes 655360 | tf_op jit(solution)/shard_map/all_gather | solution.py:232
  31.4 1.2 copy-done.3
  32.6 0.8 copy-done.4
  33.4 0.8 copy-done.6
  34.3 0.2 shard_map.127
  34.5 1.7 copy-done.2
  36.2 7.3 %all-to-all-start = ((bf16[16,384,256]{2,1,0:T(8,128)(2,1)}), bf16[16,384,256]{2,1,0:T(8,128)(2,1)}, u32[]{:S(2)}, u32[]{:S(2)}) async-start(bf16[16,384,256]{2,1,0:T(8,128)(2,1)} %copy-done.2), calls=%async_computation | async-start | bytes 6291456 | tf_op jit(solution)/shard_map/all_to_all | solution.py:236
  43.5 0.0 reduce-scatter.2.cloned.1.call-start
  43.5 0.6 reshape.19.gain
  44.2 0.6 constant_dynamic-slice_fusion.kv
  44.8 44.1 %all-to-all-done.got = bf16[16,384,256]{2,1,0:T(8,128)(2,1)} async-done(((bf16[16,384,256]{2,1,0:T(8,128)(2,1)}), bf16[16,384,256]{2,1,0:T(8,128)(2,1)}, u32[]{:S(2)}, u32[]{:S(2)}) %all-to-all-start) | async-done | bytes 3145760 | tf_op jit(solution)/shard_map/all_to_all | solution.py:236
  88.9 4.9 %shard_map.128 = (bf16[128,4096]{1,0:T(8,128)(2,1)}, bf16[128,4096]{1,0:T(8,128)(2,1)}, bf16[4096,128]{1,0:T(8,128)(2,1)}, bf16[4096,128]{1,0:T(8,128)(2,1)}, f3...) custom-call(bf16[16,384,256]{2,1,0:T(8,128)(2,1)} %all-to-all-done.got, bf16[128,256]{1,0:T(8,128)(2,1)} %stream.5, ...), custom_call_target="tpu_custom_call" | custom-call | tf_op jit(solution)/shard_map/pallas_call | solution.py:237
  93.8 8.6 %shard_map.130 = (bf16[4096,512]{1,0:T(8,128)(2,1)}, bf16[6,128,256]{2,1,0:T(8,128)(2,1)}) custom-call(bf16[128,4096]{1,0:T(8,128)(2,1)} %get-tuple-element.21.normed_in, bf16[128,4096]{1,0:T(8,128)(2,1)} %get-tuple-element.22.cot_in, bf16[4096,128]{1,0:T(8,128)(2,1)} %get-tuple-element.23.normed_t_in, bf16[4096,128]{1,0:T(8,128)(2,1)} %get-tuple-element.24.cot_t_in, ...), custom_call_target="tpu_custom_call" | custom-call | flops 1073741824 | tf_op jit(solution)/shard_map/pallas_call | solution.py:241
  102.4 6.3 %shard_map.131 = (bf16[1,128,4096]{2,1,0:T(8,128)(2,1)}, bf16[16,400,256]{2,1,0:T(8,128)(2,1)}) custom-call(bf16[6,128,256]{2,1,0:T(8,128)(2,1)} %get-tuple-element.25.kept, bf16[4096,512]{1,0:T(8,128)(2,1)} %all-gather.2.cloned.1.call-done.weights, bf16[16,384,256]{2,1,0:T(8,128)(2,1)} %all-to-all-done.got, bf16[1,4096]{1,0:T(2,128)(2,1)} %reshape.19.gain, ...), custom_call_target="tpu_custom_call" | custom-call | flops 536870912 | tf_op jit(solution)/shard_map/pallas_call | solution.py:266
  108.7 43.7 %all_to_all.15.got = bf16[16,400,256]{2,1,0:T(8,128)(2,1)} all-to-all(bf16[16,400,256]{2,1,0:T(8,128)(2,1)} %get-tuple-element.27), channel_id=1, replica_groups=mesh['zh'=4,'y'=8,'zl'=2,'x'=4,'c'=2] {'zl','x','c'}, dimensions={0} | all-to-all | bytes 6553600 | tf_op jit(solution)/shard_map/all_to_all | solution.py:275
  152.4 6.2 %reduce-scatter.2.cloned.1.call-done = bf16[512,512]{1,0:T(8,128)(2,1)} async-done(((bf16[4096,512]{1,0:T(8,128)(2,1)}), bf16[512,512]{1,0:T(8,128)(2,1)}) %reduce-scatter.2.cloned.1.call-update) | async-done | bytes 524304 | tf_op jit(solution)/shard_map/reduce_scatter | solution.py:261
  158.6 7.4 %all-to-all-start.2 = ((bf16[4,128,512]{2,1,0:T(8,128)(2,1)}), bf16[4,128,512]{2,1,0:T(8,128)(2,1)S(1)}, u32[]{:S(2)}, u32[]{:S(2)}) async-start(bf16[4,128,512]{2,1,0:T(8,128)(2,1)} %bitcast.1), calls=%async_computation.3 | async-start | bytes 1048576 | tf_op jit(solution)/shard_map/all_to_all | solution.py:262
  166.0 0.1 dynamic-slice.3
  166.1 1.9 %copy-done.1 = bf16[16,400,256]{2,1,0:T(8,128)(2,1)S(1)} copy-done((bf16[16,400,256]{2,1,0:T(8,128)(2,1)S(1)}, bf16[16,400,256]{2,1,0:T(8,128)(2,1)}, u32[]{:S(2)}) %copy-start.1) | copy-done | bytes 3276824
  168.0 1.4 shard_map.132
  169.5 11.9 %all-to-all-done.2.got = bf16[4,128,512]{2,1,0:T(8,128)(2,1)S(1)} async-done(((bf16[4,128,512]{2,1,0:T(8,128)(2,1)}), bf16[4,128,512]{2,1,0:T(8,128)(2,1)S(1)}, u32[]{:S(2)}, u32[]{:S(2)}) %all-to-all-start.2) | async-done | bytes 524320 | tf_op jit(solution)/shard_map/all_to_all | solution.py:262
  181.3 0.7 shard_map.133
  (19 shorter events, 0.1 us)
Async XLA Ops:
  7.2 37.0 %copy-start = (bf16[128,2048]{1,0:T(8,128)(2,1)S(1)}, bf16[128,2048]{1,0:T(8,128)(2,1)}, u32[]{:S(2)}) copy-start(bf16[128,2048]{1,0:T(8,128)(2,1)} %param.12) | copy-start | bytes 1572868
  7.2 86.6 %all-gather.2.cloned.1.call-start = ((), (), s32[]{:S(2)}) async-start(), calls=%async_computation.4 | async-start | bytes 4718592 | tf_op jit(solution)/shard_map/all_gather | solution.py:233
  31.4 1.2 copy-start.3
  32.6 0.8 copy-start.4
  33.4 0.8 copy-start.6
  34.5 1.7 copy-start.2
  36.2 7.4 %copy-start.9 = (bf16[4096]{0:T(1024)(128)(2,1)S(1)}, bf16[4096]{0:T(1024)(128)(2,1)}, u32[]{:S(2)}) copy-start(bf16[4096]{0:T(1024)(128)(2,1)} %param.10) | copy-start | bytes 24580
  36.2 52.7 %all-to-all-start = ((bf16[16,384,256]{2,1,0:T(8,128)(2,1)}), bf16[16,384,256]{2,1,0:T(8,128)(2,1)}, u32[]{:S(2)}, u32[]{:S(2)}) async-start(bf16[16,384,256]{2,1,0:T(8,128)(2,1)} %copy-done.2), calls=%async_computation | async-start | bytes 6291456 | tf_op jit(solution)/shard_map/all_to_all | solution.py:236
  43.5 115.2 %reduce-scatter.2.cloned.1.call-start = ((), (), s32[]{:S(2)}) async-start(), calls=%async_computation.5 | async-start | bytes 4718592 | tf_op jit(solution)/shard_map/reduce_scatter | solution.py:261
  108.7 57.4 %copy-start.5 = (bf16[128,256]{1,0:T(8,128)(2,1)S(1)}, bf16[128,256]{1,0:T(8,128)(2,1)}, u32[]{:S(2)}) copy-start(bf16[128,256]{1,0:T(8,128)(2,1)} %stream.5) | copy-start | bytes 196612
  108.7 57.4 %copy-start.7 = (bf16[128,256]{1,0:T(8,128)(2,1)S(1)}, bf16[128,256]{1,0:T(8,128)(2,1)}, u32[]{:S(2)}) copy-start(bf16[128,256]{1,0:T(8,128)(2,1)} %cot_stream.1) | copy-start | bytes 196612
  108.7 57.4 %copy-start.8 = (f32[128,128]{1,0:T(8,128)S(1)}, f32[128,128]{1,0:T(8,128)}, u32[]{:S(2)}) copy-start(f32[128,128]{1,0:T(8,128)} %get-tuple-element.28.inv_in) | copy-start | bytes 196612
  158.6 22.7 %all-to-all-start.2 = ((bf16[4,128,512]{2,1,0:T(8,128)(2,1)}), bf16[4,128,512]{2,1,0:T(8,128)(2,1)S(1)}, u32[]{:S(2)}, u32[]{:S(2)}) async-start(bf16[4,128,512]{2,1,0:T(8,128)(2,1)} %bitcast.1), calls=%async_computation.3 | async-start | bytes 1048576 | tf_op jit(solution)/shard_map/all_to_all | solution.py:262
  166.1 1.9 %copy-start.1 = (bf16[16,400,256]{2,1,0:T(8,128)(2,1)S(1)}, bf16[16,400,256]{2,1,0:T(8,128)(2,1)}, u32[]{:S(2)}) copy-start(bf16[16,400,256]{2,1,0:T(8,128)(2,1)} %all_to_all.15.got) | copy-start | bytes 9830404
Sparse Core Ops, SparseCore 0:
  31.5 57.3 all-gather.1
  102.5 56.0 reduce-scatter.1

commit v5 on v4

--- a/solution.py
+++ b/solution.py
@@ -20,6 +20,7 @@
 B = D // NF
 EXTRA = 16
 F32, BF16 = jnp.float32, jnp.bfloat16
+ANY = pl.BlockSpec(memory_space=pl.ANY)
 HBM = pl.BlockSpec(memory_space=pltpu.HBM)
 VMEM = pl.BlockSpec(memory_space=pltpu.VMEM)
 STEP = 512
@@ -64,23 +65,24 @@
     copies[1].wait()
 
 
-def pack_forward(stream, cot, partial, out):
+def pack_forward(stream, cot, out):
     for t in range(NT):
         out[t, :S] = stream[...]
-        out[t, S : 2 * S] = cot[...]
-        out[t, 2 * S :] = partial[0, :, t * W : (t + 1) * W]
-
-
-def prepare(got, stream, gain, normed, cot, normed_t, cot_t, inv_out, out_slice):
+        out[t, S:] = cot[...]
+
+
+def pack_partial(partial, _, out):
+    for t in range(NT):
+        out[t] = partial[0, :, t * W : (t + 1) * W]
+
+
+def prepare(got, gain, normed, cot, normed_t, cot_t, inv_out):
     squares = jnp.zeros((S, 1), F32)
-    pending = jnp.zeros((S, W), F32)
     for t in range(NT):
         block = got[t, :S].astype(F32)
         squares += jnp.sum(block * block, -1, keepdims=True)
-        pending += got[t, 2 * S :].astype(F32)
     inv = lax.rsqrt(squares * (1.0 / D) + 1e-05)
     inv_out[...] = jnp.broadcast_to(inv, (S, 128))
-    out_slice[...] = (stream[...].astype(F32) + pending).astype(BF16)
     for f in range(NF):
         t, half = f // 2, (f % 2) * B
         at = place(f) * B
@@ -93,24 +95,16 @@
         cot_t[at : at + B] = flip(piece).astype(BF16)
 
 
-def attend(
-    normed_in, cot_in, normed_t_in, cot_t_in, weights, kv,
-    terms, kept,
-    normed, cot, normed_t, cot_t, w_held, t_held, sem, w_sem, t_sem,
-):
+def attend(normed, cot, normed_t, cot_t, weights, kv, terms, kept, w_held, t_held, w_sem, t_sem):
     scale = 1.0 / math.sqrt(HS)
     chunks = [slice(i * STEP, (i + 1) * STEP) for i in range(D // STEP)]
-    pairs = ((normed_in, normed), (cot_in, cot), (normed_t_in, normed_t), (cot_t_in, cot_t))
-    brought = [pltpu.make_async_copy(a, b, sem.at[i]) for i, (a, b) in enumerate(pairs)]
     arrived = [
         pltpu.make_async_copy(weights.at[k], w_held.at[k], w_sem.at[i]) for i, k in enumerate(chunks)
     ]
-    for copy in brought[:2] + arrived + brought[2:]:
+    for copy in arrived:
         copy.start()
     queries = jnp.zeros((S, W), F32)
     grads = jnp.zeros((S, W), F32)
-    for copy in brought[:2]:
-        copy.wait()
     for copy, k in zip(arrived, chunks):
         copy.wait()
         queries += nn(normed[:, k], w_held[k, :W])
@@ -136,8 +130,6 @@
         low_out[:, at] = low
         gs_out[:, at] = gs
     att, gq = att_out[...], gq_out[...]
-    for copy in brought[2:]:
-        copy.wait()
     leaving = []
     for i, k in enumerate(chunks):
         t_held[k, :W] = nn(normed_t[k], gq).astype(BF16)
@@ -148,7 +140,11 @@
         copy.wait()
 
 
-def project(kept, weights, got, gain, out_slice, partial, send):
+def project(kept, weights, got, gain, own, pieces_in, partial, send):
+    pending = jnp.zeros((S, W), F32)
+    for t in range(NT):
+        pending += pieces_in[t].astype(F32)
+    out_slice = (own[...].astype(F32) + pending).astype(BF16)
     att, gq, low, gs, q, g = (kept.at[i] for i in range(6))
     grad_keys = jnp.zeros((S, HS), F32)
     grad_values = jnp.zeros((S, HS), F32)
@@ -181,7 +177,7 @@
     pieces = jnp.concatenate([pieces, jnp.zeros((EXTRA, W - S), F32)], 1).astype(BF16)
     for t in range(NT):
         send[t, S : 2 * S] = kv_part
-        send[t, 2 * S : 3 * S] = out_slice[...]
+        send[t, 2 * S : 3 * S] = out_slice
         send[t, 3 * S :] = pieces
 
 
@@ -232,27 +228,24 @@
     weights = lax.all_gather(weights, "zh", axis=0, tiled=True)
     weights = lax.all_gather(weights, "y", axis=0, tiled=True)
 
-    send = call(pack_forward, arr(NT, 3 * S, W), 10)(stream_in, cot_attn, newer_partial)
+    send = call(pack_forward, arr(NT, 2 * S, W), 56)(stream_in, cot_attn)
     got = lax.all_to_all(send, TENSOR, 0, 0, tiled=True)
-    normed, cot, normed_t, cot_t, inv, out_slice = call(
-        prepare, [arr(S, D), arr(S, D), arr(D, S), arr(D, S), arr(S, 128, of=F32), arr(S, W)], 56
-    )(got, stream_in, gain)
+    normed, cot, normed_t, cot_t, inv = call(
+        prepare, [arr(S, D), arr(S, D), arr(D, S), arr(D, S), arr(S, 128, of=F32)], 14
+    )(got, gain)
+    send = call(pack_partial, arr(NT, S, W), 56, in_specs=[VMEM, ANY])(newer_partial, inv)
+    partials = lax.all_to_all(send, TENSOR, 0, 0, tiled=True)
 
     terms, kept = call(
         attend,
         [arr(D, 2 * W), arr(6, S, W)],
-        56,
+        46,
         flops=8 * S * D * W,
-        in_specs=[HBM] * 5 + [VMEM],
+        in_specs=[VMEM] * 4 + [HBM, VMEM],
         out_specs=[HBM, VMEM],
         scratch_shapes=[
-            pltpu.VMEM((S, D), BF16),
-            pltpu.VMEM((S, D), BF16),
-            pltpu.VMEM((D, S), BF16),
-            pltpu.VMEM((D, S), BF16),
             pltpu.VMEM((D, 2 * W), BF16),
             pltpu.VMEM((D, 2 * W), BF16),
-            pltpu.SemaphoreType.DMA((4,)),
             pltpu.SemaphoreType.DMA((D // STEP,)),
             pltpu.SemaphoreType.DMA((D // STEP,)),
         ],
@@ -269,9 +262,9 @@
         56,
         flops=4 * S * D * W,
         grid=(1,),
-        in_specs=[VMEM] * 2 + [streams] + [VMEM] * 2,
+        in_specs=[VMEM] * 2 + [streams] + [VMEM] * 3,
         out_specs=[VMEM, VMEM],
-    )(kept, weights, got, gain, out_slice)
+    )(kept, weights, got, gain, stream_in, partials)
     got = lax.all_to_all(send, TENSOR, 0, 0, tiled=True)
     stream_out, stream_grad, kv_grad = call(
         finish, [arr(S, D), arr(S, W), arr(*keys_values.shape)], 12

time: 190 us -> 206 us (1.084)
  blocking collectives: 66.1 us -> 88 us
  waiting for transfers between devices: 62.2 us -> 54.4 us
  local copies, waits for them, and re-layouts: 7.86 us -> 12.2 us
    all_to_all x0 -> x1, blocking collectives: none -> 20.3 us  [per_device(): partials = lax.all_to_all(send, TENSOR, 0, 0, tiled=True)]
    all_to_all x1, waiting for transfers between devices: 44.1 us -> 29.2 us  [per_device(): got = lax.all_to_all(send, TENSOR, 0, 0, tiled=True)]
    all_gather x1, waiting for transfers between devices: 0.01 us -> 13 us  [per_device(): weights = lax.all_gather(weights, 'y', axis=0, tiled=True)]
    reduce_scatter x1, waiting for transfers between devices: 6.24 us -> 0.01 us  [per_device(): terms = lax.psum_scatter(terms, 'y', scatter_dimension=0, tiled=True)]
    unnamed x20 -> x36, local copies, waits for them, and re-layouts: 6.53 us -> 12.1 us
    pallas_call x1, Pallas kernels: 4.88 us -> 1.05 us  [per_device(): call(prepare, [arr(S, D), arr(S, D), arr(D, S), arr(D, S), arr(S, 128, of...]
    pallas_call x2 -> x3, Pallas kernels: 8.77 us -> 10.5 us  [the longest x1 5.91 us: per_device(): call(attend, [arr(D, 2 * W), arr(6, S, W)], 46, flops=8 * S * D * W, in_s...]
  transfers between devices with their start and end apart: 4 -> 4, of which waited for: 3 -> 3; matrix products, arithmetic and copies ran while one was open for 1% -> 0% of each run, Pallas kernels for 7% -> 7%
where the time goes in v5:
time: 206 us; the launch traced here: 205 us
  blocking collectives  88 us (43%)
  waiting for transfers between devices  54.4 us (26%)
  Pallas kernels  22.2 us (11%)
  between operations  14.2 us (7%)
  starting transfers between devices  13.5 us (7%)
  local copies, waits for them, and re-layouts  12.2 us (6%)
    all_to_all x1, blocking collectives, per_device(): got = lax.all_to_all(send, TENSOR, 0, 0, tiled=True)  45.1 us
    all_to_all x1, waiting for transfers between devices, per_device(): got = lax.all_to_all(send, TENSOR, 0, 0, tiled=True)  29.2 us
    all_gather x1, blocking collectives, per_device(): weights = lax.all_gather(weights, 'zh', axis=0, tiled=True)  22.6 us
    all_to_all x1, blocking collectives, per_device(): partials = lax.all_to_all(send, TENSOR, 0, 0, tiled=True)  20.3 us
    all_gather x1, waiting for transfers between devices, per_device(): weights = lax.all_gather(weights, 'y', axis=0, tiled=True)  13 us
    all_to_all x1, waiting for transfers between devices, per_device(): terms = lax.all_to_all(terms.reshape(ZH, B, 2 * W), 'zh', 0, 0, tiled=True)  12.1 us
    unnamed x36, local copies, waits for them, and re-layouts  12.1 us
    all_to_all x1, starting transfers between devices, per_device(): got = lax.all_to_all(send, TENSOR, 0, 0, tiled=True)  7.01 us
  transfers between devices with their start and end apart: 4, of which 3 were waited for; matrix products, arithmetic and copies ran while one was open for 0% of the time, Pallas kernels for 7%

profile of v5, /device:TPU:6, one launch (start us, length us, event | category | flops | bytes accessed | tf_op | source)
XLA Modules:
  0.0 204.6 jit_solution(2158056000276844254)
XLA Ops:
  7.2 1.7 shard_map.129
  8.9 22.6 %all_gather.6 = bf16[512,512]{1,0:T(8,128)(2,1)} all-gather(bf16[128,512]{1,0:T(8,128)(2,1)} %shard_map.129), channel_id=1, replica_groups=mesh['zh'=4,'y'=8,'zl'=2,'x'=4,'c'=2] {'zh'}, dimensions={0}, use_global_device_ids=true | all-gather | bytes 655360 | tf_op jit(solution)/shard_map/all_gather | solution.py:228
  31.5 2.4 %shard_map.127 = bf16[16,256,256]{2,1,0:T(8,128)(2,1)} custom-call(bf16[128,256]{1,0:T(8,128)(2,1)} %stream.3, bf16[128,256]{1,0:T(8,128)(2,1)} %cot.1), custom_call_target="tpu_custom_call" | custom-call | tf_op jit(solution)/shard_map/pallas_call | solution.py:231
  33.9 7.0 %all-to-all-start = ((bf16[16,256,256]{2,1,0:T(8,128)(2,1)}), bf16[16,256,256]{2,1,0:T(8,128)(2,1)S(1)}, u32[]{:S(2)}, u32[]{:S(2)}) async-start(bf16[16,256,256]{2,1,0:T(8,128)(2,1)} %shard_map.127), calls=%async_computation | async-start | bytes 4194304 | tf_op jit(solution)/shard_map/all_to_all | solution.py:232
  41.1 29.2 %all-to-all-done.got = bf16[16,256,256]{2,1,0:T(8,128)(2,1)S(1)} async-done(((bf16[16,256,256]{2,1,0:T(8,128)(2,1)}), bf16[16,256,256]{2,1,0:T(8,128)(2,1)S(1)}, u32[]{:S(2)}, u32[]{:S(2)}) %all-to-all-start) | async-done | bytes 2097184 | tf_op jit(solution)/shard_map/all_to_all | solution.py:232
  70.3 1.1 shard_map.128
  71.3 1.0 copy-done.3
  72.3 1.0 copy-done.5
  73.3 1.0 copy-done.7
  74.3 1.0 copy-done.9
  75.9 13.0 %all-gather.2.cloned.1.call-done.weights = bf16[4096,512]{1,0:T(8,128)(2,1)} async-done(((bf16[512,512]{1,0:T(8,128)(2,1)}), bf16[4096,512]{1,0:T(8,128)(2,1)}) %all-gather.2.cloned.1.call-update) | async-done | bytes 4194320 | tf_op jit(solution)/shard_map/all_gather | solution.py:229
  88.9 1.2 copy-done.4
  90.1 1.2 copy-done.6
  91.3 1.2 copy-done.8
  92.5 1.2 copy-done.10
  93.8 5.9 %shard_map.130 = (bf16[4096,512]{1,0:T(8,128)(2,1)}, bf16[6,128,256]{2,1,0:T(8,128)(2,1)S(1)}) custom-call(bf16[128,4096]{1,0:T(8,128)(2,1)S(1)} %copy-done.4, bf16[128,4096]{1,0:T(8,128)(2,1)S(1)} %copy-done.6, bf16[4096,128]{1,0:T(8,128)(2,1)S(1)} %copy-done.8, bf16[4096,128]{1,0:T(8,128)(2,1)S(1)} %copy-done.10, ...), custom_call_target="tpu_custom_call" | custom-call | flops 1073741824 | tf_op jit(solution)/shard_map/pallas_call | solution.py:239
  100.5 2.3 %shard_map.131 = bf16[16,128,256]{2,1,0:T(8,128)(2,1)} custom-call(bf16[1,128,4096]{2,1,0:T(8,128)(2,1)} %partial.1, f32[128,128]{1,0:T(8,128)} %copy-done.13), custom_call_target="tpu_custom_call" | custom-call | tf_op jit(solution)/shard_map/pallas_call | solution.py:236
  102.7 20.3 %all_to_all.20.pieces_in = bf16[16,128,256]{2,1,0:T(8,128)(2,1)} all-to-all(bf16[16,128,256]{2,1,0:T(8,128)(2,1)} %shard_map.131), channel_id=1, replica_groups=mesh['zh'=4,'y'=8,'zl'=2,'x'=4,'c'=2] {'zl','x','c'}, dimensions={0} | all-to-all | bytes 2097152 | tf_op jit(solution)/shard_map/all_to_all | solution.py:237
  123.0 6.8 %shard_map.132 = (bf16[1,128,4096]{2,1,0:T(8,128)(2,1)}, bf16[16,400,256]{2,1,0:T(8,128)(2,1)}) custom-call(bf16[6,128,256]{2,1,0:T(8,128)(2,1)} %copy-done.12, bf16[4096,512]{1,0:T(8,128)(2,1)} %all-gather.2.cloned.1.call-done.weights, bf16[16,256,256]{2,1,0:T(8,128)(2,1)} %copy-done.1, bf16[1,4096]{1,0:T(2,128)(2,1)} %copy-done.15, ...), custom_call_target="tpu_custom_call" | custom-call | flops 536870912 | tf_op jit(solution)/shard_map/pallas_call | solution.py:259
  129.8 45.1 %all_to_all.21.got = bf16[16,400,256]{2,1,0:T(8,128)(2,1)} all-to-all(bf16[16,400,256]{2,1,0:T(8,128)(2,1)} %get-tuple-element.26), channel_id=1, replica_groups=mesh['zh'=4,'y'=8,'zl'=2,'x'=4,'c'=2] {'zl','x','c'}, dimensions={0} | all-to-all | bytes 6553600 | tf_op jit(solution)/shard_map/all_to_all | solution.py:268
  174.9 6.4 %all-to-all-start.3 = ((bf16[4,128,512]{2,1,0:T(8,128)(2,1)}), bf16[4,128,512]{2,1,0:T(8,128)(2,1)S(1)}, u32[]{:S(2)}, u32[]{:S(2)}) async-start(bf16[4,128,512]{2,1,0:T(8,128)(2,1)} %bitcast.1), calls=%async_computation.4 | async-start | bytes 1048576 | tf_op jit(solution)/shard_map/all_to_all | solution.py:255
  181.5 1.9 copy-done.2
  183.4 1.4 shard_map.133
  184.9 12.1 %all-to-all-done.3.got = bf16[4,128,512]{2,1,0:T(8,128)(2,1)S(1)} async-done(((bf16[4,128,512]{2,1,0:T(8,128)(2,1)}), bf16[4,128,512]{2,1,0:T(8,128)(2,1)S(1)}, u32[]{:S(2)}, u32[]{:S(2)}) %all-to-all-start.3) | async-done | bytes 524320 | tf_op jit(solution)/shard_map/all_to_all | solution.py:255
  (37 shorter events, 2.4 us)
Async XLA Ops:
  7.2 33.9 %copy-start = (bf16[128,2048]{1,0:T(8,128)(2,1)S(1)}, bf16[128,2048]{1,0:T(8,128)(2,1)}, u32[]{:S(2)}) copy-start(bf16[128,2048]{1,0:T(8,128)(2,1)} %param.12) | copy-start | bytes 1572868
  7.2 81.7 %all-gather.2.cloned.1.call-start = ((), (), s32[]{:S(2)}) async-start(), calls=%async_computation.5 | async-start | bytes 4718592 | tf_op jit(solution)/shard_map/all_gather | solution.py:229
  31.5 9.5 %copy-start.17 = (bf16[4096]{0:T(1024)(128)(2,1)S(1)}, bf16[4096]{0:T(1024)(128)(2,1)}, u32[]{:S(2)}) copy-start(bf16[4096]{0:T(1024)(128)(2,1)} %param.10) | copy-start | bytes 24580
  33.9 36.4 %all-to-all-start = ((bf16[16,256,256]{2,1,0:T(8,128)(2,1)}), bf16[16,256,256]{2,1,0:T(8,128)(2,1)S(1)}, u32[]{:S(2)}, u32[]{:S(2)}) async-start(bf16[16,256,256]{2,1,0:T(8,128)(2,1)} %shard_map.127), calls=%async_computation | async-start | bytes 4194304 | tf_op jit(solution)/shard_map/all_to_all | solution.py:232
  40.9 134.1 %reduce-scatter.2.cloned.1.call-start = ((), (), s32[]{:S(2)}) async-start(), calls=%async_computation.6 | async-start | bytes 4718592 | tf_op jit(solution)/shard_map/reduce_scatter | solution.py:254
  41.0 58.7 %copy-start.15 = (bf16[1,4096]{1,0:T(2,128)(2,1)}, bf16[1,4096]{1,0:T(2,128)(2,1)S(1)}, u32[]{:S(2)}) copy-start(bf16[1,4096]{1,0:T(2,128)(2,1)S(1)} %reshape.19.gain) | copy-start | bytes 24580
  70.3 29.4 %copy-start.1 = (bf16[16,256,256]{2,1,0:T(8,128)(2,1)}, bf16[16,256,256]{2,1,0:T(8,128)(2,1)S(1)}, u32[]{:S(2)}) copy-start(bf16[16,256,256]{2,1,0:T(8,128)(2,1)S(1)} %all-to-all-done.got) | copy-start | bytes 6291460
  71.3 1.0 copy-start.3
  72.3 1.0 copy-start.5
  73.3 1.0 copy-start.7
  74.3 1.0 copy-start.9
  75.3 0.6 copy-start.13
  88.9 1.2 copy-start.4
  90.1 1.2 copy-start.6
  91.3 1.2 copy-start.8
  92.5 1.2 copy-start.10
  99.7 0.7 copy-start.12
  129.8 51.6 %copy-start.11 = (bf16[128,256]{1,0:T(8,128)(2,1)S(1)}, bf16[128,256]{1,0:T(8,128)(2,1)}, u32[]{:S(2)}) copy-start(bf16[128,256]{1,0:T(8,128)(2,1)} %stream.3) | copy-start | bytes 196612
  129.8 51.6 %copy-start.14 = (f32[128,128]{1,0:T(8,128)S(1)}, f32[128,128]{1,0:T(8,128)}, u32[]{:S(2)}) copy-start(f32[128,128]{1,0:T(8,128)} %copy-done.13) | copy-start | bytes 196612
  129.8 51.6 %copy-start.16 = (bf16[128,256]{1,0:T(8,128)(2,1)S(1)}, bf16[128,256]{1,0:T(8,128)(2,1)}, u32[]{:S(2)}) copy-start(bf16[128,256]{1,0:T(8,128)(2,1)} %cot_stream.1) | copy-start | bytes 196612
  174.9 22.1 %all-to-all-start.3 = ((bf16[4,128,512]{2,1,0:T(8,128)(2,1)}), bf16[4,128,512]{2,1,0:T(8,128)(2,1)S(1)}, u32[]{:S(2)}, u32[]{:S(2)}) async-start(bf16[4,128,512]{2,1,0:T(8,128)(2,1)} %bitcast.1), calls=%async_computation.4 | async-start | bytes 1048576 | tf_op jit(solution)/shard_map/all_to_all | solution.py:255
  181.5 1.9 copy-start.2
Sparse Core Ops, SparseCore 0:
  31.6 57.1 all-gather.1
  100.6 56.6 reduce-scatter.1

commit v6 on v4

--- a/solution.py
+++ b/solution.py
@@ -94,31 +94,36 @@
 
 
 def attend(
-    normed_in, cot_in, normed_t_in, cot_t_in, weights, kv,
-    terms, kept,
-    normed, cot, normed_t, cot_t, w_held, t_held, sem, w_sem, t_sem,
+    normed_in, cot_in, normed_t_in, cot_t_in, weights, kv_in, terms, kept_out,
+    normed, cot, normed_t, cot_t, w_held, t_held, kv, kept, sem, in_sem, t_sem,
 ):
     scale = 1.0 / math.sqrt(HS)
     chunks = [slice(i * STEP, (i + 1) * STEP) for i in range(D // STEP)]
-    pairs = ((normed_in, normed), (cot_in, cot), (normed_t_in, normed_t), (cot_t_in, cot_t))
+    pairs = ((kv_in, kv), (normed_t_in, normed_t), (cot_t_in, cot_t))
     brought = [pltpu.make_async_copy(a, b, sem.at[i]) for i, (a, b) in enumerate(pairs)]
     arrived = [
-        pltpu.make_async_copy(weights.at[k], w_held.at[k], w_sem.at[i]) for i, k in enumerate(chunks)
+        (
+            pltpu.make_async_copy(normed_in.at[:, k], normed.at[:, k], in_sem.at[0, i]),
+            pltpu.make_async_copy(cot_in.at[:, k], cot.at[:, k], in_sem.at[1, i]),
+            pltpu.make_async_copy(weights.at[k], w_held.at[k], in_sem.at[2, i]),
+        )
+        for i, k in enumerate(chunks)
     ]
-    for copy in brought[:2] + arrived + brought[2:]:
-        copy.start()
+    for copies in arrived + [brought]:
+        for copy in copies:
+            copy.start()
     queries = jnp.zeros((S, W), F32)
     grads = jnp.zeros((S, W), F32)
-    for copy in brought[:2]:
-        copy.wait()
-    for copy, k in zip(arrived, chunks):
-        copy.wait()
+    for copies, k in zip(arrived, chunks):
+        for copy in copies:
+            copy.wait()
         queries += nn(normed[:, k], w_held[k, :W])
         grads += nn(cot[:, k], w_held[k, W:])
     queries, grads = queries.astype(BF16), grads.astype(BF16)
     att_out, gq_out, low_out, gs_out = (kept.at[i] for i in range(4))
     kept[4] = queries
     kept[5] = grads
+    brought[0].wait()
     keys, values = kv[:, :HS], kv[:, HS:]
     causal = lax.broadcasted_iota(jnp.int32, (S, S), 0) >= lax.broadcasted_iota(jnp.int32, (S, S), 1)
     for h in range(W // HS):
@@ -136,9 +141,10 @@
         low_out[:, at] = low
         gs_out[:, at] = gs
     att, gq = att_out[...], gq_out[...]
-    for copy in brought[2:]:
+    leaving = [pltpu.make_async_copy(kept, kept_out, sem.at[3])]
+    leaving[0].start()
+    for copy in brought[1:]:
         copy.wait()
-    leaving = []
     for i, k in enumerate(chunks):
         t_held[k, :W] = nn(normed_t[k], gq).astype(BF16)
         t_held[k, W:] = nn(cot_t[k], att).astype(BF16)
@@ -232,7 +238,7 @@
     weights = lax.all_gather(weights, "zh", axis=0, tiled=True)
     weights = lax.all_gather(weights, "y", axis=0, tiled=True)
 
-    send = call(pack_forward, arr(NT, 3 * S, W), 10)(stream_in, cot_attn, newer_partial)
+    send = call(pack_forward, arr(NT, 3 * S, W), 56)(stream_in, cot_attn, newer_partial)
     got = lax.all_to_all(send, TENSOR, 0, 0, tiled=True)
     normed, cot, normed_t, cot_t, inv, out_slice = call(
         prepare, [arr(S, D), arr(S, D), arr(D, S), arr(D, S), arr(S, 128, of=F32), arr(S, W)], 56
@@ -243,8 +249,8 @@
         [arr(D, 2 * W), arr(6, S, W)],
         56,
         flops=8 * S * D * W,
-        in_specs=[HBM] * 5 + [VMEM],
-        out_specs=[HBM, VMEM],
+        in_specs=[HBM] * 6,
+        out_specs=[HBM, HBM],
         scratch_shapes=[
             pltpu.VMEM((S, D), BF16),
             pltpu.VMEM((S, D), BF16),
@@ -252,8 +258,10 @@
             pltpu.VMEM((D, S), BF16),
             pltpu.VMEM((D, 2 * W), BF16),
             pltpu.VMEM((D, 2 * W), BF16),
+            pltpu.VMEM((S, 2 * HS), BF16),
+            pltpu.VMEM((6, S, W), BF16),
             pltpu.SemaphoreType.DMA((4,)),
-            pltpu.SemaphoreType.DMA((D // STEP,)),
+            pltpu.SemaphoreType.DMA((3, D // STEP)),
             pltpu.SemaphoreType.DMA((D // STEP,)),
         ],
     )(normed, cot, normed_t, cot_t, weights, kv_own)

time: 190 us -> 186 us (0.979)
  local copies, waits for them, and re-layouts: 7.86 us -> 3.28 us
    unnamed x20 -> x12, local copies, waits for them, and re-layouts: 6.53 us -> 1.94 us
    pallas_call x1, Pallas kernels: 0.2 us -> 3.2 us  [per_device(): call(pack_forward, arr(NT, 3 * S, W), 56)]
  transfers between devices with their start and end apart: 4 -> 4, of which waited for: 3 -> 3; matrix products, arithmetic and copies ran while one was open for 1% -> 1% of each run, Pallas kernels for 7% -> 9%
where the time goes in v6:
time: 186 us
  blocking collectives  66.1 us (36%)
  waiting for transfers between devices  62.2 us (33%)
  Pallas kernels  25.5 us (14%)
  starting transfers between devices  14.7 us (8%)
  between operations  14.1 us (8%)
  local copies, waits for them, and re-layouts  3.28 us (2%)
    all_to_all x1, waiting for transfers between devices, per_device(): got = lax.all_to_all(send, TENSOR, 0, 0, tiled=True)  44.1 us
    all_to_all x1, blocking collectives, per_device(): got = lax.all_to_all(send, TENSOR, 0, 0, tiled=True)  43.7 us
    all_gather x1, blocking collectives, per_device(): weights = lax.all_gather(weights, 'zh', axis=0, tiled=True)  22.4 us
    all_to_all x1, waiting for transfers between devices, per_device(): terms = lax.all_to_all(terms.reshape(ZH, B, 2 * W), 'zh', 0, 0, tiled=True)  11.9 us
    all_to_all x1, starting transfers between devices, per_device(): terms = lax.all_to_all(terms.reshape(ZH, B, 2 * W), 'zh', 0, 0, tiled=True)  7.38 us
    all_to_all x1, starting transfers between devices, per_device(): got = lax.all_to_all(send, TENSOR, 0, 0, tiled=True)  7.27 us
    pallas_call x1, Pallas kernels, per_device(): call(attend, [arr(D, 2 * W), arr(6, S, W)], 56, flops=8 * S * D * W, in_s...  7.23 us
    pallas_call x1, Pallas kernels, per_device(): call(project, [arr(1, S, D), arr(NT, 3 * S + EXTRA, W)], 56, flops=4 * S...  6.35 us
  transfers between devices with their start and end apart: 4, of which 3 were waited for; matrix products, arithmetic and copies ran while one was open for 1% of the time, Pallas kernels for 9%

profile of v6, /device:TPU:6, one launch (start us, length us, event | category | flops | bytes accessed | tf_op | source)
XLA Modules:
  0.0 186.0 jit_solution(12092437403086190348)
XLA Ops:
  7.2 0.0 copy-start
  7.2 0.0 all-gather.2.cloned.1.call-start
  7.2 1.7 shard_map.129
  8.9 22.4 %all_gather.6 = bf16[512,512]{1,0:T(8,128)(2,1)} all-gather(bf16[128,512]{1,0:T(8,128)(2,1)} %shard_map.129), channel_id=1, replica_groups=mesh['zh'=4,'y'=8,'zl'=2,'x'=4,'c'=2] {'zh'}, dimensions={0}, use_global_device_ids=true | all-gather | bytes 655360 | tf_op jit(solution)/shard_map/all_gather | solution.py:238
  31.3 0.0 all-gather.2.cloned.1.call-update
  31.4 3.2 %shard_map.127 = bf16[16,384,256]{2,1,0:T(8,128)(2,1)} custom-call(bf16[128,256]{1,0:T(8,128)(2,1)} %stream.5, bf16[128,256]{1,0:T(8,128)(2,1)} %cot.1, bf16[1,128,4096]{2,1,0:T(8,128)(2,1)} %partial.1), custom_call_target="tpu_custom_call" | custom-call | tf_op jit(solution)/shard_map/pallas_call | solution.py:241
  34.6 7.3 %all-to-all-start = ((bf16[16,384,256]{2,1,0:T(8,128)(2,1)}), bf16[16,384,256]{2,1,0:T(8,128)(2,1)}, u32[]{:S(2)}, u32[]{:S(2)}) async-start(bf16[16,384,256]{2,1,0:T(8,128)(2,1)} %shard_map.127), calls=%async_computation | async-start | bytes 6291456 | tf_op jit(solution)/shard_map/all_to_all | solution.py:242
  41.8 0.0 reduce-scatter.2.cloned.1.call-start
  41.9 0.6 reshape.19.gain
  42.6 0.6 constant_dynamic-slice_fusion.kv_in
  43.2 44.1 %all-to-all-done.got = bf16[16,384,256]{2,1,0:T(8,128)(2,1)} async-done(((bf16[16,384,256]{2,1,0:T(8,128)(2,1)}), bf16[16,384,256]{2,1,0:T(8,128)(2,1)}, u32[]{:S(2)}, u32[]{:S(2)}) %all-to-all-start) | async-done | bytes 3145760 | tf_op jit(solution)/shard_map/all_to_all | solution.py:242
  87.3 4.9 %shard_map.128 = (bf16[128,4096]{1,0:T(8,128)(2,1)}, bf16[128,4096]{1,0:T(8,128)(2,1)}, bf16[4096,128]{1,0:T(8,128)(2,1)}, bf16[4096,128]{1,0:T(8,128)(2,1)}, f3...) custom-call(bf16[16,384,256]{2,1,0:T(8,128)(2,1)} %all-to-all-done.got, bf16[128,256]{1,0:T(8,128)(2,1)} %stream.5, ...), custom_call_target="tpu_custom_call" | custom-call | tf_op jit(solution)/shard_map/pallas_call | solution.py:243
  92.2 7.2 %shard_map.130 = (bf16[4096,512]{1,0:T(8,128)(2,1)}, bf16[6,128,256]{2,1,0:T(8,128)(2,1)}) custom-call(bf16[128,4096]{1,0:T(8,128)(2,1)} %get-tuple-element.21.normed_in, bf16[128,4096]{1,0:T(8,128)(2,1)} %get-tuple-element.22.cot_in, bf16[4096,128]{1,0:T(8,128)(2,1)} %get-tuple-element.23.normed_t_in, bf16[4096,128]{1,0:T(8,128)(2,1)} %get-tuple-element.24.cot_t_in, ...), custom_call_target="tpu_custom_call" | custom-call | flops 1073741824 | tf_op jit(solution)/shard_map/pallas_call | solution.py:247
  99.4 0.0 reduce-scatter.2.cloned.1.call-update
  99.4 6.3 %shard_map.131 = (bf16[1,128,4096]{2,1,0:T(8,128)(2,1)}, bf16[16,400,256]{2,1,0:T(8,128)(2,1)}) custom-call(bf16[6,128,256]{2,1,0:T(8,128)(2,1)} %get-tuple-element.25.kept, bf16[4096,512]{1,0:T(8,128)(2,1)} %all-gather.2.cloned.1.call-done.weights, bf16[16,384,256]{2,1,0:T(8,128)(2,1)} %all-to-all-done.got, bf16[1,4096]{1,0:T(2,128)(2,1)} %reshape.19.gain, ...), custom_call_target="tpu_custom_call" | custom-call | flops 536870912 | tf_op jit(solution)/shard_map/pallas_call | solution.py:274
  105.8 43.7 %all_to_all.15.got = bf16[16,400,256]{2,1,0:T(8,128)(2,1)} all-to-all(bf16[16,400,256]{2,1,0:T(8,128)(2,1)} %get-tuple-element.27), channel_id=1, replica_groups=mesh['zh'=4,'y'=8,'zl'=2,'x'=4,'c'=2] {'zl','x','c'}, dimensions={0} | all-to-all | bytes 6553600 | tf_op jit(solution)/shard_map/all_to_all | solution.py:283
  149.5 6.2 %reduce-scatter.2.cloned.1.call-done = bf16[512,512]{1,0:T(8,128)(2,1)} async-done(((bf16[4096,512]{1,0:T(8,128)(2,1)}), bf16[512,512]{1,0:T(8,128)(2,1)}) %reduce-scatter.2.cloned.1.call-update) | async-done | bytes 524304 | tf_op jit(solution)/shard_map/reduce_scatter | solution.py:269
  155.7 7.4 %all-to-all-start.2 = ((bf16[4,128,512]{2,1,0:T(8,128)(2,1)}), bf16[4,128,512]{2,1,0:T(8,128)(2,1)S(1)}, u32[]{:S(2)}, u32[]{:S(2)}) async-start(bf16[4,128,512]{2,1,0:T(8,128)(2,1)} %bitcast.1), calls=%async_computation.3 | async-start | bytes 1048576 | tf_op jit(solution)/shard_map/all_to_all | solution.py:270
  163.0 0.1 dynamic-slice.3
  163.1 0.0 copy-done.3
  163.2 1.9 %copy-done.1 = bf16[16,400,256]{2,1,0:T(8,128)(2,1)S(1)} copy-done((bf16[16,400,256]{2,1,0:T(8,128)(2,1)S(1)}, bf16[16,400,256]{2,1,0:T(8,128)(2,1)}, u32[]{:S(2)}) %copy-start.1) | copy-done | bytes 3276824
  165.1 1.4 shard_map.132
  166.5 11.9 %all-to-all-done.2.got = bf16[4,128,512]{2,1,0:T(8,128)(2,1)S(1)} async-done(((bf16[4,128,512]{2,1,0:T(8,128)(2,1)}), bf16[4,128,512]{2,1,0:T(8,128)(2,1)S(1)}, u32[]{:S(2)}, u32[]{:S(2)}) %all-to-all-start.2) | async-done | bytes 524320 | tf_op jit(solution)/shard_map/all_to_all | solution.py:270
  178.4 0.7 shard_map.133
  (11 shorter events, 0.0 us)
Async XLA Ops:
  7.2 35.4 %copy-start = (bf16[128,2048]{1,0:T(8,128)(2,1)S(1)}, bf16[128,2048]{1,0:T(8,128)(2,1)}, u32[]{:S(2)}) copy-start(bf16[128,2048]{1,0:T(8,128)(2,1)} %param.12) | copy-start | bytes 1572868
  7.2 85.0 %all-gather.2.cloned.1.call-start = ((), (), s32[]{:S(2)}) async-start(), calls=%async_computation.4 | async-start | bytes 4718592 | tf_op jit(solution)/shard_map/all_gather | solution.py:239
  34.6 7.4 %copy-start.5 = (bf16[4096]{0:T(1024)(128)(2,1)S(1)}, bf16[4096]{0:T(1024)(128)(2,1)}, u32[]{:S(2)}) copy-start(bf16[4096]{0:T(1024)(128)(2,1)} %param.10) | copy-start | bytes 24580
  34.6 52.7 %all-to-all-start = ((bf16[16,384,256]{2,1,0:T(8,128)(2,1)}), bf16[16,384,256]{2,1,0:T(8,128)(2,1)}, u32[]{:S(2)}, u32[]{:S(2)}) async-start(bf16[16,384,256]{2,1,0:T(8,128)(2,1)} %shard_map.127), calls=%async_computation | async-start | bytes 6291456 | tf_op jit(solution)/shard_map/all_to_all | solution.py:242
  41.8 113.8 %reduce-scatter.2.cloned.1.call-start = ((), (), s32[]{:S(2)}) async-start(), calls=%async_computation.5 | async-start | bytes 4718592 | tf_op jit(solution)/shard_map/reduce_scatter | solution.py:269
  105.8 57.4 %copy-start.2 = (bf16[128,256]{1,0:T(8,128)(2,1)S(1)}, bf16[128,256]{1,0:T(8,128)(2,1)}, u32[]{:S(2)}) copy-start(bf16[128,256]{1,0:T(8,128)(2,1)} %stream.5) | copy-start | bytes 196612
  105.8 57.4 %copy-start.3 = (bf16[128,256]{1,0:T(8,128)(2,1)S(1)}, bf16[128,256]{1,0:T(8,128)(2,1)}, u32[]{:S(2)}) copy-start(bf16[128,256]{1,0:T(8,128)(2,1)} %cot_stream.1) | copy-start | bytes 196612
  105.8 57.4 %copy-start.4 = (f32[128,128]{1,0:T(8,128)S(1)}, f32[128,128]{1,0:T(8,128)}, u32[]{:S(2)}) copy-start(f32[128,128]{1,0:T(8,128)} %get-tuple-element.28.inv_in) | copy-start | bytes 196612
  155.7 22.7 %all-to-all-start.2 = ((bf16[4,128,512]{2,1,0:T(8,128)(2,1)}), bf16[4,128,512]{2,1,0:T(8,128)(2,1)S(1)}, u32[]{:S(2)}, u32[]{:S(2)}) async-start(bf16[4,128,512]{2,1,0:T(8,128)(2,1)} %bitcast.1), calls=%async_computation.3 | async-start | bytes 1048576 | tf_op jit(solution)/shard_map/all_to_all | solution.py:270
  163.1 1.9 %copy-start.1 = (bf16[16,400,256]{2,1,0:T(8,128)(2,1)S(1)}, bf16[16,400,256]{2,1,0:T(8,128)(2,1)}, u32[]{:S(2)}) copy-start(bf16[16,400,256]{2,1,0:T(8,128)(2,1)} %all_to_all.15.got) | copy-start | bytes 9830404
Sparse Core Ops, SparseCore 0:
  31.5 57.3 all-gather.1
  99.5 56.0 reduce-scatter.1

commit v7 on v6

--- a/solution.py
+++ b/solution.py
@@ -64,33 +64,63 @@
     copies[1].wait()
 
 
-def pack_forward(stream, cot, partial, out):
+def pack_forward(stream, cot, partial, out, sem):
+    copies = []
     for t in range(NT):
-        out[t, :S] = stream[...]
-        out[t, S : 2 * S] = cot[...]
-        out[t, 2 * S :] = partial[0, :, t * W : (t + 1) * W]
-
-
-def prepare(got, stream, gain, normed, cot, normed_t, cot_t, inv_out, out_slice):
+        parts = (stream, cot, partial.at[0, :, t * W : (t + 1) * W])
+        for i, part in enumerate(parts):
+            copies.append(pltpu.make_async_copy(part, out.at[t, i * S : (i + 1) * S], sem.at[i, t]))
+            copies[-1].start()
+    for copy in copies:
+        copy.wait()
+
+
+def prepare(
+    got_in, stream, gain, normed_out, cot_out, normed_t_out, cot_t_out, inv_out, out_slice,
+    got, normed, cot, normed_t, cot_t, in_sem, cot_sem, normed_sem,
+):
+    arrived = [pltpu.make_async_copy(got_in.at[t], got.at[t], in_sem.at[t]) for t in range(NT)]
+    for copy in arrived:
+        copy.start()
     squares = jnp.zeros((S, 1), F32)
     pending = jnp.zeros((S, W), F32)
     for t in range(NT):
+        arrived[t].wait()
         block = got[t, :S].astype(F32)
         squares += jnp.sum(block * block, -1, keepdims=True)
         pending += got[t, 2 * S :].astype(F32)
+        for f in (2 * t, 2 * t + 1):
+            at, half = place(f) * B, (f % 2) * B
+            piece = got[t, S : 2 * S, half : half + B]
+            cot[:, at : at + B] = piece
+            cot_t[at : at + B] = flip(piece).astype(BF16)
+    leaving = [
+        pltpu.make_async_copy(cot, cot_out, cot_sem.at[0]),
+        pltpu.make_async_copy(cot_t, cot_t_out, cot_sem.at[1]),
+    ]
+    for copy in leaving:
+        copy.start()
     inv = lax.rsqrt(squares * (1.0 / D) + 1e-05)
     inv_out[...] = jnp.broadcast_to(inv, (S, 128))
     out_slice[...] = (stream[...].astype(F32) + pending).astype(BF16)
-    for f in range(NF):
-        t, half = f // 2, (f % 2) * B
-        at = place(f) * B
-        block = got[t, :S, half : half + B].astype(F32)
-        block = block * inv * gain[:, f * B : (f + 1) * B].astype(F32)
-        normed[:, at : at + B] = block.astype(BF16)
-        normed_t[at : at + B] = block.T.astype(BF16)
-        piece = got[t, S : 2 * S, half : half + B]
-        cot[:, at : at + B] = piece
-        cot_t[at : at + B] = flip(piece).astype(BF16)
+    for y in range(Y):
+        for z in range(ZH):
+            f = z * Y + y
+            t, half, at = f // 2, (f % 2) * B, place(f) * B
+            block = got[t, :S, half : half + B].astype(F32)
+            block = block * inv * gain[:, f * B : (f + 1) * B].astype(F32)
+            normed[:, at : at + B] = block.astype(BF16)
+            normed_t[at : at + B] = block.T.astype(BF16)
+        k = slice(y * ZH * B, (y + 1) * ZH * B)
+        new = [
+            pltpu.make_async_copy(normed.at[:, k], normed_out.at[:, k], normed_sem.at[0, y]),
+            pltpu.make_async_copy(normed_t.at[k], normed_t_out.at[k], normed_sem.at[1, y]),
+        ]
+        for copy in new:
+            copy.start()
+        leaving += new
+    for copy in leaving:
+        copy.wait()
 
 
 def attend(
@@ -238,10 +268,31 @@
     weights = lax.all_gather(weights, "zh", axis=0, tiled=True)
     weights = lax.all_gather(weights, "y", axis=0, tiled=True)
 
-    send = call(pack_forward, arr(NT, 3 * S, W), 56)(stream_in, cot_attn, newer_partial)
+    send = call(
+        pack_forward,
+        arr(NT, 3 * S, W),
+        56,
+        in_specs=[VMEM, VMEM, HBM],
+        out_specs=HBM,
+        scratch_shapes=[pltpu.SemaphoreType.DMA((3, NT))],
+    )(stream_in, cot_attn, newer_partial)
     got = lax.all_to_all(send, TENSOR, 0, 0, tiled=True)
     normed, cot, normed_t, cot_t, inv, out_slice = call(
-        prepare, [arr(S, D), arr(S, D), arr(D, S), arr(D, S), arr(S, 128, of=F32), arr(S, W)], 56
+        prepare,
+        [arr(S, D), arr(S, D), arr(D, S), arr(D, S), arr(S, 128, of=F32), arr(S, W)],
+        56,
+        in_specs=[HBM, VMEM, VMEM],
+        out_specs=[HBM] * 4 + [VMEM] * 2,
+        scratch_shapes=[
+            pltpu.VMEM((NT, 3 * S, W), BF16),
+            pltpu.VMEM((S, D), BF16),
+            pltpu.VMEM((S, D), BF16),
+            pltpu.VMEM((D, S), BF16),
+            pltpu.VMEM((D, S), BF16),
+            pltpu.SemaphoreType.DMA((NT,)),
+            pltpu.SemaphoreType.DMA((2,)),
+            pltpu.SemaphoreType.DMA((2, Y)),
+        ],
     )(got, stream_in, gain)
 
     terms, kept = call(

time: 186 us -> 220 us (1.18)
  Pallas kernels: 25.5 us -> 58.9 us
    pallas_call x1, Pallas kernels: 3.2 us -> 34.2 us  [per_device(): call(pack_forward, arr(NT, 3 * S, W), 56, in_specs=[VMEM, VMEM, HBM], out...]
    pallas_call x1, Pallas kernels: 4.88 us -> 7.31 us  [per_device(): call(prepare, [arr(S, D), arr(S, D), arr(D, S), arr(D, S), arr(S, 128, of...]
  transfers between devices with their start and end apart: 4 -> 4, of which waited for: 3 -> 3; matrix products, arithmetic and copies ran while one was open for 1% -> 1% of each run, Pallas kernels for 9% -> 22%
where the time goes in v7:
time: 220 us; the launch traced here: 219 us
  blocking collectives  66.1 us (30%)
  waiting for transfers between devices  62.2 us (28%)
  Pallas kernels  58.9 us (27%)
  starting transfers between devices  14.6 us (7%)
  between operations  14.2 us (6%)
  local copies, waits for them, and re-layouts  3.28 us (1%)
    all_to_all x1, waiting for transfers between devices, per_device(): got = lax.all_to_all(send, TENSOR, 0, 0, tiled=True)  44.1 us
    all_to_all x1, blocking collectives, per_device(): got = lax.all_to_all(send, TENSOR, 0, 0, tiled=True)  43.7 us
    pallas_call x1, Pallas kernels, per_device(): call(pack_forward, arr(NT, 3 * S, W), 56, in_specs=[VMEM, VMEM, HBM], out...  34.2 us
    all_gather x1, blocking collectives, per_device(): weights = lax.all_gather(weights, 'zh', axis=0, tiled=True)  22.4 us
    all_to_all x1, waiting for transfers between devices, per_device(): terms = lax.all_to_all(terms.reshape(ZH, B, 2 * W), 'zh', 0, 0, tiled=True)  11.9 us
    all_to_all x1, starting transfers between devices, per_device(): terms = lax.all_to_all(terms.reshape(ZH, B, 2 * W), 'zh', 0, 0, tiled=True)  7.38 us
    pallas_call x1, Pallas kernels, per_device(): call(prepare, [arr(S, D), arr(S, D), arr(D, S), arr(D, S), arr(S, 128, of...  7.31 us
    pallas_call x1, Pallas kernels, per_device(): call(attend, [arr(D, 2 * W), arr(6, S, W)], 56, flops=8 * S * D * W, in_s...  7.23 us
  transfers between devices with their start and end apart: 4, of which 3 were waited for; matrix products, arithmetic and copies ran while one was open for 1% of the time, Pallas kernels for 22%

profile of v7, /device:TPU:6, one launch (start us, length us, event | category | flops | bytes accessed | tf_op | source)
XLA Modules:
  0.0 219.3 jit_solution(1383227449903708816)
XLA Ops:
  7.2 0.0 copy-start
  7.2 0.0 all-gather.2.cloned.1.call-start
  7.2 1.7 shard_map.129
  8.9 22.4 %all_gather.6 = bf16[512,512]{1,0:T(8,128)(2,1)} all-gather(bf16[128,512]{1,0:T(8,128)(2,1)} %shard_map.129), channel_id=1, replica_groups=mesh['zh'=4,'y'=8,'zl'=2,'x'=4,'c'=2] {'zh'}, dimensions={0}, use_global_device_ids=true | all-gather | bytes 655360 | tf_op jit(solution)/shard_map/all_gather | solution.py:268
  31.3 0.0 all-gather.2.cloned.1.call-update
  31.4 34.2 %shard_map.127 = bf16[16,384,256]{2,1,0:T(8,128)(2,1)} custom-call(bf16[128,256]{1,0:T(8,128)(2,1)} %stream.5, bf16[128,256]{1,0:T(8,128)(2,1)} %cot.1, bf16[1,128,4096]{2,1,0:T(8,128)(2,1)} %partial.1), custom_call_target="tpu_custom_call" | custom-call | tf_op jit(solution)/shard_map/pallas_call | solution.py:271
  65.6 7.2 %all-to-all-start = ((bf16[16,384,256]{2,1,0:T(8,128)(2,1)}), bf16[16,384,256]{2,1,0:T(8,128)(2,1)}, u32[]{:S(2)}, u32[]{:S(2)}) async-start(bf16[16,384,256]{2,1,0:T(8,128)(2,1)} %shard_map.127), calls=%async_computation | async-start | bytes 6291456 | tf_op jit(solution)/shard_map/all_to_all | solution.py:279
  72.7 0.0 reduce-scatter.2.cloned.1.call-start
  72.8 0.6 reshape.19.gain
  73.4 0.6 constant_dynamic-slice_fusion.kv_in
  74.1 44.1 %all-to-all-done.got_in.got = bf16[16,384,256]{2,1,0:T(8,128)(2,1)} async-done(((bf16[16,384,256]{2,1,0:T(8,128)(2,1)}), bf16[16,384,256]{2,1,0:T(8,128)(2,1)}, u32[]{:S(2)}, u32[]{:S(2)}) %all-to-all-start) | async-done | bytes 3145760 | tf_op jit(solution)/shard_map/all_to_all | solution.py:279
  118.1 7.3 %shard_map.128 = (bf16[128,4096]{1,0:T(8,128)(2,1)}, bf16[128,4096]{1,0:T(8,128)(2,1)}, bf16[4096,128]{1,0:T(8,128)(2,1)}, bf16[4096,128]{1,0:T(8,128)(2,1)}, f3...) custom-call(bf16[16,384,256]{2,1,0:T(8,128)(2,1)} %all-to-all-done.got_in.got, bf16[128,256]{1,0:T(8,128)(2,1)} %stream.5, ...), custom_call_target="tpu_custom_call" | custom-call | tf_op jit(solution)/shard_map/pallas_call | solution.py:280
  125.5 0.0 all-gather.2.cloned.1.call-done.weights
  125.5 7.2 %shard_map.130 = (bf16[4096,512]{1,0:T(8,128)(2,1)}, bf16[6,128,256]{2,1,0:T(8,128)(2,1)}) custom-call(bf16[128,4096]{1,0:T(8,128)(2,1)} %get-tuple-element.21.normed_in, bf16[128,4096]{1,0:T(8,128)(2,1)} %get-tuple-element.22.cot_in, bf16[4096,128]{1,0:T(8,128)(2,1)} %get-tuple-element.23.normed_t_in, bf16[4096,128]{1,0:T(8,128)(2,1)} %get-tuple-element.24.cot_t_in, ...), custom_call_target="tpu_custom_call" | custom-call | flops 1073741824 | tf_op jit(solution)/shard_map/pallas_call | solution.py:298
  132.7 0.0 reduce-scatter.2.cloned.1.call-update
  132.7 6.3 %shard_map.131 = (bf16[1,128,4096]{2,1,0:T(8,128)(2,1)}, bf16[16,400,256]{2,1,0:T(8,128)(2,1)}) custom-call(bf16[6,128,256]{2,1,0:T(8,128)(2,1)} %get-tuple-element.25.kept, bf16[4096,512]{1,0:T(8,128)(2,1)} %all-gather.2.cloned.1.call-done.weights, bf16[16,384,256]{2,1,0:T(8,128)(2,1)} %all-to-all-done.got_in.got, bf16[1,4096]{1,0:T(2,128)(2,1)} %reshape.19.gain, ...), custom_call_target="tpu_custom_call" | custom-call | flops 536870912 | tf_op jit(solution)/shard_map/pallas_call | solution.py:325
  139.1 43.7 %all_to_all.15.got = bf16[16,400,256]{2,1,0:T(8,128)(2,1)} all-to-all(bf16[16,400,256]{2,1,0:T(8,128)(2,1)} %get-tuple-element.27), channel_id=1, replica_groups=mesh['zh'=4,'y'=8,'zl'=2,'x'=4,'c'=2] {'zl','x','c'}, dimensions={0} | all-to-all | bytes 6553600 | tf_op jit(solution)/shard_map/all_to_all | solution.py:334
  182.8 6.2 %reduce-scatter.2.cloned.1.call-done = bf16[512,512]{1,0:T(8,128)(2,1)} async-done(((bf16[4096,512]{1,0:T(8,128)(2,1)}), bf16[512,512]{1,0:T(8,128)(2,1)}) %reduce-scatter.2.cloned.1.call-update) | async-done | bytes 524304 | tf_op jit(solution)/shard_map/reduce_scatter | solution.py:320
  189.0 7.4 %all-to-all-start.2 = ((bf16[4,128,512]{2,1,0:T(8,128)(2,1)}), bf16[4,128,512]{2,1,0:T(8,128)(2,1)S(1)}, u32[]{:S(2)}, u32[]{:S(2)}) async-start(bf16[4,128,512]{2,1,0:T(8,128)(2,1)} %bitcast.1), calls=%async_computation.3 | async-start | bytes 1048576 | tf_op jit(solution)/shard_map/all_to_all | solution.py:321
  196.4 0.1 dynamic-slice.3
  196.5 1.9 copy-done.1
  198.4 1.4 shard_map.132
  199.8 11.9 %all-to-all-done.2.got = bf16[4,128,512]{2,1,0:T(8,128)(2,1)S(1)} async-done(((bf16[4,128,512]{2,1,0:T(8,128)(2,1)}), bf16[4,128,512]{2,1,0:T(8,128)(2,1)S(1)}, u32[]{:S(2)}, u32[]{:S(2)}) %all-to-all-start.2) | async-done | bytes 524320 | tf_op jit(solution)/shard_map/all_to_all | solution.py:321
  211.7 0.7 shard_map.133
  (11 shorter events, 0.0 us)
Async XLA Ops:
  7.2 66.3 %copy-start = (bf16[128,2048]{1,0:T(8,128)(2,1)S(1)}, bf16[128,2048]{1,0:T(8,128)(2,1)}, u32[]{:S(2)}) copy-start(bf16[128,2048]{1,0:T(8,128)(2,1)} %param.12) | copy-start | bytes 1572868
  7.2 118.3 %all-gather.2.cloned.1.call-start = ((), (), s32[]{:S(2)}) async-start(), calls=%async_computation.4 | async-start | bytes 4718592 | tf_op jit(solution)/shard_map/all_gather | solution.py:269
  65.5 7.3 %copy-start.5 = (bf16[4096]{0:T(1024)(128)(2,1)S(1)}, bf16[4096]{0:T(1024)(128)(2,1)}, u32[]{:S(2)}) copy-start(bf16[4096]{0:T(1024)(128)(2,1)} %param.10) | copy-start | bytes 24580
  65.6 52.6 %all-to-all-start = ((bf16[16,384,256]{2,1,0:T(8,128)(2,1)}), bf16[16,384,256]{2,1,0:T(8,128)(2,1)}, u32[]{:S(2)}, u32[]{:S(2)}) async-start(bf16[16,384,256]{2,1,0:T(8,128)(2,1)} %shard_map.127), calls=%async_computation | async-start | bytes 6291456 | tf_op jit(solution)/shard_map/all_to_all | solution.py:279
  72.7 116.3 %reduce-scatter.2.cloned.1.call-start = ((), (), s32[]{:S(2)}) async-start(), calls=%async_computation.5 | async-start | bytes 4718592 | tf_op jit(solution)/shard_map/reduce_scatter | solution.py:320
  139.1 57.4 %copy-start.2 = (bf16[128,256]{1,0:T(8,128)(2,1)S(1)}, bf16[128,256]{1,0:T(8,128)(2,1)}, u32[]{:S(2)}) copy-start(bf16[128,256]{1,0:T(8,128)(2,1)} %stream.5) | copy-start | bytes 196612
  139.1 57.4 %copy-start.3 = (bf16[128,256]{1,0:T(8,128)(2,1)S(1)}, bf16[128,256]{1,0:T(8,128)(2,1)}, u32[]{:S(2)}) copy-start(bf16[128,256]{1,0:T(8,128)(2,1)} %cot_stream.1) | copy-start | bytes 196612
  139.1 57.4 %copy-start.4 = (f32[128,128]{1,0:T(8,128)S(1)}, f32[128,128]{1,0:T(8,128)}, u32[]{:S(2)}) copy-start(f32[128,128]{1,0:T(8,128)} %get-tuple-element.28.inv_in) | copy-start | bytes 196612
  189.0 22.7 %all-to-all-start.2 = ((bf16[4,128,512]{2,1,0:T(8,128)(2,1)}), bf16[4,128,512]{2,1,0:T(8,128)(2,1)S(1)}, u32[]{:S(2)}, u32[]{:S(2)}) async-start(bf16[4,128,512]{2,1,0:T(8,128)(2,1)} %bitcast.1), calls=%async_computation.3 | async-start | bytes 1048576 | tf_op jit(solution)/shard_map/all_to_all | solution.py:321
  196.5 1.9 copy-start.1
Sparse Core Ops, SparseCore 0:
  31.5 57.3 all-gather.1
  132.9 56.0 reduce-scatter.1

commit v8 on v6

--- a/solution.py
+++ b/solution.py
@@ -65,22 +65,19 @@
 
 
 def pack_forward(stream, cot, partial, out):
-    for t in range(NT):
+    for t in range(out.shape[0]):
         out[t, :S] = stream[...]
         out[t, S : 2 * S] = cot[...]
         out[t, 2 * S :] = partial[0, :, t * W : (t + 1) * W]
 
 
-def prepare(got, stream, gain, normed, cot, normed_t, cot_t, inv_out, out_slice):
+def prepare(got, gain, normed, cot, normed_t, cot_t, inv_out):
     squares = jnp.zeros((S, 1), F32)
-    pending = jnp.zeros((S, W), F32)
     for t in range(NT):
         block = got[t, :S].astype(F32)
         squares += jnp.sum(block * block, -1, keepdims=True)
-        pending += got[t, 2 * S :].astype(F32)
     inv = lax.rsqrt(squares * (1.0 / D) + 1e-05)
     inv_out[...] = jnp.broadcast_to(inv, (S, 128))
-    out_slice[...] = (stream[...].astype(F32) + pending).astype(BF16)
     for f in range(NF):
         t, half = f // 2, (f % 2) * B
         at = place(f) * B
@@ -154,7 +151,11 @@
         copy.wait()
 
 
-def project(kept, weights, got, gain, out_slice, partial, send):
+def project(kept, weights, got, pending_in, gain, own, partial, send):
+    pending = jnp.zeros((S, W), F32)
+    for t in range(NT):
+        pending += pending_in[t].astype(F32)
+    out_slice = (own[...].astype(F32) + pending).astype(BF16)
     att, gq, low, gs, q, g = (kept.at[i] for i in range(6))
     grad_keys = jnp.zeros((S, HS), F32)
     grad_values = jnp.zeros((S, HS), F32)
@@ -187,7 +188,7 @@
     pieces = jnp.concatenate([pieces, jnp.zeros((EXTRA, W - S), F32)], 1).astype(BF16)
     for t in range(NT):
         send[t, S : 2 * S] = kv_part
-        send[t, 2 * S : 3 * S] = out_slice[...]
+        send[t, 2 * S : 3 * S] = out_slice
         send[t, 3 * S :] = pieces
 
 
@@ -238,11 +239,24 @@
     weights = lax.all_gather(weights, "zh", axis=0, tiled=True)
     weights = lax.all_gather(weights, "y", axis=0, tiled=True)
 
-    send = call(pack_forward, arr(NT, 3 * S, W), 56)(stream_in, cot_attn, newer_partial)
+    whole, steps = pl.BlockSpec((S, W), lambda i: (0, 0)), 4
+    send = call(
+        pack_forward,
+        arr(NT, 3 * S, W),
+        56,
+        grid=(steps,),
+        in_specs=[whole, whole, pl.BlockSpec((1, S, D // steps), lambda i: (0, 0, i))],
+        out_specs=pl.BlockSpec((NT // steps, 3 * S, W), lambda i: (i, 0, 0)),
+    )(stream_in, cot_attn, newer_partial)
     got = lax.all_to_all(send, TENSOR, 0, 0, tiled=True)
-    normed, cot, normed_t, cot_t, inv, out_slice = call(
-        prepare, [arr(S, D), arr(S, D), arr(D, S), arr(D, S), arr(S, 128, of=F32), arr(S, W)], 56
-    )(got, stream_in, gain)
+    normed, cot, normed_t, cot_t, inv = call(
+        prepare,
+        [arr(S, D), arr(S, D), arr(D, S), arr(D, S), arr(S, 128, of=F32)],
+        56,
+        grid=(1,),
+        in_specs=[pl.BlockSpec((NT, 2 * S, W), lambda i: (0, 0, 0)), VMEM],
+        out_specs=[VMEM] * 5,
+    )(got, gain)
 
     terms, kept = call(
         attend,
@@ -271,15 +285,16 @@
     wq_grad, wo_grad = call(add_up, [arr(B, W), arr(W, B)], 4)(terms)
 
     streams = pl.BlockSpec((NT, S, W), lambda i: (0, 0, 0))
+    pieces = pl.BlockSpec((NT, S, W), lambda i: (0, 2, 0))
     attn_partial, send = call(
         project,
         [arr(1, S, D), arr(NT, 3 * S + EXTRA, W)],
         56,
         flops=4 * S * D * W,
         grid=(1,),
-        in_specs=[VMEM] * 2 + [streams] + [VMEM] * 2,
+        in_specs=[VMEM] * 2 + [streams, pieces] + [VMEM] * 2,
         out_specs=[VMEM, VMEM],
-    )(kept, weights, got, gain, out_slice)
+    )(kept, weights, got, got, gain, stream_in)
     got = lax.all_to_all(send, TENSOR, 0, 0, tiled=True)
     stream_out, stream_grad, kv_grad = call(
         finish, [arr(S, D), arr(S, W), arr(*keys_values.shape)], 12

time: 186 us -> 187 us (level)
  no operation moved by 1% of the time
where the time goes in v8:
time: 187 us; the launch traced here: 186 us
  blocking collectives  66.1 us (35%)
  waiting for transfers between devices  61.8 us (33%)
  Pallas kernels  26.2 us (14%)
  starting transfers between devices  14.7 us (8%)
  between operations  14.1 us (8%)
  local copies, waits for them, and re-layouts  3.28 us (2%)
    all_to_all x1, waiting for transfers between devices, per_device(): got = lax.all_to_all(send, TENSOR, 0, 0, tiled=True)  44.1 us
    all_to_all x1, blocking collectives, per_device(): got = lax.all_to_all(send, TENSOR, 0, 0, tiled=True)  43.7 us
    all_gather x1, blocking collectives, per_device(): weights = lax.all_gather(weights, 'zh', axis=0, tiled=True)  22.4 us
    all_to_all x1, waiting for transfers between devices, per_device(): terms = lax.all_to_all(terms.reshape(ZH, B, 2 * W), 'zh', 0, 0, tiled=True)  11.9 us
    all_to_all x1, starting transfers between devices, per_device(): terms = lax.all_to_all(terms.reshape(ZH, B, 2 * W), 'zh', 0, 0, tiled=True)  7.37 us
    all_to_all x1, starting transfers between devices, per_device(): got = lax.all_to_all(send, TENSOR, 0, 0, tiled=True)  7.27 us
    pallas_call x1, Pallas kernels, per_device(): call(attend, [arr(D, 2 * W), arr(6, S, W)], 56, flops=8 * S * D * W, in_s...  7.23 us
    pallas_call x1, Pallas kernels, per_device(): call(project, [arr(1, S, D), arr(NT, 3 * S + EXTRA, W)], 56, flops=4 * S...  6.71 us
  transfers between devices with their start and end apart: 4, of which 3 were waited for; matrix products, arithmetic and copies ran while one was open for 1% of the time, Pallas kernels for 9%

profile of v8, /device:TPU:6, one launch (start us, length us, event | category | flops | bytes accessed | tf_op | source)
XLA Modules:
  0.0 186.3 jit_solution(7487128692966554019)
XLA Ops:
  7.2 0.0 copy-start
  7.2 0.0 all-gather.2.cloned.1.call-start
  7.2 1.7 shard_map.129
  8.9 22.4 %all_gather.6 = bf16[512,512]{1,0:T(8,128)(2,1)} all-gather(bf16[128,512]{1,0:T(8,128)(2,1)} %shard_map.129), channel_id=1, replica_groups=mesh['zh'=4,'y'=8,'zl'=2,'x'=4,'c'=2] {'zh'}, dimensions={0}, use_global_device_ids=true | all-gather | bytes 655360 | tf_op jit(solution)/shard_map/all_gather | solution.py:239
  31.3 0.0 all-gather.2.cloned.1.call-update
  31.4 3.8 %shard_map.127 = bf16[16,384,256]{2,1,0:T(8,128)(2,1)} custom-call(bf16[128,256]{1,0:T(8,128)(2,1)} %stream.3, bf16[128,256]{1,0:T(8,128)(2,1)} %cot.1, bf16[1,128,4096]{2,1,0:T(8,128)(2,1)} %partial.1), custom_call_target="tpu_custom_call" | custom-call | tf_op jit(solution)/shard_map/pallas_call | solution.py:243
  35.2 7.3 %all-to-all-start = ((bf16[16,384,256]{2,1,0:T(8,128)(2,1)}), bf16[16,384,256]{2,1,0:T(8,128)(2,1)}, u32[]{:S(2)}, u32[]{:S(2)}) async-start(bf16[16,384,256]{2,1,0:T(8,128)(2,1)} %shard_map.127), calls=%async_computation | async-start | bytes 6291456 | tf_op jit(solution)/shard_map/all_to_all | solution.py:251
  42.5 0.0 reduce-scatter.2.cloned.1.call-start
  42.6 0.6 reshape.19.gain
  43.2 0.0 copy-done
  43.2 0.6 constant_dynamic-slice_fusion.kv_in
  43.8 44.1 %all-to-all-done.got.pending_in = bf16[16,384,256]{2,1,0:T(8,128)(2,1)} async-done(((bf16[16,384,256]{2,1,0:T(8,128)(2,1)}), bf16[16,384,256]{2,1,0:T(8,128)(2,1)}, u32[]{:S(2)}, u32[]{:S(2)}) %all-to-all-start) | async-done | bytes 3145760 | tf_op jit(solution)/shard_map/all_to_all | solution.py:251
  87.9 4.6 %shard_map.128 = (bf16[128,4096]{1,0:T(8,128)(2,1)}, bf16[128,4096]{1,0:T(8,128)(2,1)}, bf16[4096,128]{1,0:T(8,128)(2,1)}, bf16[4096,128]{1,0:T(8,128)(2,1)}, f32[128,128]{1,0:T(8,128)}) custom-call(bf16[16,384,256]{2,1,0:T(8,128)(2,1)} %all-to-all-done.got.pending_in, bf16[1,4096]{1,0:T(2,128)(2,1)} %reshape.19.gain), custom_call_target="tpu_custom_call" | custom-call | tf_op jit(solution)/shard_map/pallas_call | solution.py:252
  92.5 7.2 %shard_map.130 = (bf16[4096,512]{1,0:T(8,128)(2,1)}, bf16[6,128,256]{2,1,0:T(8,128)(2,1)}) custom-call(bf16[128,4096]{1,0:T(8,128)(2,1)} %get-tuple-element.20.normed_in, bf16[128,4096]{1,0:T(8,128)(2,1)} %get-tuple-element.21.cot_in, bf16[4096,128]{1,0:T(8,128)(2,1)} %get-tuple-element.22.normed_t_in, bf16[4096,128]{1,0:T(8,128)(2,1)} %get-tuple-element.23.cot_t_in, ...), custom_call_target="tpu_custom_call" | custom-call | flops 1073741824 | tf_op jit(solution)/shard_map/pallas_call | solution.py:261
  99.7 0.0 reduce-scatter.2.cloned.1.call-update
  99.8 6.7 %shard_map.131 = (bf16[1,128,4096]{2,1,0:T(8,128)(2,1)}, bf16[16,400,256]{2,1,0:T(8,128)(2,1)}) custom-call(bf16[6,128,256]{2,1,0:T(8,128)(2,1)} %get-tuple-element.24.kept, bf16[4096,512]{1,0:T(8,128)(2,1)} %all-gather.2.cloned.1.call-done.weights, bf16[16,384,256]{2,1,0:T(8,128)(2,1)} %all-to-all-done.got.pending_in, ...), custom_call_target="tpu_custom_call" | custom-call | flops 536870912 | tf_op jit(solution)/shard_map/pallas_call | solution.py:289
  106.5 43.7 %all_to_all.15.got = bf16[16,400,256]{2,1,0:T(8,128)(2,1)} all-to-all(bf16[16,400,256]{2,1,0:T(8,128)(2,1)} %get-tuple-element.25), channel_id=1, replica_groups=mesh['zh'=4,'y'=8,'zl'=2,'x'=4,'c'=2] {'zl','x','c'}, dimensions={0} | all-to-all | bytes 6553600 | tf_op jit(solution)/shard_map/all_to_all | solution.py:298
  150.2 5.8 %reduce-scatter.2.cloned.1.call-done = bf16[512,512]{1,0:T(8,128)(2,1)} async-done(((bf16[4096,512]{1,0:T(8,128)(2,1)}), bf16[512,512]{1,0:T(8,128)(2,1)}) %reduce-scatter.2.cloned.1.call-update) | async-done | bytes 524304 | tf_op jit(solution)/shard_map/reduce_scatter | solution.py:283
  156.0 7.4 %all-to-all-start.2 = ((bf16[4,128,512]{2,1,0:T(8,128)(2,1)}), bf16[4,128,512]{2,1,0:T(8,128)(2,1)S(1)}, u32[]{:S(2)}, u32[]{:S(2)}) async-start(bf16[4,128,512]{2,1,0:T(8,128)(2,1)} %bitcast.1), calls=%async_computation.3 | async-start | bytes 1048576 | tf_op jit(solution)/shard_map/all_to_all | solution.py:284
  163.4 0.1 dynamic-slice.3
  163.5 1.9 %copy-done.1 = bf16[16,400,256]{2,1,0:T(8,128)(2,1)S(1)} copy-done((bf16[16,400,256]{2,1,0:T(8,128)(2,1)S(1)}, bf16[16,400,256]{2,1,0:T(8,128)(2,1)}, u32[]{:S(2)}) %copy-start.1) | copy-done | bytes 3276824
  165.4 1.4 shard_map.132
  166.8 11.9 %all-to-all-done.2.got = bf16[4,128,512]{2,1,0:T(8,128)(2,1)S(1)} async-done(((bf16[4,128,512]{2,1,0:T(8,128)(2,1)}), bf16[4,128,512]{2,1,0:T(8,128)(2,1)S(1)}, u32[]{:S(2)}, u32[]{:S(2)}) %all-to-all-start.2) | async-done | bytes 524320 | tf_op jit(solution)/shard_map/all_to_all | solution.py:284
  178.7 0.7 shard_map.133
  (11 shorter events, 0.0 us)
Async XLA Ops:
  7.2 36.0 %copy-start = (bf16[128,2048]{1,0:T(8,128)(2,1)S(1)}, bf16[128,2048]{1,0:T(8,128)(2,1)}, u32[]{:S(2)}) copy-start(bf16[128,2048]{1,0:T(8,128)(2,1)} %param.12) | copy-start | bytes 1572868
  7.2 85.3 %all-gather.2.cloned.1.call-start = ((), (), s32[]{:S(2)}) async-start(), calls=%async_computation.4 | async-start | bytes 4718592 | tf_op jit(solution)/shard_map/all_gather | solution.py:240
  35.2 7.4 %copy-start.5 = (bf16[4096]{0:T(1024)(128)(2,1)S(1)}, bf16[4096]{0:T(1024)(128)(2,1)}, u32[]{:S(2)}) copy-start(bf16[4096]{0:T(1024)(128)(2,1)} %param.10) | copy-start | bytes 24580
  35.2 52.7 %all-to-all-start = ((bf16[16,384,256]{2,1,0:T(8,128)(2,1)}), bf16[16,384,256]{2,1,0:T(8,128)(2,1)}, u32[]{:S(2)}, u32[]{:S(2)}) async-start(bf16[16,384,256]{2,1,0:T(8,128)(2,1)} %shard_map.127), calls=%async_computation | async-start | bytes 6291456 | tf_op jit(solution)/shard_map/all_to_all | solution.py:251
  42.5 113.5 %reduce-scatter.2.cloned.1.call-start = ((), (), s32[]{:S(2)}) async-start(), calls=%async_computation.5 | async-start | bytes 4718592 | tf_op jit(solution)/shard_map/reduce_scatter | solution.py:283
  106.5 57.0 %copy-start.2 = (bf16[128,256]{1,0:T(8,128)(2,1)S(1)}, bf16[128,256]{1,0:T(8,128)(2,1)}, u32[]{:S(2)}) copy-start(bf16[128,256]{1,0:T(8,128)(2,1)} %stream.3) | copy-start | bytes 196612
  106.5 57.0 %copy-start.3 = (bf16[128,256]{1,0:T(8,128)(2,1)S(1)}, bf16[128,256]{1,0:T(8,128)(2,1)}, u32[]{:S(2)}) copy-start(bf16[128,256]{1,0:T(8,128)(2,1)} %cot_stream.1) | copy-start | bytes 196612
  106.5 57.0 %copy-start.4 = (f32[128,128]{1,0:T(8,128)S(1)}, f32[128,128]{1,0:T(8,128)}, u32[]{:S(2)}) copy-start(f32[128,128]{1,0:T(8,128)} %get-tuple-element.26.inv_in) | copy-start | bytes 196612
  156.0 22.7 %all-to-all-start.2 = ((bf16[4,128,512]{2,1,0:T(8,128)(2,1)}), bf16[4,128,512]{2,1,0:T(8,128)(2,1)S(1)}, u32[]{:S(2)}, u32[]{:S(2)}) async-start(bf16[4,128,512]{2,1,0:T(8,128)(2,1)} %bitcast.1), calls=%async_computation.3 | async-start | bytes 1048576 | tf_op jit(solution)/shard_map/all_to_all | solution.py:284
  163.5 1.9 %copy-start.1 = (bf16[16,400,256]{2,1,0:T(8,128)(2,1)S(1)}, bf16[16,400,256]{2,1,0:T(8,128)(2,1)}, u32[]{:S(2)}) copy-start(bf16[16,400,256]{2,1,0:T(8,128)(2,1)} %all_to_all.15.got) | copy-start | bytes 9830404
Sparse Core Ops, SparseCore 0:
  31.5 57.3 all-gather.1
  99.9 56.0 reduce-scatter.1

commit v9 on v6

--- a/solution.py
+++ b/solution.py
@@ -211,10 +211,10 @@
     stream_grad[...] = (cot_stream[...].astype(F32) + grad).astype(BF16)
 
 
-def add_up(got, wq_grad, wo_grad):
-    total = got[0].astype(F32)
-    for z in range(1, ZH):
-        total += got[z].astype(F32)
+def add_up(own, first, second, third, wq_grad, wo_grad):
+    total = own[...].astype(F32)
+    for got in (first, second, third):
+        total += got[...].astype(F32)
     wq_grad[...] = total[:, :W].astype(BF16)
     wo_grad[...] = total[:, W:].T.astype(BF16)
 
@@ -267,8 +267,15 @@
     )(normed, cot, normed_t, cot_t, weights, kv_own)
 
     terms = lax.psum_scatter(terms, "y", scatter_dimension=0, tiled=True)
-    terms = lax.all_to_all(terms.reshape(ZH, B, 2 * W), "zh", 0, 0, tiled=True)
-    wq_grad, wo_grad = call(add_up, [arr(B, W), arr(W, B)], 4)(terms)
+    mine = lax.axis_index("zh")
+
+    def ahead(d):
+        return lax.dynamic_slice_in_dim(terms, lax.rem(mine + d, ZH) * B, B, 0)
+
+    brought = [
+        lax.ppermute(ahead(d), "zh", [(i, (i + d) % ZH) for i in range(ZH)]) for d in (2, 1, 3)
+    ]
+    wq_grad, wo_grad = call(add_up, [arr(B, W), arr(W, B)], 4)(ahead(0), *brought)
 
     streams = pl.BlockSpec((NT, S, W), lambda i: (0, 0, 0))
     attn_partial, send = call(

time: 186 us -> 187 us (level)
  blocking collectives: 66.1 us -> 22.4 us
  waiting for transfers between devices: 62.2 us -> 90.6 us
  starting transfers between devices: 14.7 us -> 28.6 us
  Pallas kernels: 25.5 us -> 27.4 us
    all_to_all x1 -> x0, blocking collectives: 43.7 us -> none  [per_device(): got = lax.all_to_all(send, TENSOR, 0, 0, tiled=True)]
    reduce_scatter x1, waiting for transfers between devices: 6.21 us -> 44.7 us  [per_device(): terms = lax.psum_scatter(terms, 'y', scatter_dimension=0, tiled=True)]
    ppermute x0 -> x3, starting transfers between devices: none -> 16 us  [per_device(): lax.ppermute(ahead(d), 'zh', [(i, (i + d) % ZH) for i in range(ZH)])]
    all_to_all x1 -> x0, waiting for transfers between devices: 11.9 us -> none  [per_device(): terms = lax.all_to_all(terms.reshape(ZH, B, 2 * W), 'zh', 0, 0, tiled=True)]
    all_to_all x1 -> x0, starting transfers between devices: 7.38 us -> none  [per_device(): terms = lax.all_to_all(terms.reshape(ZH, B, 2 * W), 'zh', 0, 0, tiled=True)]
    all_to_all x1 -> x2, starting transfers between devices: 7.27 us -> 12.5 us  [per_device(): got = lax.all_to_all(send, TENSOR, 0, 0, tiled=True)]
    pallas_call x1, Pallas kernels: 1.44 us -> 3.36 us  [per_device(): call(finish, [arr(S, D), arr(S, W), arr(*keys_values.shape)], 12)]
    unnamed x12 -> x10, local copies, waits for them, and re-layouts: 1.94 us -> 0.02 us
  transfers between devices with their start and end apart: 4 -> 7, of which waited for: 3 -> 3; matrix products, arithmetic and copies ran while one was open for 1% -> 1% of each run, Pallas kernels for 9% -> 10%
where the time goes in v9:
time: 187 us; the launch traced here: 186 us
  waiting for transfers between devices  90.6 us (48%)
  starting transfers between devices  28.6 us (15%)
  Pallas kernels  27.4 us (15%)
  blocking collectives  22.4 us (12%)
  between operations  14.2 us (8%)
  local copies, waits for them, and re-layouts  2.5 us (1%)
    reduce_scatter x1, waiting for transfers between devices, per_device(): terms = lax.psum_scatter(terms, 'y', scatter_dimension=0, tiled=True)  44.7 us
    all_to_all x2, waiting for transfers between devices, per_device(): got = lax.all_to_all(send, TENSOR, 0, 0, tiled=True)  44.1 us
    all_gather x1, blocking collectives, per_device(): weights = lax.all_gather(weights, 'zh', axis=0, tiled=True)  22.4 us
    ppermute x3, starting transfers between devices, per_device(): lax.ppermute(ahead(d), 'zh', [(i, (i + d) % ZH) for i in range(ZH)])  16 us
    all_to_all x2, starting transfers between devices, per_device(): got = lax.all_to_all(send, TENSOR, 0, 0, tiled=True)  12.5 us
    pallas_call x1, Pallas kernels, per_device(): call(attend, [arr(D, 2 * W), arr(6, S, W)], 56, flops=8 * S * D * W, in_s...  7.23 us
    pallas_call x1, Pallas kernels, per_device(): call(project, [arr(1, S, D), arr(NT, 3 * S + EXTRA, W)], 56, flops=4 * S...  6.33 us
    pallas_call x1, Pallas kernels, per_device(): call(prepare, [arr(S, D), arr(S, D), arr(D, S), arr(D, S), arr(S, 128, of...  4.88 us
  transfers between devices with their start and end apart: 7, of which 3 were waited for; matrix products, arithmetic and copies ran while one was open for 1% of the time, Pallas kernels for 10%

profile of v9, /device:TPU:6, one launch (start us, length us, event | category | flops | bytes accessed | tf_op | source)
XLA Modules:
  0.0 185.7 jit_solution(1597414764587979816)
XLA Ops:
  7.2 0.0 all-gather.2.cloned.1.call-start
  7.2 1.7 shard_map.129
  8.9 22.4 %all_gather.6 = bf16[512,512]{1,0:T(8,128)(2,1)} all-gather(bf16[128,512]{1,0:T(8,128)(2,1)} %shard_map.129), channel_id=1, replica_groups=mesh['zh'=4,'y'=8,'zl'=2,'x'=4,'c'=2] {'zh'}, dimensions={0}, use_global_device_ids=true | all-gather | bytes 655360 | tf_op jit(solution)/shard_map/all_gather | solution.py:238
  31.3 0.0 all-gather.2.cloned.1.call-update
  31.4 3.2 %shard_map.127 = bf16[16,384,256]{2,1,0:T(8,128)(2,1)} custom-call(bf16[128,256]{1,0:T(8,128)(2,1)} %stream.5, bf16[128,256]{1,0:T(8,128)(2,1)} %cot.1, bf16[1,128,4096]{2,1,0:T(8,128)(2,1)} %partial.1), custom_call_target="tpu_custom_call" | custom-call | tf_op jit(solution)/shard_map/pallas_call | solution.py:241
  34.6 7.3 %all-to-all-start = ((bf16[16,384,256]{2,1,0:T(8,128)(2,1)}), bf16[16,384,256]{2,1,0:T(8,128)(2,1)}, u32[]{:S(2)}, u32[]{:S(2)}) async-start(bf16[16,384,256]{2,1,0:T(8,128)(2,1)} %shard_map.127), calls=%async_computation | async-start | bytes 6291456 | tf_op jit(solution)/shard_map/all_to_all | solution.py:242
  41.8 0.0 reduce-scatter.2.cloned.1.call-start
  41.9 0.6 reshape.16.gain
  42.6 0.6 constant_dynamic-slice_fusion.4.kv_in
  43.2 44.1 %all-to-all-done.got = bf16[16,384,256]{2,1,0:T(8,128)(2,1)} async-done(((bf16[16,384,256]{2,1,0:T(8,128)(2,1)}), bf16[16,384,256]{2,1,0:T(8,128)(2,1)}, u32[]{:S(2)}, u32[]{:S(2)}) %all-to-all-start) | async-done | bytes 3145760 | tf_op jit(solution)/shard_map/all_to_all | solution.py:242
  87.3 4.9 %shard_map.128 = (bf16[128,4096]{1,0:T(8,128)(2,1)}, bf16[128,4096]{1,0:T(8,128)(2,1)}, bf16[4096,128]{1,0:T(8,128)(2,1)}, bf16[4096,128]{1,0:T(8,128)(2,1)}, f3...) custom-call(bf16[16,384,256]{2,1,0:T(8,128)(2,1)} %all-to-all-done.got, bf16[128,256]{1,0:T(8,128)(2,1)} %stream.5, ...), custom_call_target="tpu_custom_call" | custom-call | tf_op jit(solution)/shard_map/pallas_call | solution.py:243
  92.2 7.2 %shard_map.130 = (bf16[4096,512]{1,0:T(8,128)(2,1)}, bf16[6,128,256]{2,1,0:T(8,128)(2,1)}) custom-call(bf16[128,4096]{1,0:T(8,128)(2,1)} %get-tuple-element.21.normed_in, bf16[128,4096]{1,0:T(8,128)(2,1)} %get-tuple-element.22.cot_in, bf16[4096,128]{1,0:T(8,128)(2,1)} %get-tuple-element.23.normed_t_in, bf16[4096,128]{1,0:T(8,128)(2,1)} %get-tuple-element.24.cot_t_in, ...), custom_call_target="tpu_custom_call" | custom-call | flops 1073741824 | tf_op jit(solution)/shard_map/pallas_call | solution.py:247
  99.4 0.0 reduce-scatter.2.cloned.1.call-update
  99.4 6.3 %shard_map.131 = (bf16[1,128,4096]{2,1,0:T(8,128)(2,1)}, bf16[16,400,256]{2,1,0:T(8,128)(2,1)}) custom-call(bf16[6,128,256]{2,1,0:T(8,128)(2,1)} %get-tuple-element.25.kept, bf16[4096,512]{1,0:T(8,128)(2,1)} %all-gather.2.cloned.1.call-done.weights, bf16[16,384,256]{2,1,0:T(8,128)(2,1)} %all-to-all-done.got, bf16[1,4096]{1,0:T(2,128)(2,1)} %reshape.16.gain, ...), custom_call_target="tpu_custom_call" | custom-call | flops 536870912 | tf_op jit(solution)/shard_map/pallas_call | solution.py:281
  105.8 5.2 %all-to-all-start.1 = ((bf16[16,400,256]{2,1,0:T(8,128)(2,1)}), bf16[16,400,256]{2,1,0:T(8,128)(2,1)}, u32[]{:S(2)}, u32[]{:S(2)}) async-start(bf16[16,400,256]{2,1,0:T(8,128)(2,1)} %get-tuple-element.27), calls=%async_computation.1 | async-start | bytes 6553600 | tf_op jit(solution)/shard_map/all_to_all | solution.py:290
  111.0 44.7 %reduce-scatter.2.cloned.1.call-done = bf16[512,512]{1,0:T(8,128)(2,1)} async-done(((bf16[4096,512]{1,0:T(8,128)(2,1)}), bf16[512,512]{1,0:T(8,128)(2,1)}) %reduce-scatter.2.cloned.1.call-update) | async-done | bytes 524304 | tf_op jit(solution)/shard_map/reduce_scatter | solution.py:269
  155.7 1.1 constant_dynamic-slice_fusion
  156.8 8.0 %collective-permute-start = (bf16[128,512]{1,0:T(8,128)(2,1)S(1)}, bf16[128,512]{1,0:T(8,128)(2,1)S(1)}, u32[]{:S(2)}, u32[]{:S(2)}) collective-permute-start(bf16[128,512]{1,0:T(8,128)(2,1)S(1)} %get-tuple-element.38), channel_id=1, source_target_pairs={{0,256},{128,384},{256,0},{384,128},{1,257},{129,385},{257,1},{385... | collective-permute-start | bytes 393224 | tf_op jit(solution)/shard_map/ppermute | solution.py:276
  164.8 2.8 %collective-permute-start.1 = (bf16[128,512]{1,0:T(8,128)(2,1)S(1)}, bf16[128,512]{1,0:T(8,128)(2,1)S(1)}, u32[]{:S(2)}, u32[]{:S(2)}) collective-permute-start(bf16[128,512]{1,0:T(8,128)(2,1)S(1)} %get-tuple-element.37), channel_id=1, source_target_pairs={{0,128},{128,256},{256,384},{384,0},{1,129},{129,257},{257,385},{3... | collective-permute-start | bytes 393224 | tf_op jit(solution)/shard_map/ppermute | solution.py:276
  167.7 5.1 %collective-permute-start.2 = (bf16[128,512]{1,0:T(8,128)(2,1)S(1)}, bf16[128,512]{1,0:T(8,128)(2,1)S(1)}, u32[]{:S(2)}, u32[]{:S(2)}) collective-permute-start(bf16[128,512]{1,0:T(8,128)(2,1)S(1)} %get-tuple-element.36), channel_id=1, source_target_pairs={{0,384},{128,0},{256,128},{384,256},{1,385},{129,1},{257,129},{385... | collective-permute-start | bytes 393224 | tf_op jit(solution)/shard_map/ppermute | solution.py:276
  172.8 0.1 dynamic-slice.3
  172.9 3.4 %shard_map.132 = (bf16[128,4096]{1,0:T(8,128)(2,1)}, bf16[128,256]{1,0:T(8,128)(2,1)}, bf16[128,2048]{1,0:T(8,128)(2,1)}) custom-call(bf16[16,400,256]{2,1,0:T(8,128)(2,1)} %all-to-all-done.1.got, bf16[128,256]{1,0:T(8,128)(2,1)S(1)} %copy-done.1, bf16[128,256]{1,0:T(8,128)(2,1)S(1)} %copy-done.2, bf16[1,256]{1,0:T(2,128)(2,1)S(1)} %dynamic_slice.19.gain, ...), custom_call_target="tpu_custom_call" | custom-call | tf_op jit(solution)/shard_map/pallas_call | solution.py:291
  176.3 1.8 collective-permute-done.2.third
  178.1 0.7 shard_map.133
  (15 shorter events, 0.0 us)
Async XLA Ops:
  7.2 35.4 %copy-start = (bf16[128,2048]{1,0:T(8,128)(2,1)S(1)}, bf16[128,2048]{1,0:T(8,128)(2,1)}, u32[]{:S(2)}) copy-start(bf16[128,2048]{1,0:T(8,128)(2,1)} %param.12) | copy-start | bytes 1572868
  7.2 85.0 %all-gather.2.cloned.1.call-start = ((), (), s32[]{:S(2)}) async-start(), calls=%async_computation.3 | async-start | bytes 4718592 | tf_op jit(solution)/shard_map/all_gather | solution.py:239
  34.6 7.4 %copy-start.4 = (bf16[4096]{0:T(1024)(128)(2,1)S(1)}, bf16[4096]{0:T(1024)(128)(2,1)}, u32[]{:S(2)}) copy-start(bf16[4096]{0:T(1024)(128)(2,1)} %param.10) | copy-start | bytes 24580
  34.6 52.7 %all-to-all-start = ((bf16[16,384,256]{2,1,0:T(8,128)(2,1)}), bf16[16,384,256]{2,1,0:T(8,128)(2,1)}, u32[]{:S(2)}, u32[]{:S(2)}) async-start(bf16[16,384,256]{2,1,0:T(8,128)(2,1)} %shard_map.127), calls=%async_computation | async-start | bytes 6291456 | tf_op jit(solution)/shard_map/all_to_all | solution.py:242
  41.8 113.8 %reduce-scatter.2.cloned.1.call-start = ((), (), s32[]{:S(2)}) async-start(), calls=%async_computation.4 | async-start | bytes 4718592 | tf_op jit(solution)/shard_map/reduce_scatter | solution.py:269
  105.8 67.1 %copy-start.1 = (bf16[128,256]{1,0:T(8,128)(2,1)S(1)}, bf16[128,256]{1,0:T(8,128)(2,1)}, u32[]{:S(2)}) copy-start(bf16[128,256]{1,0:T(8,128)(2,1)} %stream.5) | copy-start | bytes 196612
  105.8 67.1 %copy-start.2 = (bf16[128,256]{1,0:T(8,128)(2,1)S(1)}, bf16[128,256]{1,0:T(8,128)(2,1)}, u32[]{:S(2)}) copy-start(bf16[128,256]{1,0:T(8,128)(2,1)} %cot_stream.1) | copy-start | bytes 196612
  105.8 67.1 %copy-start.3 = (f32[128,128]{1,0:T(8,128)S(1)}, f32[128,128]{1,0:T(8,128)}, u32[]{:S(2)}) copy-start(f32[128,128]{1,0:T(8,128)} %get-tuple-element.28.inv_in) | copy-start | bytes 196612
  105.8 67.1 %all-to-all-start.1 = ((bf16[16,400,256]{2,1,0:T(8,128)(2,1)}), bf16[16,400,256]{2,1,0:T(8,128)(2,1)}, u32[]{:S(2)}, u32[]{:S(2)}) async-start(bf16[16,400,256]{2,1,0:T(8,128)(2,1)} %get-tuple-element.27), calls=%async_computation.1 | async-start | bytes 6553600 | tf_op jit(solution)/shard_map/all_to_all | solution.py:290
  156.8 19.5 %collective-permute-start = (bf16[128,512]{1,0:T(8,128)(2,1)S(1)}, bf16[128,512]{1,0:T(8,128)(2,1)S(1)}, u32[]{:S(2)}, u32[]{:S(2)}) collective-permute-start(bf16[128,512]{1,0:T(8,128)(2,1)S(1)} %get-tuple-element.38), channel_id=1, source_target_pairs={{0,256},{128,384},{256,0},{384,128},{1,257},{129,385},{257,1},{385... | collective-permute-start | bytes 393224 | tf_op jit(solution)/shard_map/ppermute | solution.py:276
  164.8 11.5 %collective-permute-start.1 = (bf16[128,512]{1,0:T(8,128)(2,1)S(1)}, bf16[128,512]{1,0:T(8,128)(2,1)S(1)}, u32[]{:S(2)}, u32[]{:S(2)}) collective-permute-start(bf16[128,512]{1,0:T(8,128)(2,1)S(1)} %get-tuple-element.37), channel_id=1, source_target_pairs={{0,128},{128,256},{256,384},{384,0},{1,129},{129,257},{257,385},{3... | collective-permute-start | bytes 393224 | tf_op jit(solution)/shard_map/ppermute | solution.py:276
  167.7 10.4 %collective-permute-start.2 = (bf16[128,512]{1,0:T(8,128)(2,1)S(1)}, bf16[128,512]{1,0:T(8,128)(2,1)S(1)}, u32[]{:S(2)}, u32[]{:S(2)}) collective-permute-start(bf16[128,512]{1,0:T(8,128)(2,1)S(1)} %get-tuple-element.36), channel_id=1, source_target_pairs={{0,384},{128,0},{256,128},{384,256},{1,385},{129,1},{257,129},{385... | collective-permute-start | bytes 393224 | tf_op jit(solution)/shard_map/ppermute | solution.py:276
Sparse Core Ops, SparseCore 0:
  31.5 57.3 all-gather.1
  99.5 56.0 reduce-scatter.1
